TPU v7x, 32 devices: a whole 2x2x4 slice. The times are simulated.
32 devices in a mesh: band: 4 (over y, x), wave: 8 (over z, core).
Axes of the slice: x: 2, y: 2, z: 4, core: 2. Of those that a mesh axis runs over, the one named last changes fastest.
Arguments:
- spectral: bfloat16 [640, 1408, 8], P('wave', 'band'), may hold values from -0.119628906 to 0.119628906
- legendre: bfloat16 [640, 1280, 1408], P('wave', 'band'), may hold values from -0.15625 to 0.15625
- slot_pair: int32 [640], replicated, may hold values from 0 to 639, each once
- quad_weight: float32 [1280], P('band'), may hold values from 0.4 to 2.5
- depart_code: int32 [1, 2, 1280, 5120], P(None, None, ('band', 'wave')), may hold values from 0 to 15
- stencil_pick: int32 [1, 2, 1280, 5120], P(None, None, ('band', 'wave')), may hold values from 0 to 15
- stencil_weight: float32 [16, 16], replicated, may hold values from -0.05 to 0.175
Outputs:
- arrival: bfloat16 [1, 4, 2, 1280, 5120], P(None, None, None, ('band', 'wave'))
- spectral_out: bfloat16 [640, 1408, 8], P('wave', 'band')
Inputs may be any that keep to these rules, and one draw needn't show every extreme that they name: A permutation: slot s holds the wavenumbers slot_pair[s] and 1279 - slot_pair[s]. Decodes to a latitude step depart_code // 4 - 2 and a longitude step depart_code % 4 - 2.
All inputs are finite; a program needn't handle non-finite values.
Results may differ from a plain program's by a relative error of at most 0.02.
Values may be sent and summed in bfloat16 or wider, within the bound.
No kernel may reach another device: no remote copies, remote signals or barrier semaphores. Data moves between devices by JAX's collectives and lax.ppermute only.
A program may use at most 640 MiB of HBM per device.

v0:
```python
import math

import jax
import jax.numpy as jnp
from jax import lax
from jax.sharding import PartitionSpec as P

M = 1280
NLON = 5120
FIELDS = 4
LEV = 1
DR = 2
DL = 2
NSTEN = 16
RIM = 3


def extended_2(array, sides, width):
    for axis, dim in sides:
        devices, length = (lax.axis_size(axis), array.shape[dim])
        up = [(i, (i + 1) % devices) for i in range(devices - 1)]
        down = [(j, i) for i, j in up]
        last = lax.slice_in_dim(array, length - width, length, axis=dim)
        first = lax.slice_in_dim(array, 0, width, axis=dim)
        before = lax.ppermute(last, axis, up)
        after = lax.ppermute(first, axis, down)
        array = jnp.concatenate([before, array, after], axis=dim)
    return array


def row_weights(pair_ids, row_index, wavenumbers):
    low_count = wavenumbers - pair_ids[:, None]
    higher = row_index[None, :] >= low_count
    in_use = (row_index[None, :] <= wavenumbers).astype(jnp.float32)
    degree = jnp.where(higher, row_index[None, :] - low_count, row_index[None, :])
    parity_sign = 1.0 - 2.0 * (degree % 2).astype(jnp.float32)
    high_part = higher.astype(jnp.float32)
    holder = jnp.stack([1.0 - high_part, high_part], axis=-1) * in_use[..., None]
    hemisphere = jnp.stack([jnp.ones_like(parity_sign), parity_sign], axis=-1)
    return holder[..., :, None] * hemisphere[..., None, :]


def wave_factor(slot_pair, wavenumbers):
    wave_pair = jnp.stack([slot_pair, wavenumbers - 1 - slot_pair], axis=1)
    return jnp.where(wave_pair == 0, 1.0, 2.0).astype(jnp.float32)


def angle_table(slot_pair, wavenumbers, longitudes):
    row_count = slot_pair.shape[0] * 4
    row_id = jnp.arange(row_count, dtype=jnp.int32)
    pair_of_row = jnp.repeat(slot_pair, 4)
    upper = row_id // 2 % 2
    wave_of_row = jnp.where(upper == 1, wavenumbers - 1 - pair_of_row, pair_of_row)
    sine_row = (row_id % 2 == 1)[:, None]
    factor = jnp.where(wave_of_row == 0, 1.0, 2.0).astype(jnp.float32)[:, None]
    column = jnp.arange(longitudes, dtype=jnp.int32)
    residue = wave_of_row[:, None] * column[None, :] % longitudes
    angles = residue.astype(jnp.float32) * (2.0 * math.pi / longitudes)
    values = jnp.where(sine_row, -factor * jnp.sin(angles), factor * jnp.cos(angles))
    return values.astype(jnp.bfloat16)


def interpolate_window(padded, departure, tap_weight):
    levels, fields, hemispheres, padded_rows, longitudes = padded.shape
    height = padded_rows - 2 * RIM
    row_shift = departure // (2 * DL) - DR
    col_shift = departure % (2 * DL) - DL
    row_match = {}
    for value in range(-DR, DR):
        row_match[value] = row_shift == value
    col_match = {}
    for value in range(-DL, DL):
        col_match[value] = col_shift == value
    tap_values = [tap_weight(tap_index) for tap_index in range(16)]
    running = jnp.zeros((levels, fields, hemispheres, height, longitudes), jnp.float32)
    for shift_row in range(-DR - 1, DR + 2):
        row_slab = padded[:, :, :, RIM + shift_row : RIM + shift_row + height, :].astype(
            jnp.float32
        )
        for shift_col in range(-DL - 1, DL + 2):
            factor = jnp.zeros(departure.shape, jnp.float32)
            for tap_row in range(4):
                need_row = shift_row - tap_row + 1
                if need_row < -DR or need_row >= DR:
                    continue
                for tap_col in range(4):
                    need_col = shift_col - tap_col + 1
                    if need_col < -DL or need_col >= DL:
                        continue
                    hit = row_match[need_row] & col_match[need_col]
                    factor = factor + jnp.where(hit, tap_values[4 * tap_row + tap_col], 0.0)
            moved = jnp.roll(row_slab, -shift_col, axis=4)
            running = running + factor[:, None] * moved
    return running


def per_device(
    spectral, legendre, slot_pair, quad_weight, depart_code, stencil_pick, stencil_weight
):
    slot_local, row_local, col_total = spectral.shape
    height = depart_code.shape[2]
    slot_total = slot_pair.shape[0]
    wave_rank = lax.axis_index("wave")
    my_pairs = lax.dynamic_slice_in_dim(slot_pair, wave_rank * slot_local, slot_local)
    segment = lax.all_gather(spectral, "band", axis=1, tiled=True)
    row_count = segment.shape[1]
    masks = row_weights(my_pairs, jnp.arange(row_count, dtype=jnp.int32), M)
    masked = (segment.astype(jnp.float32)[:, :, None, None, :] * masks[..., None]).astype(
        jnp.bfloat16
    )
    leg_rows = legendre
    fourier = jnp.einsum(
        "sjohc,sij->isohc", masked, leg_rows, preferred_element_type=jnp.float32
    ).astype(jnp.bfloat16)
    by_latitude = lax.all_to_all(fourier, "wave", split_axis=0, concat_axis=1, tiled=True)
    left_rows = by_latitude.reshape(height, slot_total, 2, 2, LEV, FIELDS, 2)
    left_rows = left_rows.transpose(4, 5, 3, 0, 1, 2, 6).reshape(
        LEV * FIELDS * 2 * height, slot_total * 4
    )
    angle_rows = angle_table(slot_pair, M, NLON)
    grid_values = jnp.dot(left_rows, angle_rows, preferred_element_type=jnp.float32)
    grid_values = grid_values.astype(jnp.bfloat16).reshape(LEV, FIELDS, 2, height, NLON)
    extended = extended_2(grid_values, ((("band", "wave"), 3),), RIM)
    lat_rank = lax.axis_index(("band", "wave"))
    lat_devices = lax.axis_size(("band", "wave"))
    pole_rows = jnp.roll(jnp.flip(grid_values[:, :, :, :RIM], 3), NLON // 2, 4)
    equator_rows = jnp.flip(grid_values[:, :, ::-1, height - RIM :], 3)
    lower_rows = jnp.where(lat_rank == 0, pole_rows, extended[:, :, :, :RIM])
    upper_rows = jnp.where(
        lat_rank == lat_devices - 1, equator_rows, extended[:, :, :, height + RIM :]
    )
    padded = jnp.concatenate([lower_rows, grid_values, upper_rows], 3)
    selector = (jnp.arange(NSTEN, dtype=jnp.int32)[:, None] == stencil_pick.reshape(1, -1)).astype(
        jnp.float32
    )
    tap_table = jnp.dot(stencil_weight.T, selector, precision=lax.Precision.HIGHEST)

    def tap_weight(tap_index):
        return tap_table[tap_index].reshape(stencil_pick.shape)

    arrival = interpolate_window(padded, depart_code, tap_weight).astype(jnp.bfloat16)
    sums = lax.dot_general(
        arrival.reshape(-1, NLON),
        angle_rows,
        (((1,), (1,)), ((), ())),
        preferred_element_type=jnp.float32,
    )
    sums = sums.reshape(LEV, FIELDS, 2, height, slot_total, 2, 2)
    my_weight = lax.dynamic_slice_in_dim(quad_weight, wave_rank * height, height)
    scaling = my_weight[:, None, None] / (wave_factor(slot_pair, M)[None] * math.sqrt(NLON))
    coeffs = (sums * scaling[None, None, None, :, :, :, None]).astype(jnp.bfloat16)
    coeffs = coeffs.transpose(3, 4, 5, 2, 0, 1, 6).reshape(height, slot_total, 2, 2, col_total)
    by_wave = lax.all_to_all(coeffs, "wave", split_axis=1, concat_axis=0, tiled=True)
    leg_rows = legendre
    raw_sum = lax.psum_scatter(
        jnp.einsum("isohc,sij->jsohc", by_wave, leg_rows, preferred_element_type=jnp.float32)
        .reshape(row_local * lax.axis_size("band"), slot_local, 4 * col_total)
        .astype(jnp.bfloat16),
        "band",
        scatter_dimension=0,
        tiled=True,
    ).astype(jnp.float32)
    band_rank = lax.axis_index("band")
    masks = row_weights(my_pairs, band_rank * row_local + jnp.arange(row_local, dtype=jnp.int32), M)
    summed = jnp.einsum(
        "jsohc,sjoh->jsc",
        raw_sum.reshape(row_local, slot_local, 2, 2, col_total),
        masks,
        precision=lax.Precision.HIGHEST,
    )
    spectral_out = summed.transpose(1, 0, 2).astype(jnp.bfloat16)
    return (arrival, spectral_out)


def solution(mesh):
    in_specs = (
        P("wave", "band", None),
        P("wave", "band", None),
        P(),
        P("band"),
        P(None, None, ("band", "wave"), None),
        P(None, None, ("band", "wave"), None),
        P(),
    )
    out_specs = (P(None, None, None, ("band", "wave"), None), P("wave", "band", None))
    return jax.shard_map(
        per_device, mesh=mesh, in_specs=in_specs, out_specs=out_specs, check_vma=False
    )
```

profile of v0, /device:TPU:0, one launch (start us, length us, event | category | flops | bytes accessed | tf_op | source)
XLA Modules:
  0.0 1558.1 jit_solution(16962670653038843067)
XLA Ops:
  10.1 14.4 convolution_bitcast_fusion
  24.5 137.9 %slice_reduce_fusion.15 = (f32[409600]{0:T(1024)}, f32[409600]{0:T(1024)}, f32[409600]{0:T(1024)}, f32[409600]{0:T(1024)}, f32[409600]{0:T(1024)S(1)}, /*index=5...) fusion(f32[16,409600]{1,0:T(8,128)} %convolution_bitcast_fusion), kind=kLoop, calls=%fused_computation.173 | loop fusion | bytes 52428800 | tf_op jit(solution)/shard_map/slice | solution.py:139
  200.1 5.4 select_bitcast_fusion.3
  212.4 5.2 add_bitcast_fusion.25
  222.0 6.3 add_bitcast_fusion.30
  228.3 7.0 add_bitcast_fusion.36
  235.3 5.9 add_bitcast_fusion.29
  241.3 6.1 add_bitcast_fusion.24
  247.5 5.9 add_bitcast_fusion.23
  253.5 7.4 add_bitcast_fusion.22
  261.0 5.5 add_bitcast_fusion.21
  274.9 5.4 add_bitcast_fusion.14
  280.4 8.1 add_bitcast_fusion.20
  292.1 225.4 %fusion.183 = bf16[640,2,2,5120,1,1]{3,0,2,1,5,4:T(8,128)(2,1)} fusion(f32[640,2,2]{0,2,1:T(2,128)S(1)} %get-tuple-element.204, s32[640,2,2]{0,2,1:T(2,128)S(1)} %compare_select_fusion.7, f32[640,2,2]{0,2,1:T(2,128)S(1)} %get-tuple-element.203, pred[640,2,2]{0,2,1:T(4,128)(4,1)S(1)} %fusion.119), kind=kLoop, calls=%fused_computation.21.clone.clone.clone.clone.clone.clone.1 | loop fusion | flops 170393600 | bytes 26247680 | tf_op jit(solution)/shard_map/dot_general | solution.py:142
  528.1 13.2 add_bitcast_fusion.35
  548.1 32.1 %convert_bitcast_fusion = bf16[320,80,2,2,8]{0,4,3,2,1:T(8,128)(2,1)} fusion(bf16[80,320,1408]{2,1,0:T(8,128)(2,1)} %param.8, f32[80,1408,2,2]{1,3,2,0:T(2,128)} %broadcast_multiply_fusion, f32[80,1408,8]{1,2,0:T(8,128)S(1)} %convert_element_type.185), kind=kOutput, calls=%fused_computation.152 | convolution fusion | flops 2314895360 | bytes 79134720 | tf_op jit(solution)/shard_map/sjohc,sij->isohc/dot_general | solution.py:112
  585.1 6.3 all-to-all-start
  592.3 13.2 add_bitcast_fusion.17
  605.5 46.4 %all-to-all-done = bf16[320,80,2,2,8]{1,4,3,2,0:T(8,128)(2,1)} async-done(((bf16[320,80,2,2,8]{1,4,3,2,0:T(8,128)(2,1)}), bf16[320,80,2,2,8]{1,4,3,2,0:T(8,128)(2,1)}, u32[]{:S(2)}, u32[]{:S(2)}) %all-to-all-start) | async-done | bytes 1638432 | tf_op jit(solution)/shard_map/all_to_all | solution.py:115
  658.2 11.3 copy.55
  669.6 16.5 %reshape.2052 = bf16[320,2560]{0,1:T(8,128)(2,1)} reshape(bf16[1,4,2,40,640,2,2]{3,2,1,6,5,4,0:T(2,128)(2,1)} %copy.55) | data formatting | bytes 3276800 | tf_op jit(solution)/shard_map/reshape | solution.py:117
  686.1 237.0 %fusion.23 = bf16[320,5120]{1,0:T(8,128)(2,1)S(1)} fusion(bf16[320,2560]{0,1:T(8,128)(2,1)} %reshape.2052, f32[2560]{0:T(1024)S(1)} %compare_select_fusion.8, s32[2560]{0:T(1024)S(1)} %get-tuple-element.61, f32[2560]{0:T(1024)S(1)} %get-tuple-element.60, pred[2560]{0:T(1024)(128)(4,1)S(1)} %fusion.110), kind=kOutput, calls=%fused_computation.31 | convolution fusion | flops 8560640000 | bytes 4948480 | tf_op jit(solution)/shard_map/dot_general | solution.py:121
  925.1 6.4 fusion.170
  931.5 6.4 fusion.172
  937.9 6.5 fusion.174
  950.9 18.9 %rev.6 = bf16[1,4,2,3,5120]{4,3,2,1,0:T(4,128)(2,1)} reverse(bf16[1,4,2,3,5120]{4,3,2,1,0:T(4,128)(2,1)} %get-tuple-element.193), dimensions={2,3} | reverse | bytes 491520 | tf_op jit(solution)/shard_map/jit(_flip)/rev | solution.py:127
  969.8 9.4 slice.362
  979.2 9.4 slice.364
  990.8 13.1 fusion.83
  1003.9 19.1 %fusion.145 = (f32[1,4,2,40,5117]{4,3,2,1,0:T(8,128)}, f32[1,4,2,40,5117]{4,3,2,1,0:T(8,128)}, f32[1,4,2,40,5117]{4,3,2,1,0:T(8,128)}, f32[1,4,2,40,5117]{4,3,2,1,0:T(8,128)}) fusion(f32[1,4,2,40,5120]{4,3,2,1,0:T(8,128)} %get-tuple-element.170, f32[1,4,2,40,5120]{4,3,2,1,0:T(8,128)} %get-tuple-element.177), kind=kLoop, calls=%fused_computation.317 | loop fusion | bytes 52398080 | tf_op jit(solution)/shard_map/jit(_roll_static)/slice | solution.py:92
  1023.0 19.1 %fusion.147 = (f32[1,4,2,40,5118]{4,3,2,1,0:T(8,128)}, f32[1,4,2,40,5118]{4,3,2,1,0:T(8,128)}, f32[1,4,2,40,5118]{4,3,2,1,0:T(8,128)}, f32[1,4,2,40,5118]{4,3,2,1,0:T(8,128)}) fusion(f32[1,4,2,40,5120]{4,3,2,1,0:T(8,128)} %get-tuple-element.170, f32[1,4,2,40,5120]{4,3,2,1,0:T(8,128)} %get-tuple-element.177), kind=kLoop, calls=%fused_computation.319 | loop fusion | bytes 52408320 | tf_op jit(solution)/shard_map/jit(_roll_static)/slice | solution.py:92
  1042.1 19.2 %fusion.149 = (f32[1,4,2,40,5119]{4,3,2,1,0:T(8,128)}, f32[1,4,2,40,5119]{4,3,2,1,0:T(8,128)}, f32[1,4,2,40,5119]{4,3,2,1,0:T(8,128)}, f32[1,4,2,40,5119]{4,3,2,1,0:T(8,128)}) fusion(f32[1,4,2,40,5120]{4,3,2,1,0:T(8,128)} %get-tuple-element.170, f32[1,4,2,40,5120]{4,3,2,1,0:T(8,128)} %get-tuple-element.177), kind=kLoop, calls=%fused_computation.321 | loop fusion | bytes 52418560 | tf_op jit(solution)/shard_map/jit(_roll_static)/slice | solution.py:92
  1061.3 18.9 %fusion.133 = (f32[1,4,2,40,5117]{4,3,2,1,0:T(8,128)}, f32[1,4,2,40,5117]{4,3,2,1,0:T(8,128)}, f32[1,4,2,40,5117]{4,3,2,1,0:T(8,128)}, f32[1,4,2,40,5117]{4,3,2,1,0:T(8,128)}) fusion(f32[1,4,2,40,5120]{4,3,2,1,0:T(8,128)} %get-tuple-element.169, f32[1,4,2,40,5120]{4,3,2,1,0:T(8,128)} %get-tuple-element.171), kind=kLoop, calls=%fused_computation.305 | loop fusion | bytes 52398080 | tf_op jit(solution)/shard_map/jit(_roll_static)/slice | solution.py:92
  1080.3 19.1 %fusion.135 = (f32[1,4,2,40,5118]{4,3,2,1,0:T(8,128)}, f32[1,4,2,40,5118]{4,3,2,1,0:T(8,128)}, f32[1,4,2,40,5118]{4,3,2,1,0:T(8,128)}, f32[1,4,2,40,5118]{4,3,2,1,0:T(8,128)}) fusion(f32[1,4,2,40,5120]{4,3,2,1,0:T(8,128)} %get-tuple-element.169, f32[1,4,2,40,5120]{4,3,2,1,0:T(8,128)} %get-tuple-element.171), kind=kLoop, calls=%fused_computation.307 | loop fusion | bytes 52408320 | tf_op jit(solution)/shard_map/jit(_roll_static)/slice | solution.py:92
  1099.4 19.0 %fusion.137 = (f32[1,4,2,40,5119]{4,3,2,1,0:T(8,128)}, f32[1,4,2,40,5119]{4,3,2,1,0:T(8,128)}, f32[1,4,2,40,5119]{4,3,2,1,0:T(8,128)}, f32[1,4,2,40,5119]{4,3,2,1,0:T(8,128)}) fusion(f32[1,4,2,40,5120]{4,3,2,1,0:T(8,128)} %get-tuple-element.169, f32[1,4,2,40,5120]{4,3,2,1,0:T(8,128)} %get-tuple-element.171), kind=kLoop, calls=%fused_computation.309 | loop fusion | bytes 52418560 | tf_op jit(solution)/shard_map/jit(_roll_static)/slice | solution.py:92
  1130.9 18.9 %fusion.161 = (f32[1,4,2,40,5119]{4,3,2,1,0:T(8,128)}, f32[1,4,2,40,5119]{4,3,2,1,0:T(8,128)}, f32[1,4,2,40,5119]{4,3,2,1,0:T(8,128)}, f32[1,4,2,40,5119]{4,3,2,1,0:T(8,128)}) fusion(f32[1,4,2,40,5120]{4,3,2,1,0:T(8,128)} %get-tuple-element.175, f32[1,4,2,40,5120]{4,3,2,1,0:T(8,128)} %get-tuple-element.176), kind=kLoop, calls=%fused_computation.333 | loop fusion | bytes 52418560 | tf_op jit(solution)/shard_map/jit(_roll_static)/slice | solution.py:92
  1151.9 18.9 %fusion.159 = (f32[1,4,2,40,5118]{4,3,2,1,0:T(8,128)}, f32[1,4,2,40,5118]{4,3,2,1,0:T(8,128)}, f32[1,4,2,40,5118]{4,3,2,1,0:T(8,128)}, f32[1,4,2,40,5118]{4,3,2,1,0:T(8,128)}) fusion(f32[1,4,2,40,5120]{4,3,2,1,0:T(8,128)} %get-tuple-element.175, f32[1,4,2,40,5120]{4,3,2,1,0:T(8,128)} %get-tuple-element.176), kind=kLoop, calls=%fused_computation.331 | loop fusion | bytes 52408320 | tf_op jit(solution)/shard_map/jit(_roll_static)/slice | solution.py:92
  1172.9 19.1 %fusion.157 = (f32[1,4,2,40,5117]{4,3,2,1,0:T(8,128)}, f32[1,4,2,40,5117]{4,3,2,1,0:T(8,128)}, f32[1,4,2,40,5117]{4,3,2,1,0:T(8,128)}, f32[1,4,2,40,5117]{4,3,2,1,0:T(8,128)}) fusion(f32[1,4,2,40,5120]{4,3,2,1,0:T(8,128)} %get-tuple-element.175, f32[1,4,2,40,5120]{4,3,2,1,0:T(8,128)} %get-tuple-element.176), kind=kLoop, calls=%fused_computation.329 | loop fusion | bytes 52398080 | tf_op jit(solution)/shard_map/jit(_roll_static)/slice | solution.py:92
  1194.0 137.7 %fusion.72 = bf16[1,4,2,40,5120]{4,3,2,1,0:T(8,128)(2,1)} fusion(f32[1,4,2,40,3]{4,3,2,1,0:T(8,128)} %get-tuple-element.233, f32[1,4,2,40,5117]{4,3,2,1,0:T(8,128)} %get-tuple-element.235, f32[1,4,2,40,2]{4,3,2,1,0:T(8,128)} %get-tuple-element.237, f32[1,4,2,40,5118]{4,3,2,1,0:T(8,128)} %get-tuple-element.239, f32[1,4,2,40,1]{4,3,2,1,0:T(8,128)} %get-tuple-element.241, ...), kind=kLoop, calls=%fused_computation.122 | loop fusion | flops 270336000 | bytes 362577920 | tf_op jit(solution)/shard_map/convert_element_type | solution.py:141
  1331.7 14.6 fusion.96
  1346.5 8.2 copy.57
  1354.7 9.3 reshape.2146
  1364.0 45.5 %all_to_all.33 = bf16[8,2,51200]{2,1,0:T(2,128)(2,1)S(1)} all-to-all(bf16[8,2,51200]{2,1,0:T(2,128)(2,1)S(1)} %reshape.2146), channel_id=1, replica_groups=mesh['band'=4,'wave'=8] {'wave'}, dimensions={0} | all-to-all | bytes 3276800 | tf_op jit(solution)/shard_map/all_to_all | solution.py:153
  1409.5 8.9 reshape.2147
  1418.4 8.5 copy.59
  1430.4 28.4 %fusion.73 = bf16[80,2,2,8,1408]{4,3,2,1,0:T(8,128)(2,1)} fusion(bf16[320,80,2,2,8]{0,4,3,2,1:T(8,128)(2,1)} %copy.60, bf16[80,320,1408]{2,1,0:T(8,128)(2,1)} %param.8), kind=kOutput, calls=%fused_computation.123 | convolution fusion | flops 2310471680 | bytes 80936960 | tf_op jit(solution)/shard_map/isohc,sij->jsohc/dot_general | solution.py:156
  1458.9 10.0 copy.75
  1470.1 75.7 %reduce-scatter.4.cloned.1.call-done = bf16[352,2560]{1,0:T(8,128)(2,1)} async-done(((bf16[1408,2560]{1,0:T(8,128)(2,1)}), bf16[352,2560]{1,0:T(8,128)(2,1)}) %reduce-scatter.4.cloned.1.call-update) | async-done | bytes 1802256
  (206 shorter events, 132.3 us)
Async XLA Ops:
  7.2 534.1 %all-gather.2.cloned.1.call-start = ((), (), s32[]{:S(2)}) async-start(), calls=%async_computation.3 | async-start | bytes 3604480 | tf_op jit(solution)/shard_map/all_gather | solution.py:105
  200.1 5.4 copy-start.4
  200.1 5.4 copy-start.5
  200.1 5.4 copy-start.10
  205.6 12.1 copy-start.36
  208.7 9.0 copy-start.26
  208.7 9.0 copy-start.28
  208.7 9.0 copy-start.48
  208.7 9.0 copy-start.49
  211.8 5.9 copy-start.31
  211.8 5.9 copy-start.33
  211.8 5.9 copy-start.50
  211.8 5.9 copy-start.51
  217.7 57.2 %copy-start.23 = (pred[1,2,40,5120]{3,2,1,0:T(8,128)(4,1)}, pred[1,2,40,5120]{3,2,1,0:T(8,128)(4,1)S(1)}, u32[]{:S(2)}) copy-start(pred[1,2,40,5120]{3,2,1,0:T(8,128)(4,1)S(1)} %get-tuple-element.165) | copy-start | bytes 1228804
  221.9 53.0 %copy-start.24 = (pred[1,2,40,5120]{3,2,1,0:T(8,128)(4,1)}, pred[1,2,40,5120]{3,2,1,0:T(8,128)(4,1)S(1)}, u32[]{:S(2)}) copy-start(pred[1,2,40,5120]{3,2,1,0:T(8,128)(4,1)S(1)} %get-tuple-element.46) | copy-start | bytes 1228804
  221.9 58.4 %copy-start.25 = (pred[1,2,40,5120]{3,2,1,0:T(8,128)(4,1)}, pred[1,2,40,5120]{3,2,1,0:T(8,128)(4,1)S(1)}, u32[]{:S(2)}) copy-start(pred[1,2,40,5120]{3,2,1,0:T(8,128)(4,1)S(1)} %get-tuple-element.79) | copy-start | bytes 1228804
  228.2 7.1 copy-start.11
  228.2 7.1 copy-start.13
  228.2 7.1 copy-start.27
  228.2 7.1 copy-start.29
  228.2 7.1 copy-start.30
  241.3 6.1 copy-start.12
  247.4 6.0 copy-start.14
  247.4 6.0 copy-start.15
  247.4 6.0 copy-start.16
  247.4 6.0 copy-start.18
  247.4 6.0 copy-start.32
  247.4 6.0 copy-start.34
  247.4 6.0 copy-start.37
  247.5 6.0 copy-start.38
  247.5 6.0 copy-start.42
  253.4 7.5 copy-start.40
  253.5 7.4 copy-start.21
  260.9 5.5 copy-start.20
  260.9 5.5 copy-start.39
  260.9 5.5 copy-start.41
  261.0 5.5 copy-start.43
  261.0 5.5 copy-start.44
  274.9 5.5 copy-start.22
  274.9 5.5 copy-start.35
  274.9 5.5 copy-start.46
  280.4 8.1 copy-start.57
  585.1 66.7 %all-to-all-start = ((bf16[320,80,2,2,8]{1,4,3,2,0:T(8,128)(2,1)}), bf16[320,80,2,2,8]{1,4,3,2,0:T(8,128)(2,1)}, u32[]{:S(2)}, u32[]{:S(2)}) async-start(bf16[320,80,2,2,8]{1,4,3,2,0:T(8,128)(2,1)} %copy.53), calls=%async_computation | async-start | bytes 5242880 | tf_op jit(solution)/shard_map/all_to_all | solution.py:115
  591.4 954.4 %reduce-scatter.4.cloned.1.call-start = ((), (), s32[]{:S(2)}) async-start(), calls=%async_computation.4 | async-start | bytes 9011200
  945.1 44.3 %collective-permute-start.1 = (bf16[1,4,2,3,5120]{4,3,2,1,0:T(4,128)(2,1)}, bf16[1,4,2,3,5120]{4,3,2,1,0:T(4,128)(2,1)}, u32[]{:S(2)}, u32[]{:S(2)}) collective-permute-start(bf16[1,4,2,3,5120]{4,3,2,1,0:T(4,128)(2,1)} %get-tuple-element.192), channel_id=1, source_target_pairs={{1,0},{2,1},{3,2},{4,3},{5,4},{6,5},{7,6},{8,7},{9,8},{10,9},{11,1... | collective-permute-start | bytes 737288 | tf_op jit(solution)/shard_map/ppermute | solution.py:26
  947.1 43.4 %collective-permute-start = (bf16[1,4,2,3,5120]{4,3,2,1,0:T(4,128)(2,1)}, bf16[1,4,2,3,5120]{4,3,2,1,0:T(4,128)(2,1)}, u32[]{:S(2)}, u32[]{:S(2)}) collective-permute-start(bf16[1,4,2,3,5120]{4,3,2,1,0:T(4,128)(2,1)} %get-tuple-element.193), channel_id=1, source_target_pairs={{0,1},{1,2},{2,3},{3,4},{4,5},{5,6},{6,7},{7,8},{8,9},{9,10},{10,1... | collective-permute-start | bytes 737288 | tf_op jit(solution)/shard_map/ppermute | solution.py:25
  990.5 13.4 copy-start.52
  990.8 13.1 copy-start.53
  (17 other events, 58.2 us)
Sparse Core Ops, SparseCore 0:
  9.9 44.4 all-gather.1
  1469.0 76.7 reduce-scatter.3
where the time goes:
time: 1570 us; the launch traced here: 1560 us
  local copies, waits for them, and re-layouts  533 us (34%)
  other arithmetic  504 us (32%)
  matrix products  327 us (21%)
  waiting for transfers between devices  122 us (8%)
  blocking collectives  45.5 us (3%)
    dot_general x1, matrix products, per_device(): jnp.dot(left_rows, angle_rows, preferred_element_type=jnp.float32)  237 us
    dot_general x1, other arithmetic, per_device(): lax.dot_general(arrival.reshape(-1, NLON), angle_rows, (((1,), (1,)), (()...  225 us
    slice x24, local copies, waits for them, and re-layouts, interpolate_window(): moved = jnp.roll(row_slab, -shift_col, axis=4)  212 us
    slice x1, local copies, waits for them, and re-layouts, tap_weight(): return tap_table[tap_index].reshape(stencil_pick.shape)  138 us
    convert_element_type x1, other arithmetic, per_device(): interpolate_window(padded, depart_code, tap_weight).astype(jnp.bfloat16)  138 us
    mul x18, other arithmetic, interpolate_window(): running = running + factor[:, None] * moved  113 us
    unnamed x3, waiting for transfers between devices  75.7 us
    all_to_all x1, waiting for transfers between devices, per_device(): lax.all_to_all(fourier, 'wave', split_axis=0, concat_axis=1, tiled=True)  46.4 us
  transfers between devices with their start and end apart: 5, of which 2 were waited for; matrix products, arithmetic and copies ran while one was open for 38% of the time, Pallas kernels for 0%

commit v1 on v0

v1 whole, which is shorter than its diff:
```python
import functools
import math

import jax
import jax.numpy as jnp
import numpy as np
from jax import lax
from jax.experimental import pallas as pl
from jax.experimental.pallas import tpu as pltpu
from jax.sharding import PartitionSpec as P

M = 1280
NLON = 5120
HALF = NLON // 2
FIELDS = 4
NSTEN = 16
RIM = 3
COLS = 8
GROUP = 8
WIDE = GROUP * 4 * COLS
RUN = 5
SUB = 8
REACH = RUN + 2 * RIM
BLOCKS = NLON // 128
TILES = 10
F32 = jnp.float32
BF16 = jnp.bfloat16
VMEM_LIMIT = 60 * 2**20


def dot_nt(left, right):
    return lax.dot_general(left, right, (((1,), (1,)), ((), ())), preferred_element_type=F32)


def lane_order():
    index = np.arange(WIDE).reshape(GROUP, 2, 2, FIELDS, 2).transpose(1, 2, 3, 0, 4).reshape(-1)
    matrix = np.zeros((WIDE, WIDE), np.float32)
    matrix[index, np.arange(WIDE)] = 1.0
    return jnp.asarray(matrix, BF16)


def row_masks(pair, rows):
    row = lax.broadcasted_iota(jnp.int32, (1, rows), 1)
    low_count = M - pair
    higher = row >= low_count
    degree = jnp.where(higher, row - low_count, row)
    sign = (1 - 2 * (degree & 1)).astype(F32)
    in_use = row <= M
    side = jnp.where(higher, 1, 0) ^ (pair & 1)
    even = jnp.where(in_use & (side == 0), 1.0, 0.0)
    odd = jnp.where(in_use & (side == 1), 1.0, 0.0)
    return even, odd, sign


def forward_kernel(height, pair_ref, spec_ref, leg_ref, out_ref, rhs_ref, acc_ref):
    group = pl.program_id(0)
    rows = spec_ref.shape[2]
    sub = height // RUN

    @pl.when(group == 0)
    def _():
        rhs_ref[...] = jnp.zeros_like(rhs_ref)

    for u in range(GROUP):
        even, odd, sign = row_masks(pair_ref[group * GROUP + u], rows)
        spec = spec_ref[u].astype(F32)
        south = spec * sign
        parts = [spec * even, south * even, spec * odd, south * odd]
        rhs_ref[u, 32 * u : 32 * u + 32, :] = jnp.concatenate(parts, axis=0).astype(BF16)
        part = dot_nt(leg_ref[u], rhs_ref[u])
        for half in range(2):
            piece = part[:, 128 * half : 128 * half + 128]
            if u == 0:
                acc_ref[half] = piece
            else:
                acc_ref[half] += piece
    for dest in range(out_ref.shape[0]):
        halves = []
        for half in range(2):
            pieces = [
                acc_ref[half, pl.ds(dest * height + k, sub, stride=RUN), :] for k in range(RUN)
            ]
            halves.append(jnp.concatenate(pieces, axis=0))
        out_ref[dest, 0] = jnp.concatenate(halves, axis=1).astype(BF16)


def legendre_forward(pairs, spec, legendre, waves):
    slots, lats, rows = legendre.shape
    groups = slots // GROUP
    height = lats // waves
    return pl.pallas_call(
        functools.partial(forward_kernel, height),
        out_shape=jax.ShapeDtypeStruct((waves, groups, height, WIDE), BF16),
        grid=(groups,),
        in_specs=[
            pl.BlockSpec(memory_space=pltpu.SMEM),
            pl.BlockSpec((GROUP, COLS, rows), lambda g: (g, 0, 0)),
            pl.BlockSpec((GROUP, lats, rows), lambda g: (g, 0, 0)),
        ],
        out_specs=pl.BlockSpec((waves, 1, height, WIDE), lambda g: (0, g, 0, 0)),
        scratch_shapes=[
            pltpu.VMEM((GROUP, WIDE, rows), BF16),
            pltpu.VMEM((2, lats, 128), F32),
        ],
        compiler_params=pltpu.CompilerParams(vmem_limit_bytes=VMEM_LIMIT),
        cost_estimate=pl.CostEstimate(
            flops=2 * slots * lats * rows * WIDE,
            bytes_accessed=2 * slots * lats * rows,
            transcendentals=0,
        ),
        name="legendre_forward",
    )(pairs, spec, legendre)


def backward_kernel(height, pair_ref, perm_ref, coef_ref, leg_ref, out_ref, rows_ref):
    group = pl.program_id(0)
    rows = leg_ref.shape[2]
    sub = height // RUN
    for source in range(coef_ref.shape[0]):
        block = coef_ref[source, 0].astype(F32)
        for k in range(RUN):
            for half in range(2):
                rows_ref[half, pl.ds(source * height + k, sub, stride=RUN), :] = block[
                    k * sub : (k + 1) * sub, 128 * half : 128 * half + 128
                ]
    natural = jnp.concatenate([rows_ref[0], rows_ref[1]], axis=1).astype(BF16)
    turned = dot_nt(perm_ref[...], natural).astype(BF16)
    sums = []
    for u in range(GROUP):
        even, odd, sign = row_masks(pair_ref[group * GROUP + u], rows)
        raw = jnp.dot(turned[32 * u : 32 * u + 32], leg_ref[u], preferred_element_type=F32)
        low = raw[0:8] + sign * raw[8:16]
        high = raw[16:24] + sign * raw[24:32]
        sums.append(low * even + high * odd)
        if u % 2 == 1:
            out_ref[8 * (u - 1) : 8 * (u + 1), :] = jnp.concatenate(sums[-2:], axis=0).astype(BF16)


def legendre_backward(pairs, perm, coefs, legendre):
    slots, lats, rows = legendre.shape
    waves, groups, height, _ = coefs.shape
    return pl.pallas_call(
        functools.partial(backward_kernel, height),
        out_shape=jax.ShapeDtypeStruct((slots * COLS, rows), BF16),
        grid=(groups,),
        in_specs=[
            pl.BlockSpec(memory_space=pltpu.SMEM),
            pl.BlockSpec((WIDE, WIDE), lambda g: (0, 0)),
            pl.BlockSpec((waves, 1, height, WIDE), lambda g: (0, g, 0, 0)),
            pl.BlockSpec((GROUP, lats, rows), lambda g: (g, 0, 0)),
        ],
        out_specs=pl.BlockSpec((GROUP * COLS, rows), lambda g: (g, 0)),
        scratch_shapes=[pltpu.VMEM((2, lats, 128), F32)],
        compiler_params=pltpu.CompilerParams(vmem_limit_bytes=VMEM_LIMIT),
        cost_estimate=pl.CostEstimate(
            flops=2 * slots * lats * rows * 32,
            bytes_accessed=2 * slots * lats * rows,
            transcendentals=0,
        ),
        name="legendre_backward",
    )(pairs, perm, coefs, legendre)


def table_kernel(cos_ref, sin_ref, step_cos_ref, step_sin_ref, out_ref):
    def body(i, carry):
        rows = pl.ds(pl.multiple_of(i * 16, 16), 16)
        c, s = cos_ref[rows, :], sin_ref[rows, :]
        step_c, step_s = step_cos_ref[rows, :], step_sin_ref[rows, :]
        for tile in range(HALF // 128):
            out_ref[rows, 128 * tile : 128 * tile + 128] = c.astype(BF16)
            if tile < HALF // 128 - 1:
                c, s = c * step_c - s * step_s, s * step_c + c * step_s
        return carry

    lax.fori_loop(0, out_ref.shape[0] // 16, body, 0)


def angle_tables(slot_pair):
    flipped = M - 1 - slot_pair
    odd = slot_pair % 2 == 1
    waves = jnp.stack([jnp.where(odd, flipped, slot_pair), jnp.where(odd, slot_pair, flipped)])
    factor = jnp.where(waves == 0, 1.0, 2.0).astype(F32)
    waves2 = jnp.broadcast_to(waves[..., None], waves.shape + (2,)).reshape(-1)
    factor2 = jnp.broadcast_to(factor[..., None], factor.shape + (2,)).reshape(-1)
    part = jnp.arange(waves2.shape[0], dtype=jnp.int32) % 2
    column = jnp.arange(128, dtype=jnp.int32)
    unit = 2.0 * math.pi / NLON
    turn = (waves2[:, None] * column[None, :] + (NLON // 4) * part[:, None]) % NLON
    angle = turn.astype(F32) * unit
    first_cos = factor2[:, None] * jnp.cos(angle)
    first_sin = factor2[:, None] * jnp.sin(angle)
    step = ((waves2 * 128) % NLON).astype(F32) * unit
    shape = (waves2.shape[0], 128)
    step_cos = jnp.broadcast_to(jnp.cos(step)[:, None], shape)
    step_sin = jnp.broadcast_to(jnp.sin(step)[:, None], shape)
    spec = pl.BlockSpec((256, 128), lambda i: (i, 0))
    table = pl.pallas_call(
        table_kernel,
        out_shape=jax.ShapeDtypeStruct((shape[0], HALF), BF16),
        grid=(shape[0] // 256,),
        in_specs=[spec] * 4,
        out_specs=pl.BlockSpec((256, HALF), lambda i: (i, 0)),
        cost_estimate=pl.CostEstimate(
            flops=6 * shape[0] * HALF, bytes_accessed=2 * shape[0] * HALF, transcendentals=0
        ),
        name="angle_tables",
    )(first_cos, first_sin, step_cos, step_sin)
    scale = 1.0 / (factor * math.sqrt(NLON))
    scale2 = jnp.broadcast_to(scale[:, None, :, None], (2, 8) + (scale.shape[1], 2))
    return table.reshape(2, shape[0] // 2, HALF), scale2.reshape(2, 8, -1)


def swap_blocks(tiles, lane):
    tiles = list(tiles)
    for d in (4, 2, 1):
        low = (lane // (16 * d)) % 2 == 0
        for i in range(8):
            if i & d:
                continue
            a, b = tiles[i], tiles[i + d]
            tiles[i] = jnp.where(low, a, pltpu.roll(b, 16 * d, 1))
            tiles[i + d] = jnp.where(low, pltpu.roll(a, 128 - 16 * d, 1), b)
    return tiles


def middle_kernel(
    sub, edge_ref, recv_ref, halo_ref, perm_ref, taps_ref, scale_ref, weight_ref,
    table_hbm, depart_hbm, pick_hbm,
    arrival_ref, coef_ref,
    table_ref, depart_ref, pick_ref, left_ref, plus_ref, minus_ref, grid_ref, shift_ref,
    stage_ref, code_ref, moved_ref, pair_ref, sums_ref, sems,
):
    copies = [
        pltpu.make_async_copy(table_hbm, table_ref, sems.at[0]),
        pltpu.make_async_copy(depart_hbm, depart_ref, sems.at[1]),
        pltpu.make_async_copy(pick_hbm, pick_ref, sems.at[2]),
    ]
    for copy in copies:
        copy.start()
    own = FIELDS * RUN * 16
    is_first, is_last = edge_ref[0], edge_ref[1]

    def gather_rows(tile, carry):
        lane = lax.broadcasted_iota(jnp.int32, (1, 128), 1)
        lanes = pl.ds(pl.multiple_of(tile * 128, 128), 128)
        height = RUN * SUB
        rows = pl.ds(pl.multiple_of(tile * 8 * height, 8 * height), 8 * height)
        mixed = jnp.dot(recv_ref[rows, :], perm_ref[...], preferred_element_type=F32)
        edge_rows = pl.ds(pl.multiple_of(tile * 64, 64), 64)
        edges = jnp.dot(halo_ref[edge_rows, :], perm_ref[...], preferred_element_type=F32)
        for par in range(2):
            cols = slice(128 * par, 128 * par + 128)
            tiles = swap_blocks([mixed[b * height : (b + 1) * height, cols] for b in range(8)], lane)
            for f in range(FIELDS):
                for k in range(RUN):
                    at = (f * RUN + k) * 16
                    block = [tiles[h * 4 + f][8 * k : 8 * k + 8] for h in range(2)]
                    left_ref[par, at : at + 16, lanes] = jnp.concatenate(block, axis=0).astype(BF16)
            ends = swap_blocks([edges[8 * b : 8 * b + 8, cols] for b in range(8)], lane)
            row = lax.broadcasted_iota(jnp.int32, (8, 128), 0)
            if par == 1:
                sign = jnp.where((row < RIM) & (is_first == 1), -1.0, 1.0)
                ends = [end * sign for end in ends]
            across = (row >= RIM) & (is_last == 1)
            for f in range(FIELDS):
                block = [jnp.where(across, ends[(1 - h) * 4 + f], ends[h * 4 + f]) for h in range(2)]
                at = own + f * 16
                left_ref[par, at : at + 16, lanes] = jnp.concatenate(block, axis=0).astype(BF16)
        return carry

    lax.fori_loop(0, TILES, gather_rows, 0)
    copies[0].wait()

    def to_grid(tile, carry):
        cols = pl.ds(pl.multiple_of(tile * 256, 256), 256)
        even = jnp.dot(left_ref[0], table_ref[0, :, cols], preferred_element_type=F32)
        odd = jnp.dot(left_ref[1], table_ref[1, :, cols], preferred_element_type=F32)
        plus_ref[...] = even + odd
        minus_ref[...] = even - odd
        place = lax.broadcasted_iota(jnp.int32, (8, 256), 0)
        for side, ref in enumerate((plus_ref, minus_ref)):
            to = pl.ds(pl.multiple_of(128 + side * HALF + tile * 256, 128), 256)
            for f in range(FIELDS):
                for k in range(RUN):
                    at = (f * RUN + k) * 16
                    grid_ref[f * REACH + RIM + k, :, to] = ref[at : at + 16, :].astype(BF16)
                for k in range(RIM):
                    before, after = [], []
                    for h in range(2):
                        end = own + f * 16 + 8 * h
                        at = (f * RUN + k + RUN - RIM) * 16 + 8 * h
                        rolled = pltpu.roll(ref[at : at + 8, :], 1, 0)
                        before.append(jnp.where(place == 0, ref[end + k : end + k + 1, :], rolled))
                        at = (f * RUN + k) * 16 + 8 * h
                        rolled = pltpu.roll(ref[at : at + 8, :], 7, 0)
                        end = end + RIM
                        after.append(
                            jnp.where(place == sub - 1, ref[end + k : end + k + 1, :], rolled)
                        )
                    grid_ref[f * REACH + k, :, to] = jnp.concatenate(before, 0).astype(BF16)
                    grid_ref[f * REACH + RIM + RUN + k, :, to] = jnp.concatenate(after, 0).astype(
                        BF16
                    )
        return carry

    lax.fori_loop(0, HALF // 256, to_grid, 0)
    grid_ref[:, :, 0:128] = grid_ref[:, :, NLON : NLON + 128]
    grid_ref[:, :, NLON + 128 : NLON + 256] = grid_ref[:, :, 128:256]
    copies[1].wait()
    copies[2].wait()

    def interpolate(tile, carry):
        lanes = pl.ds(pl.multiple_of(tile * 128, 128), 128)
        window = pl.ds(pl.multiple_of(tile * 128, 128), 384)
        for row in range(FIELDS * REACH):
            wide = grid_ref[row, :, window]
            for c in range(-RIM, RIM + 1):
                shift_ref[c + RIM, row] = wide[:, 128 + c : 256 + c]
        for h in range(2):
            code_ref[h] = pick_ref[h, :, lanes] * 16 + depart_ref[h, :, lanes]
        for k in range(RUN):
            index, column = [], []
            for h in range(2):
                code = code_ref[h, pl.ds(k, SUB, stride=RUN), :]
                index.append(code >> 2)
                column.append(code & 3)
            column = jnp.concatenate(column, axis=0).astype(F32).astype(BF16)
            hits = [column == jnp.asarray(d, BF16) for d in range(4)]
            totals = [jnp.zeros((16, 128), F32) for _ in range(FIELDS)]
            for r in range(7):
                weights = []
                for b in range(4):
                    entry = taps_ref[r * 4 + b]
                    found = [jnp.take_along_axis(entry, index[h], axis=1) for h in range(2)]
                    weights.append(jnp.concatenate(found, axis=0).astype(BF16))
                factors = []
                for c in range(-RIM, RIM + 1):
                    factor = jnp.zeros((16, 128), BF16)
                    for d in range(4):
                        b = c - (d - 2) + 1
                        if 0 <= b < 4:
                            factor = jnp.where(hits[d], weights[b], factor)
                    factors.append(factor)
                for f in range(FIELDS):
                    row = f * REACH + k + r
                    part = factors[0] * shift_ref[0, row]
                    for c in range(1, 7):
                        part = part + factors[c] * shift_ref[c, row]
                    totals[f] = totals[f] + part.astype(F32)
            for f in range(FIELDS):
                at = (f * RUN + k) * 16
                moved_ref[at : at + 16, lanes] = totals[f].astype(BF16)
                for h in range(2):
                    stage_ref[f * 2 + h, pl.ds(k, SUB, stride=RUN), :] = totals[f][
                        8 * h : 8 * h + 8
                    ]
        for f in range(FIELDS):
            for h in range(2):
                arrival_ref[f, h, :, lanes] = stage_ref[f * 2 + h].astype(BF16)
        return carry

    lax.fori_loop(0, BLOCKS, interpolate, 0)

    def fold(tile, carry):
        lanes = pl.ds(pl.multiple_of(tile * 128, 128), 128)
        other = pl.ds(pl.multiple_of(tile * 128 + HALF, 128), 128)
        a, b = moved_ref[:, lanes].astype(F32), moved_ref[:, other].astype(F32)
        pair_ref[0, :, lanes] = (a + b).astype(BF16)
        pair_ref[1, :, lanes] = (a - b).astype(BF16)
        return carry

    lax.fori_loop(0, HALF // 128, fold, 0)

    def to_waves(tile, carry):
        cols = pl.ds(pl.multiple_of(tile * 256, 256), 256)
        for par in range(2):
            out = dot_nt(pair_ref[par], table_ref[par, cols, :])
            out = out * scale_ref[par, 0:1, cols]
            for half in range(2):
                part = out[:, 128 * half : 128 * half + 128] * weight_ref[...]
                sums_ref[par, tile * 2 + half] = part
        return carry

    lax.fori_loop(0, TILES // 2, to_waves, 0)

    def scatter_rows(tile, carry):
        lane = lax.broadcasted_iota(jnp.int32, (1, 128), 1)
        height = RUN * SUB
        halves = []
        for par in range(2):
            tiles = []
            for h in range(2):
                for f in range(FIELDS):
                    pieces = []
                    for k in range(RUN):
                        at = (f * RUN + k) * 16 + 8 * h
                        pieces.append(sums_ref[par, tile, at : at + 8, :])
                    tiles.append(jnp.concatenate(pieces, axis=0))
            halves.append(jnp.concatenate(swap_blocks(tiles, lane), axis=0))
        rows = pl.ds(pl.multiple_of(tile * 8 * height, 8 * height), 8 * height)
        coef_ref[rows, :] = jnp.concatenate(halves, axis=1).astype(BF16)
        return carry

    lax.fori_loop(0, TILES, scatter_rows, 0)


def transport(sub, edge, recv, halo, perm, taps, scale, weight, table, depart, pick):
    rows, width = recv.shape
    lats = RUN * SUB
    left = FIELDS * (RUN + 1) * 16
    own = FIELDS * RUN * 16
    slots2 = table.shape[1]
    vmem = pl.BlockSpec(memory_space=pltpu.VMEM)
    anywhere = pl.BlockSpec(memory_space=pl.ANY)
    return pl.pallas_call(
        functools.partial(middle_kernel, sub),
        out_shape=(
            jax.ShapeDtypeStruct((FIELDS, 2, lats, NLON), BF16),
            jax.ShapeDtypeStruct((rows, width), BF16),
        ),
        in_specs=[pl.BlockSpec(memory_space=pltpu.SMEM)] + [vmem] * 6 + [anywhere] * 3,
        out_specs=(vmem, vmem),
        scratch_shapes=[
            pltpu.VMEM((2, slots2, HALF), BF16),
            pltpu.VMEM((2, lats, NLON), jnp.int32),
            pltpu.VMEM((2, lats, NLON), jnp.int32),
            pltpu.VMEM((2, left, slots2), BF16),
            pltpu.VMEM((left, 256), F32),
            pltpu.VMEM((left, 256), F32),
            pltpu.VMEM((FIELDS * REACH, 16, NLON + 256), BF16),
            pltpu.VMEM((7, FIELDS * REACH, 16, 128), BF16),
            pltpu.VMEM((FIELDS * 2, lats, 128), F32),
            pltpu.VMEM((2, lats, 128), jnp.int32),
            pltpu.VMEM((own, NLON), BF16),
            pltpu.VMEM((2, own, HALF), BF16),
            pltpu.VMEM((2, TILES, own, 128), F32),
            pltpu.SemaphoreType.DMA((3,)),
        ],
        compiler_params=pltpu.CompilerParams(vmem_limit_bytes=VMEM_LIMIT),
        cost_estimate=pl.CostEstimate(
            flops=8 * left * slots2 * HALF,
            bytes_accessed=2 * rows * width * 8 + 4 * slots2 * HALF,
            transcendentals=0,
        ),
        name="transport",
    )(edge, recv, halo, perm, taps, scale, weight, table, depart, pick)


def tap_tables(stencil_weight):
    zero = jnp.zeros((NSTEN,), F32)
    rows = []
    for r in range(-3, 4):
        for b in range(4):
            picks = []
            for dy in range(-2, 2):
                a = r - dy + 1
                picks.append(stencil_weight[:, 4 * a + b] if 0 <= a < 4 else zero)
            rows.append(jnp.stack(picks, axis=1).reshape(-1))
    table = jnp.stack(rows)
    table = jnp.concatenate([table, jnp.zeros_like(table)], axis=1)
    return jnp.broadcast_to(table[:, None, :], (28, 8, 128))


def exchange(array, axis, distance):
    devices = lax.axis_size(axis)
    return lax.ppermute(array, axis, [(i, i ^ distance) for i in range(devices)])


def gather_rows(spectral):
    devices = lax.axis_size("band")
    band = lax.axis_index("band")
    turned = spectral.transpose(0, 2, 1)
    pieces = [turned] + [exchange(turned, "band", d) for d in range(1, devices)]
    stacked = jnp.stack(pieces)
    ordered = [
        lax.dynamic_index_in_dim(stacked, band ^ b, 0, keepdims=False) for b in range(devices)
    ]
    return jnp.concatenate(ordered, axis=2)


def scatter_sums(sums, slots, row_local):
    devices = lax.axis_size("band")
    band = lax.axis_index("band")
    shaped = sums.reshape(slots, COLS, -1)
    parts = jnp.stack(
        [shaped[:, :, b * row_local : (b + 1) * row_local] for b in range(devices)]
    )
    total = lax.dynamic_index_in_dim(parts, band, 0, keepdims=False).astype(F32)
    for d in range(1, devices):
        piece = lax.dynamic_index_in_dim(parts, band ^ d, 0, keepdims=False)
        total = total + exchange(piece, "band", d).astype(F32)
    return total.astype(BF16).transpose(0, 2, 1)


def per_device(
    spectral, legendre, slot_pair, quad_weight, depart_code, stencil_pick, stencil_weight
):
    slots, row_local, _ = spectral.shape
    height = depart_code.shape[2]
    waves = lax.axis_size("wave")
    sub = height // RUN
    groups = slots // GROUP
    wave_rank = lax.axis_index("wave")
    lat_rank = lax.axis_index(("band", "wave"))
    lat_devices = lax.axis_size(("band", "wave"))
    my_pairs = lax.dynamic_slice_in_dim(slot_pair, wave_rank * slots, slots)
    perm = lane_order()

    spec = gather_rows(spectral)
    sent = legendre_forward(my_pairs, spec, legendre, waves)
    table, scale = angle_tables(slot_pair)
    taps = tap_tables(stencil_weight)
    recv = lax.all_to_all(sent, "wave", split_axis=0, concat_axis=0, tiled=True)

    blocks = waves * groups
    shaped = recv.reshape(blocks, RUN, sub, WIDE)
    first = shaped[:, :RIM, 0]
    last = shaped[:, RUN - RIM :, sub - 1]
    up = [(i, i + 1) for i in range(lat_devices - 1)]
    down = [(i + 1, i) for i in range(lat_devices - 1)]
    before = lax.ppermute(last, ("band", "wave"), up)
    after = lax.ppermute(first, ("band", "wave"), down)
    is_first, is_last = lat_rank == 0, lat_rank == lat_devices - 1
    halo = [jnp.where(is_first, first[:, RIM - 1 - i], before[:, i]) for i in range(RIM)]
    halo += [jnp.where(is_last, last[:, RIM - 1 - i], after[:, i]) for i in range(RIM)]
    halo += [jnp.zeros_like(halo[0])] * (8 - 2 * RIM)
    halo = jnp.stack(halo, axis=1).reshape(blocks * 8, WIDE)
    edge = jnp.stack([is_first, is_last]).astype(jnp.int32)

    depart, pick = depart_code[0], stencil_pick[0]
    my_weight = lax.dynamic_slice_in_dim(quad_weight, wave_rank * height, height)
    weight = my_weight.reshape(sub, RUN).T
    if sub != SUB:
        gap = SUB - sub
        shaped = jnp.pad(shaped, ((0, 0), (0, 0), (0, gap), (0, 0)))
        depart = jnp.pad(depart, ((0, 0), (0, RUN * gap), (0, 0)))
        pick = jnp.pad(pick, ((0, 0), (0, RUN * gap), (0, 0)))
        weight = jnp.pad(weight, ((0, 0), (0, gap)))
    weight = jnp.broadcast_to(weight[None, :, None, :, None], (FIELDS, RUN, 2, SUB, 128))
    arrival, coefs = transport(
        sub,
        edge,
        shaped.reshape(blocks * RUN * SUB, WIDE),
        halo,
        perm,
        taps,
        scale,
        weight.reshape(-1, 128),
        table,
        depart,
        pick,
    )
    arrival = arrival[None, :, :, :height]
    coefs = coefs.reshape(blocks, RUN, SUB, WIDE)[:, :, :sub].reshape(waves, groups, height, WIDE)
    by_wave = lax.all_to_all(coefs, "wave", split_axis=0, concat_axis=0, tiled=True)
    sums = legendre_backward(my_pairs, perm, by_wave, legendre)
    return (arrival, scatter_sums(sums, slots, row_local))


def solution(mesh):
    in_specs = (
        P("wave", "band", None),
        P("wave", "band", None),
        P(),
        P("band"),
        P(None, None, ("band", "wave"), None),
        P(None, None, ("band", "wave"), None),
        P(),
    )
    out_specs = (P(None, None, None, ("band", "wave"), None), P("wave", "band", None))
    return jax.shard_map(
        per_device, mesh=mesh, in_specs=in_specs, out_specs=out_specs, check_vma=False
    )
```

time: 1570 us -> 331 us (0.21)
  local copies, waits for them, and re-layouts: 533 us -> 24.3 us
  other arithmetic: 504 us -> 12.9 us
  matrix products: 327 us -> 0 us
  Pallas kernels: 0 us -> 152 us
  waiting for transfers between devices: 122 us -> 70.5 us
    slice x29 -> x2, local copies, waits for them, and re-layouts: 370 us -> 0.48 us  [the longest x1 0.38 us: per_device(): first = shaped[:, :RIM, 0]]
    dot_general x5 -> x0, matrix products: 327 us -> none  [the longest x1 237 us: per_device(): jnp.dot(left_rows, angle_rows, preferred_element_type=jnp.float32)]
    dot_general x2 -> x0, other arithmetic: 227 us -> none  [the longest x1 225 us: per_device(): lax.dot_general(arrival.reshape(-1, NLON), angle_rows, (((1,), (1,)), (()...]
    pallas_call x0 -> x4, Pallas kernels: none -> 152 us  [the longest x1 81.4 us: transport(): pl.pallas_call(functools.partial(middle_kernel, sub), out_shape=(jax.Shap...]
    convert_element_type x7 -> x1, other arithmetic: 153 us -> 0.59 us  [per_device(): edge = jnp.stack([is_first, is_last]).astype(jnp.int32)]
    mul x22 -> x2, other arithmetic: 119 us -> 8.17 us  [the longest x1 8.17 us: angle_tables(): first_sin = factor2[:, None] * jnp.sin(angle)]
    unnamed x3 -> x0, waiting for transfers between devices: 75.7 us -> none
    ppermute x2 -> x8, waiting for transfers between devices: 0.01 us -> 42.3 us  [the longest x6 41.9 us: exchange(): lax.ppermute(array, axis, [(i, i ^ distance) for i in range(devices)])]
  transfers between devices with their start and end apart: 5 -> 9, of which waited for: 2 -> 7; matrix products, arithmetic and copies ran while one was open for 38% -> 7% of each run, Pallas kernels for 0% -> 4%
where the time goes in v1:
time: 331 us; the launch traced here: 330 us
  Pallas kernels  152 us (46%)
  waiting for transfers between devices  70.5 us (21%)
  blocking collectives  46.7 us (14%)
  local copies, waits for them, and re-layouts  24.3 us (7%)
  starting transfers between devices  22.3 us (7%)
  other arithmetic  12.9 us (4%)
    pallas_call x1, Pallas kernels, transport(): pl.pallas_call(functools.partial(middle_kernel, sub), out_shape=(jax.Shap...  81.4 us
    all_to_all x1, blocking collectives, per_device(): lax.all_to_all(coefs, 'wave', split_axis=0, concat_axis=0, tiled=True)  46.7 us
    ppermute x6, waiting for transfers between devices, exchange(): lax.ppermute(array, axis, [(i, i ^ distance) for i in range(devices)])  41.9 us
    pallas_call x1, Pallas kernels, legendre_forward(): pl.pallas_call(functools.partial(forward_kernel, height), out_shape=jax.S...  31.1 us
    all_to_all x1, waiting for transfers between devices, per_device(): recv = lax.all_to_all(sent, 'wave', split_axis=0, concat_axis=0, tiled=True)  28.2 us
    pallas_call x1, Pallas kernels, legendre_backward(): pl.pallas_call(functools.partial(backward_kernel, height), out_shape=jax....  26.4 us
    pallas_call x1, Pallas kernels, angle_tables(): pl.pallas_call(table_kernel, out_shape=jax.ShapeDtypeStruct((shape[0], HA...  13.5 us
    ppermute x6, starting transfers between devices, exchange(): lax.ppermute(array, axis, [(i, i ^ distance) for i in range(devices)])  12.7 us
  transfers between devices with their start and end apart: 9, of which 7 were waited for; matrix products, arithmetic and copies ran while one was open for 7% of the time, Pallas kernels for 4%

profile of v1, /device:TPU:0, one launch (start us, length us, event | category | flops | bytes accessed | tf_op | source)
XLA Modules:
  0.0 330.1 jit_solution(2310760077241114987)
XLA Ops:
  0.6 3.0 collective-permute-start
  3.6 1.5 collective-permute-start.1
  5.2 1.3 dynamic_slice.31.pair_ref
  6.5 9.4 %collective-permute-done = bf16[80,8,352]{2,1,0:T(8,128)(2,1)S(1)} collective-permute-done((bf16[80,8,352]{2,1,0:T(8,128)(2,1)}, bf16[80,8,352]{2,1,0:T(8,128)(2,1)S(1)}, u32[]{:S(2)}, u32[]{:S(2)}) %collective-permute-start) | collective-permute-done | bytes 450592 | tf_op jit(solution)/shard_map/ppermute | solution.py:466
  15.9 11.2 %collective-permute-done.1 = bf16[80,8,352]{2,1,0:T(8,128)(2,1)S(1)} collective-permute-done((bf16[80,8,352]{2,1,0:T(8,128)(2,1)}, bf16[80,8,352]{2,1,0:T(8,128)(2,1)S(1)}, u32[]{:S(2)}, u32[]{:S(2)}) %collective-permute-start.1) | collective-permute-done | bytes 450592 | tf_op jit(solution)/shard_map/ppermute | solution.py:466
  27.1 1.5 pad_maximum_fusion
  28.6 0.2 dynamic-slice_bitcast_fusion.3
  28.8 2.5 concatenate.14.spec_ref
  31.3 31.1 %legendre_forward.1 = bf16[8,10,40,256]{3,2,1,0:T(8,128)(2,1)} custom-call(s32[80]{0:T(128)} %dynamic_slice.31.pair_ref, bf16[80,8,1408]{2,1,0:T(8,128)(2,1)} %concatenate.14.spec_ref, bf16[80,320,1408]{2,1,0:T(8,128)(2,1)} %leg_ref.3), custom_call_target="tpu_custom_call" | custom-call | flops 18454937600 | bytes 72089600 | tf_op jit(solution)/shard_map/legendre_forward/pallas_call | solution.py:91
  62.3 5.0 %all-to-all-start = ((bf16[8,10,40,256]{3,2,1,0:T(8,128)(2,1)}), bf16[8,10,40,256]{3,2,1,0:T(8,128)(2,1)S(1)}, u32[]{:S(2)}, u32[]{:S(2)}) async-start(bf16[8,10,40,256]{3,2,1,0:T(8,128)(2,1)} %legendre_forward.1), calls=%async_computation | async-start | bytes 3276800 | tf_op jit(solution)/shard_map/all_to_all | solution.py:513
  68.8 0.2 broadcast_in_dim.70
  69.0 0.3 mul.98
  69.4 0.2 broadcast_in_dim.71
  69.6 0.3 mul.100
  70.2 8.2 %sine_multiply_fusion = (f32[2560,128]{1,0:T(8,128)}, f32[2560,128]{1,0:T(8,128)}) fusion(s32[2560]{0:T(1024)S(1)} %fusion.9, s32[2560]{0:T(1024)S(1)} %mul.100, f32[2560]{0:T(1024)S(1)} %mul.98), kind=kLoop, calls=%fused_computation.5 | loop fusion | flops 3932160 | bytes 2652160 | tf_op jit(solution)/shard_map/mul | solution.py:191
  78.4 28.2 %all-to-all-done = bf16[8,10,40,256]{3,2,1,0:T(8,128)(2,1)S(1)} async-done(((bf16[8,10,40,256]{3,2,1,0:T(8,128)(2,1)}), bf16[8,10,40,256]{3,2,1,0:T(8,128)(2,1)S(1)}, u32[]{:S(2)}, u32[]{:S(2)}) %all-to-all-start) | async-done | bytes 1638432 | tf_op jit(solution)/shard_map/all_to_all | solution.py:513
  106.6 0.4 fusion.34
  107.1 1.3 collective-permute-start.4
  113.3 0.1 stack.185
  113.5 0.8 dynamic_slice.36
  114.4 0.1 broadcast_in_dim.68
  114.5 0.2 broadcast_in_dim.32
  114.7 0.4 broadcast_in_dim.33
  115.1 1.5 broadcast_in_dim.72.step_cos_ref
  116.6 1.5 broadcast_in_dim.73.step_sin_ref
  118.1 13.5 %angle_tables.1 = bf16[2560,2560]{1,0:T(8,128)(2,1)} custom-call(f32[2560,128]{1,0:T(8,128)} %get-tuple-element.26.cos_ref, f32[2560,128]{1,0:T(8,128)} %get-tuple-element.25.sin_ref, f32[2560,128]{1,0:T(8,128)} %broadcast_in_dim.72.step_cos_ref, f32[2560,128]{1,0:T(8,128)} %broadcast_in_dim.73.step_sin_ref), custom_call_target="tpu_custom_call" | custom-call | flops 39321600 | bytes 13107200 | tf_op jit(solution)/shard_map/angle_tables/pallas_call | solution.py:197
  131.6 0.6 add_convert_fusion.edge_ref
  132.3 3.2 collective-permute-start.3
  135.6 0.4 broadcast_select_fusion
  136.0 0.4 collective-permute-done.3
  136.4 0.4 broadcast_select_fusion.3
  136.9 3.1 stack.156
  139.9 0.7 broadcast_in_dim.30.taps_ref
  140.6 0.8 broadcast_in_dim.69.weight_ref
  141.4 0.6 broadcast_in_dim.34.scale_ref
  142.0 81.4 %transport.1 = (bf16[4,2,40,5120]{3,2,1,0:T(8,128)(2,1)}, bf16[3200,256]{1,0:T(8,128)(2,1)}) custom-call(s32[2]{0:T(128)} %add_convert_fusion.edge_ref, bf16[3200,256]{1,0:T(8,128)(2,1)} %bitcast.54, bf16[640,256]{1,0:T(8,128)(2,1)} %bitcast.67, bf16[256,256]{1,0:T(8,128)(2,1)} %constant.107.clone.perm_ref, f32[28,8,128]{2,1,0:T(8,128)} %broadcast_in_dim.30.taps_ref, ...), custom_call_target="tpu_custom_call" | custom-call | flops 10066329600 | bytes 26214400 | tf_op jit(solution)/shard_map/transport/pallas_call | solution.py:415
  223.4 46.7 %all_to_all.10.coef_ref = bf16[8,10,40,256]{3,2,1,0:T(8,128)(2,1)} all-to-all(bf16[8,10,40,256]{3,2,1,0:T(8,128)(2,1)} %bitcast.55), channel_id=1, replica_groups=mesh['band'=4,'wave'=8] {'wave'}, dimensions={0} | all-to-all | bytes 3276800 | tf_op jit(solution)/shard_map/all_to_all | solution.py:555
  270.2 26.4 %legendre_backward.1 = bf16[640,1408]{1,0:T(8,128)(2,1)} custom-call(s32[80]{0:T(128)} %dynamic_slice.31.pair_ref, bf16[256,256]{1,0:T(8,128)(2,1)} %constant.107.clone.perm_ref, bf16[8,10,40,256]{3,2,1,0:T(8,128)(2,1)} %all_to_all.10.coef_ref, bf16[80,320,1408]{2,1,0:T(8,128)(2,1)} %leg_ref.3), custom_call_target="tpu_custom_call" | custom-call | flops 2306867200 | bytes 72089600 | tf_op jit(solution)/shard_map/legendre_backward/pallas_call | solution.py:142
  296.6 2.3 slice_bitcast_fusion.3
  298.8 0.5 pad_maximum_fusion.1
  299.3 0.2 dynamic-slice_bitcast_fusion.2
  299.5 5.2 %collective-permute-start.5 = (bf16[80,8,352]{2,1,0:T(8,128)(2,1)S(1)}, bf16[80,8,352]{2,1,0:T(8,128)(2,1)S(1)}, u32[]{:S(2)}, u32[]{:S(2)}) collective-permute-start(bf16[80,8,352]{2,1,0:T(8,128)(2,1)S(1)} %get-tuple-element.6), channel_id=1, source_target_pairs={{0,8},{8,0},{16,24},{24,16},{1,9},{9,1},{17,25},{25,17},{2,10},{10... | collective-permute-start | bytes 1351688 | tf_op jit(solution)/shard_map/ppermute | solution.py:466
  304.6 1.6 collective-permute-start.6
  306.3 1.4 collective-permute-start.7
  307.7 9.0 %collective-permute-done.5 = bf16[80,8,352]{2,1,0:T(8,128)(2,1)S(1)} collective-permute-done((bf16[80,8,352]{2,1,0:T(8,128)(2,1)S(1)}, bf16[80,8,352]{2,1,0:T(8,128)(2,1)S(1)}, u32[]{:S(2)}, u32[]{:S(2)}) %collective-permute-start.5) | collective-permute-done | bytes 450592 | tf_op jit(solution)/shard_map/ppermute | solution.py:466
  316.7 10.5 %collective-permute-done.6 = bf16[80,8,352]{2,1,0:T(8,128)(2,1)S(1)} collective-permute-done((bf16[80,8,352]{2,1,0:T(8,128)(2,1)S(1)}, bf16[80,8,352]{2,1,0:T(8,128)(2,1)S(1)}, u32[]{:S(2)}, u32[]{:S(2)}) %collective-permute-start.6) | collective-permute-done | bytes 450592 | tf_op jit(solution)/shard_map/ppermute | solution.py:466
  327.2 1.8 collective-permute-done.7
  329.1 1.0 fusion.8
  (104 shorter events, 6.9 us)
Async XLA Ops:
  0.6 15.3 %collective-permute-start = (bf16[80,8,352]{2,1,0:T(8,128)(2,1)}, bf16[80,8,352]{2,1,0:T(8,128)(2,1)S(1)}, u32[]{:S(2)}, u32[]{:S(2)}) collective-permute-start(bf16[80,8,352]{2,1,0:T(8,128)(2,1)} %bitcast.60), channel_id=1, source_target_pairs={{0,8},{8,0},{16,24},{24,16},{1,9},{9,1},{17,25},{25,17},{2,10},{10... | collective-permute-start | bytes 1351688 | tf_op jit(solution)/shard_map/ppermute | solution.py:466
  3.6 23.4 %collective-permute-start.1 = (bf16[80,8,352]{2,1,0:T(8,128)(2,1)}, bf16[80,8,352]{2,1,0:T(8,128)(2,1)S(1)}, u32[]{:S(2)}, u32[]{:S(2)}) collective-permute-start(bf16[80,8,352]{2,1,0:T(8,128)(2,1)} %bitcast.61), channel_id=1, source_target_pairs={{0,16},{8,24},{16,0},{24,8},{1,17},{9,25},{17,1},{25,9},{2,18},{10... | collective-permute-start | bytes 1351688 | tf_op jit(solution)/shard_map/ppermute | solution.py:466
  5.2 21.9 %collective-permute-start.2 = (bf16[80,8,352]{2,1,0:T(8,128)(2,1)}, bf16[80,8,352]{2,1,0:T(8,128)(2,1)S(1)}, u32[]{:S(2)}, u32[]{:S(2)}) collective-permute-start(bf16[80,8,352]{2,1,0:T(8,128)(2,1)} %bitcast.62), channel_id=1, source_target_pairs={{0,24},{8,16},{16,8},{24,0},{1,25},{9,17},{17,9},{25,1},{2,26},{10... | collective-permute-start | bytes 1351688 | tf_op jit(solution)/shard_map/ppermute | solution.py:466
  62.3 5.0 %copy-start.1 = (f32[16,16]{1,0:T(8,128)S(1)}, f32[16,16]{1,0:T(8,128)}, u32[]{:S(2)}) copy-start(f32[16,16]{1,0:T(8,128)} %param.14) | copy-start | bytes 3076
  62.3 6.4 %copy-start.2 = (s32[640]{0:T(1024)S(1)}, s32[640]{0:T(1024)}, u32[]{:S(2)}) copy-start(s32[640]{0:T(1024)} %param.10) | copy-start | bytes 7684
  62.3 44.2 %all-to-all-start = ((bf16[8,10,40,256]{3,2,1,0:T(8,128)(2,1)}), bf16[8,10,40,256]{3,2,1,0:T(8,128)(2,1)S(1)}, u32[]{:S(2)}, u32[]{:S(2)}) async-start(bf16[8,10,40,256]{3,2,1,0:T(8,128)(2,1)} %legendre_forward.1), calls=%async_computation | async-start | bytes 3276800 | tf_op jit(solution)/shard_map/all_to_all | solution.py:513
  106.6 8.5 %copy-start = (bf16[8,10,40,256]{3,2,1,0:T(8,128)(2,1)}, bf16[8,10,40,256]{3,2,1,0:T(8,128)(2,1)S(1)}, u32[]{:S(2)}) copy-start(bf16[8,10,40,256]{3,2,1,0:T(8,128)(2,1)S(1)} %all-to-all-done) | copy-start | bytes 4915204
  107.1 28.5 %collective-permute-start.4 = (bf16[80,3,256]{2,1,0:T(4,128)(2,1)S(1)}, bf16[80,3,256]{2,1,0:T(4,128)(2,1)S(1)}, u32[]{:S(2)}, u32[]{:S(2)}) collective-permute-start(bf16[80,3,256]{2,1,0:T(4,128)(2,1)S(1)} %bitcast.56), channel_id=1, source_target_pairs={{1,0},{2,1},{3,2},{4,3},{5,4},{6,5},{7,6},{8,7},{9,8},{10,9},{11,1... | collective-permute-start | bytes 368648 | tf_op jit(solution)/shard_map/ppermute | solution.py:522
  132.3 4.0 %collective-permute-start.3 = (bf16[80,3,256]{2,1,0:T(4,128)(2,1)S(1)}, bf16[80,3,256]{2,1,0:T(4,128)(2,1)S(1)}, u32[]{:S(2)}, u32[]{:S(2)}) collective-permute-start(bf16[80,3,256]{2,1,0:T(4,128)(2,1)S(1)} %bitcast.58), channel_id=1, source_target_pairs={{0,1},{1,2},{2,3},{3,4},{4,5},{5,6},{6,7},{7,8},{8,9},{9,10},{10,1... | collective-permute-start | bytes 368648 | tf_op jit(solution)/shard_map/ppermute | solution.py:521
  299.5 17.2 %collective-permute-start.5 = (bf16[80,8,352]{2,1,0:T(8,128)(2,1)S(1)}, bf16[80,8,352]{2,1,0:T(8,128)(2,1)S(1)}, u32[]{:S(2)}, u32[]{:S(2)}) collective-permute-start(bf16[80,8,352]{2,1,0:T(8,128)(2,1)S(1)} %get-tuple-element.6), channel_id=1, source_target_pairs={{0,8},{8,0},{16,24},{24,16},{1,9},{9,1},{17,25},{25,17},{2,10},{10... | collective-permute-start | bytes 1351688 | tf_op jit(solution)/shard_map/ppermute | solution.py:466
  304.6 22.6 %collective-permute-start.6 = (bf16[80,8,352]{2,1,0:T(8,128)(2,1)S(1)}, bf16[80,8,352]{2,1,0:T(8,128)(2,1)S(1)}, u32[]{:S(2)}, u32[]{:S(2)}) collective-permute-start(bf16[80,8,352]{2,1,0:T(8,128)(2,1)S(1)} %get-tuple-element.8), channel_id=1, source_target_pairs={{0,16},{8,24},{16,0},{24,8},{1,17},{9,25},{17,1},{25,9},{2,18},{10... | collective-permute-start | bytes 1351688 | tf_op jit(solution)/shard_map/ppermute | solution.py:466
  306.3 22.8 %collective-permute-start.7 = (bf16[80,8,352]{2,1,0:T(8,128)(2,1)S(1)}, bf16[80,8,352]{2,1,0:T(8,128)(2,1)S(1)}, u32[]{:S(2)}, u32[]{:S(2)}) collective-permute-start(bf16[80,8,352]{2,1,0:T(8,128)(2,1)S(1)} %get-tuple-element.7), channel_id=1, source_target_pairs={{0,24},{8,16},{16,8},{24,0},{1,25},{9,17},{17,9},{25,1},{2,26},{10... | collective-permute-start | bytes 1351688 | tf_op jit(solution)/shard_map/ppermute | solution.py:466

commit v2 on v1

--- a/solution.py
+++ b/solution.py
@@ -52,28 +52,21 @@
     return even, odd, sign
 
 
-def forward_kernel(height, pair_ref, spec_ref, leg_ref, out_ref, rhs_ref, acc_ref):
-    group = pl.program_id(0)
+def forward_kernel(height, base, pair_ref, spec_ref, leg_ref, out_ref, acc_ref):
+    group = pl.program_id(0) + base
     rows = spec_ref.shape[2]
     sub = height // RUN
 
-    @pl.when(group == 0)
-    def _():
-        rhs_ref[...] = jnp.zeros_like(rhs_ref)
-
+    pieces = []
     for u in range(GROUP):
         even, odd, sign = row_masks(pair_ref[group * GROUP + u], rows)
         spec = spec_ref[u].astype(F32)
         south = spec * sign
         parts = [spec * even, south * even, spec * odd, south * odd]
-        rhs_ref[u, 32 * u : 32 * u + 32, :] = jnp.concatenate(parts, axis=0).astype(BF16)
-        part = dot_nt(leg_ref[u], rhs_ref[u])
-        for half in range(2):
-            piece = part[:, 128 * half : 128 * half + 128]
-            if u == 0:
-                acc_ref[half] = piece
-            else:
-                acc_ref[half] += piece
+        masked = jnp.concatenate(parts, axis=0).astype(BF16)
+        pieces.append(dot_nt(leg_ref[u], masked))
+        if u % 4 == 3:
+            acc_ref[u // 4] = jnp.concatenate(pieces[-4:], axis=1)
     for dest in range(out_ref.shape[0]):
         halves = []
         for half in range(2):
@@ -84,36 +77,34 @@
         out_ref[dest, 0] = jnp.concatenate(halves, axis=1).astype(BF16)
 
 
-def legendre_forward(pairs, spec, legendre, waves):
+def legendre_forward(pairs, spec, legendre, waves, part, parts):
     slots, lats, rows = legendre.shape
-    groups = slots // GROUP
+    groups = slots // GROUP // parts
+    base = part * groups
     height = lats // waves
     return pl.pallas_call(
-        functools.partial(forward_kernel, height),
+        functools.partial(forward_kernel, height, base),
         out_shape=jax.ShapeDtypeStruct((waves, groups, height, WIDE), BF16),
         grid=(groups,),
         in_specs=[
             pl.BlockSpec(memory_space=pltpu.SMEM),
-            pl.BlockSpec((GROUP, COLS, rows), lambda g: (g, 0, 0)),
-            pl.BlockSpec((GROUP, lats, rows), lambda g: (g, 0, 0)),
+            pl.BlockSpec((GROUP, COLS, rows), lambda g: (g + base, 0, 0)),
+            pl.BlockSpec((GROUP, lats, rows), lambda g: (g + base, 0, 0)),
         ],
         out_specs=pl.BlockSpec((waves, 1, height, WIDE), lambda g: (0, g, 0, 0)),
-        scratch_shapes=[
-            pltpu.VMEM((GROUP, WIDE, rows), BF16),
-            pltpu.VMEM((2, lats, 128), F32),
-        ],
+        scratch_shapes=[pltpu.VMEM((2, lats, 128), F32)],
         compiler_params=pltpu.CompilerParams(vmem_limit_bytes=VMEM_LIMIT),
         cost_estimate=pl.CostEstimate(
-            flops=2 * slots * lats * rows * WIDE,
-            bytes_accessed=2 * slots * lats * rows,
+            flops=2 * groups * GROUP * lats * rows * 32,
+            bytes_accessed=2 * groups * GROUP * lats * rows,
             transcendentals=0,
         ),
         name="legendre_forward",
     )(pairs, spec, legendre)
 
 
-def backward_kernel(height, pair_ref, perm_ref, coef_ref, leg_ref, out_ref, rows_ref):
-    group = pl.program_id(0)
+def backward_kernel(height, base, pair_ref, perm_ref, coef_ref, leg_ref, out_ref, rows_ref):
+    group = pl.program_id(0) + base
     rows = leg_ref.shape[2]
     sub = height // RUN
     for source in range(coef_ref.shape[0]):
@@ -136,18 +127,20 @@
             out_ref[8 * (u - 1) : 8 * (u + 1), :] = jnp.concatenate(sums[-2:], axis=0).astype(BF16)
 
 
-def legendre_backward(pairs, perm, coefs, legendre):
-    slots, lats, rows = legendre.shape
+def legendre_backward(pairs, perm, coefs, legendre, part):
+    _, lats, rows = legendre.shape
     waves, groups, height, _ = coefs.shape
+    slots = groups * GROUP
+    base = part * groups
     return pl.pallas_call(
-        functools.partial(backward_kernel, height),
+        functools.partial(backward_kernel, height, base),
         out_shape=jax.ShapeDtypeStruct((slots * COLS, rows), BF16),
         grid=(groups,),
         in_specs=[
             pl.BlockSpec(memory_space=pltpu.SMEM),
             pl.BlockSpec((WIDE, WIDE), lambda g: (0, 0)),
             pl.BlockSpec((waves, 1, height, WIDE), lambda g: (0, g, 0, 0)),
-            pl.BlockSpec((GROUP, lats, rows), lambda g: (g, 0, 0)),
+            pl.BlockSpec((GROUP, lats, rows), lambda g: (g + base, 0, 0)),
         ],
         out_specs=pl.BlockSpec((GROUP * COLS, rows), lambda g: (g, 0)),
         scratch_shapes=[pltpu.VMEM((2, lats, 128), F32)],
@@ -224,12 +217,15 @@
 
 
 def middle_kernel(
-    sub, edge_ref, recv_ref, halo_ref, perm_ref, taps_ref, scale_ref, weight_ref,
-    table_hbm, depart_hbm, pick_hbm,
-    arrival_ref, coef_ref,
+    sub, parts, edge_ref, halo_ref, perm_ref, taps_ref, scale_ref, weight_ref,
+    table_hbm, depart_hbm, pick_hbm, *refs,
+):
+    recv_refs, arrival_ref, coef_refs = refs[:parts], refs[parts], refs[parts + 1 : 2 * parts + 1]
+    (
     table_ref, depart_ref, pick_ref, left_ref, plus_ref, minus_ref, grid_ref, shift_ref,
     stage_ref, code_ref, moved_ref, pair_ref, sums_ref, sems,
-):
+    ) = refs[2 * parts + 1 :]
+    per_part = TILES // parts
     copies = [
         pltpu.make_async_copy(table_hbm, table_ref, sems.at[0]),
         pltpu.make_async_copy(depart_hbm, depart_ref, sems.at[1]),
@@ -240,12 +236,13 @@
     own = FIELDS * RUN * 16
     is_first, is_last = edge_ref[0], edge_ref[1]
 
-    def gather_rows(tile, carry):
+    def gather_rows(part, step, carry):
+        tile = part * per_part + step
         lane = lax.broadcasted_iota(jnp.int32, (1, 128), 1)
         lanes = pl.ds(pl.multiple_of(tile * 128, 128), 128)
         height = RUN * SUB
-        rows = pl.ds(pl.multiple_of(tile * 8 * height, 8 * height), 8 * height)
-        mixed = jnp.dot(recv_ref[rows, :], perm_ref[...], preferred_element_type=F32)
+        rows = pl.ds(pl.multiple_of(step * 8 * height, 8 * height), 8 * height)
+        mixed = jnp.dot(recv_refs[part][rows, :], perm_ref[...], preferred_element_type=F32)
         edge_rows = pl.ds(pl.multiple_of(tile * 64, 64), 64)
         edges = jnp.dot(halo_ref[edge_rows, :], perm_ref[...], preferred_element_type=F32)
         for par in range(2):
@@ -268,7 +265,8 @@
                 left_ref[par, at : at + 16, lanes] = jnp.concatenate(block, axis=0).astype(BF16)
         return carry
 
-    lax.fori_loop(0, TILES, gather_rows, 0)
+    for part in range(parts):
+        lax.fori_loop(0, per_part, functools.partial(gather_rows, part), 0)
     copies[0].wait()
 
     def to_grid(tile, carry):
@@ -383,7 +381,8 @@
 
     lax.fori_loop(0, TILES // 2, to_waves, 0)
 
-    def scatter_rows(tile, carry):
+    def scatter_rows(part, step, carry):
+        tile = part * per_part + step
         lane = lax.broadcasted_iota(jnp.int32, (1, 128), 1)
         height = RUN * SUB
         halves = []
@@ -397,15 +396,17 @@
                         pieces.append(sums_ref[par, tile, at : at + 8, :])
                     tiles.append(jnp.concatenate(pieces, axis=0))
             halves.append(jnp.concatenate(swap_blocks(tiles, lane), axis=0))
-        rows = pl.ds(pl.multiple_of(tile * 8 * height, 8 * height), 8 * height)
-        coef_ref[rows, :] = jnp.concatenate(halves, axis=1).astype(BF16)
-        return carry
-
-    lax.fori_loop(0, TILES, scatter_rows, 0)
+        rows = pl.ds(pl.multiple_of(step * 8 * height, 8 * height), 8 * height)
+        coef_refs[part][rows, :] = jnp.concatenate(halves, axis=1).astype(BF16)
+        return carry
+
+    for part in range(parts):
+        lax.fori_loop(0, per_part, functools.partial(scatter_rows, part), 0)
 
 
 def transport(sub, edge, recv, halo, perm, taps, scale, weight, table, depart, pick):
-    rows, width = recv.shape
+    parts = len(recv)
+    rows, width = recv[0].shape
     lats = RUN * SUB
     left = FIELDS * (RUN + 1) * 16
     own = FIELDS * RUN * 16
@@ -413,13 +414,13 @@
     vmem = pl.BlockSpec(memory_space=pltpu.VMEM)
     anywhere = pl.BlockSpec(memory_space=pl.ANY)
     return pl.pallas_call(
-        functools.partial(middle_kernel, sub),
+        functools.partial(middle_kernel, sub, parts),
         out_shape=(
             jax.ShapeDtypeStruct((FIELDS, 2, lats, NLON), BF16),
-            jax.ShapeDtypeStruct((rows, width), BF16),
+            *[jax.ShapeDtypeStruct((rows, width), BF16)] * parts,
         ),
-        in_specs=[pl.BlockSpec(memory_space=pltpu.SMEM)] + [vmem] * 6 + [anywhere] * 3,
-        out_specs=(vmem, vmem),
+        in_specs=[pl.BlockSpec(memory_space=pltpu.SMEM)] + [vmem] * 5 + [anywhere] * 3 + [vmem] * parts,
+        out_specs=(vmem,) * (parts + 1),
         scratch_shapes=[
             pltpu.VMEM((2, slots2, HALF), BF16),
             pltpu.VMEM((2, lats, NLON), jnp.int32),
@@ -443,7 +444,7 @@
             transcendentals=0,
         ),
         name="transport",
-    )(edge, recv, halo, perm, taps, scale, weight, table, depart, pick)
+    )(edge, halo, perm, taps, scale, weight, table, depart, pick, *recv)
 
 
 def tap_tables(stencil_weight):
@@ -506,55 +507,78 @@
     my_pairs = lax.dynamic_slice_in_dim(slot_pair, wave_rank * slots, slots)
     perm = lane_order()
 
+    parts = 2 if groups % 2 == 0 else 1
+    blocks = waves * groups
+    arriving = slot_pair.reshape(waves, parts, -1).swapaxes(0, 1).reshape(-1)
+
     spec = gather_rows(spectral)
-    sent = legendre_forward(my_pairs, spec, legendre, waves)
-    table, scale = angle_tables(slot_pair)
+    table, scale = angle_tables(arriving)
     taps = tap_tables(stencil_weight)
-    recv = lax.all_to_all(sent, "wave", split_axis=0, concat_axis=0, tiled=True)
-
-    blocks = waves * groups
-    shaped = recv.reshape(blocks, RUN, sub, WIDE)
-    first = shaped[:, :RIM, 0]
-    last = shaped[:, RUN - RIM :, sub - 1]
+    my_weight = lax.dynamic_slice_in_dim(quad_weight, wave_rank * height, height)
+    weight = my_weight.reshape(sub, RUN).T
+    if sub != SUB:
+        weight = jnp.pad(weight, ((0, 0), (0, SUB - sub)))
+    weight = jnp.broadcast_to(weight[None, :, None, :, None], (FIELDS, RUN, 2, SUB, 128))
+    weight = weight.reshape(-1, 128)
+    is_first, is_last = lat_rank == 0, lat_rank == lat_devices - 1
+    edge = jnp.stack([is_first, is_last]).astype(jnp.int32)
+    spec, table, scale, taps, weight, edge, my_pairs = lax.optimization_barrier(
+        (spec, table, scale, taps, weight, edge, my_pairs)
+    )
+    received = []
+    for part in range(parts):
+        sent = legendre_forward(my_pairs, spec, legendre, waves, part, parts)
+        if received:
+            sent, received[-1] = lax.optimization_barrier((sent, received[-1]))
+        received.append(
+            lax.all_to_all(sent, "wave", split_axis=0, concat_axis=0, tiled=True)
+        )
+    recv = [r.reshape(-1, height, WIDE) for r in received]
+    first = jnp.concatenate([r[:, 0 : RIM * sub : sub] for r in recv])
+    last = jnp.concatenate([r[:, (RUN - RIM + 1) * sub - 1 :: sub] for r in recv])
     up = [(i, i + 1) for i in range(lat_devices - 1)]
     down = [(i + 1, i) for i in range(lat_devices - 1)]
     before = lax.ppermute(last, ("band", "wave"), up)
     after = lax.ppermute(first, ("band", "wave"), down)
-    is_first, is_last = lat_rank == 0, lat_rank == lat_devices - 1
     halo = [jnp.where(is_first, first[:, RIM - 1 - i], before[:, i]) for i in range(RIM)]
     halo += [jnp.where(is_last, last[:, RIM - 1 - i], after[:, i]) for i in range(RIM)]
     halo += [jnp.zeros_like(halo[0])] * (8 - 2 * RIM)
     halo = jnp.stack(halo, axis=1).reshape(blocks * 8, WIDE)
-    edge = jnp.stack([is_first, is_last]).astype(jnp.int32)
 
     depart, pick = depart_code[0], stencil_pick[0]
-    my_weight = lax.dynamic_slice_in_dim(quad_weight, wave_rank * height, height)
-    weight = my_weight.reshape(sub, RUN).T
     if sub != SUB:
         gap = SUB - sub
-        shaped = jnp.pad(shaped, ((0, 0), (0, 0), (0, gap), (0, 0)))
+        recv = [r.reshape(-1, RUN, sub, WIDE) for r in recv]
+        recv = [jnp.pad(r, ((0, 0), (0, 0), (0, gap), (0, 0))) for r in recv]
         depart = jnp.pad(depart, ((0, 0), (0, RUN * gap), (0, 0)))
         pick = jnp.pad(pick, ((0, 0), (0, RUN * gap), (0, 0)))
-        weight = jnp.pad(weight, ((0, 0), (0, gap)))
-    weight = jnp.broadcast_to(weight[None, :, None, :, None], (FIELDS, RUN, 2, SUB, 128))
-    arrival, coefs = transport(
+    arrival, *coefs = transport(
         sub,
         edge,
-        shaped.reshape(blocks * RUN * SUB, WIDE),
+        [r.reshape(-1, WIDE) for r in recv],
         halo,
         perm,
         taps,
         scale,
-        weight.reshape(-1, 128),
+        weight,
         table,
         depart,
         pick,
     )
     arrival = arrival[None, :, :, :height]
-    coefs = coefs.reshape(blocks, RUN, SUB, WIDE)[:, :, :sub].reshape(waves, groups, height, WIDE)
-    by_wave = lax.all_to_all(coefs, "wave", split_axis=0, concat_axis=0, tiled=True)
-    sums = legendre_backward(my_pairs, perm, by_wave, legendre)
-    return (arrival, scatter_sums(sums, slots, row_local))
+    coefs = [c.reshape(-1, RUN, SUB, WIDE)[:, :, :sub] for c in coefs]
+    outs, by_wave = [], None
+    for part in range(parts):
+        leaving = coefs[part].reshape(waves, groups // parts, height, WIDE)
+        if part:
+            leaving, by_wave = lax.optimization_barrier((leaving, by_wave))
+        ready = by_wave
+        by_wave = lax.all_to_all(leaving, "wave", split_axis=0, concat_axis=0, tiled=True)
+        if part:
+            outs.append(legendre_backward(my_pairs, perm, ready, legendre, part - 1))
+    outs.append(legendre_backward(my_pairs, perm, by_wave, legendre, parts - 1))
+    outs = [scatter_sums(sums, slots // parts, row_local) for sums in outs]
+    return (arrival, jnp.concatenate(outs))
 
 
 def solution(mesh):

time: 331 us -> 304 us (0.918)
  waiting for transfers between devices: 70.5 us -> 37 us
  blocking collectives: 46.7 us -> 29.2 us
  starting transfers between devices: 22.3 us -> 34.7 us
  local copies, waits for them, and re-layouts: 24.3 us -> 31.2 us
  Pallas kernels: 152 us -> 158 us
    ppermute x6 -> x9, waiting for transfers between devices: 41.9 us -> 10.6 us  [exchange(): lax.ppermute(array, axis, [(i, i ^ distance) for i in range(devices)])]
    all_to_all x1, blocking collectives: 46.7 us -> 29.2 us  [per_device(): lax.all_to_all(leaving, 'wave', split_axis=0, concat_axis=0, tiled=True)]
    all_to_all x1 -> x3, starting transfers between devices: 5.01 us -> 12.4 us  [the longest x2 8.88 us: per_device(): lax.all_to_all(sent, 'wave', split_axis=0, concat_axis=0, tiled=True)]
    pallas_call x3 -> x5, Pallas kernels: 139 us -> 144 us  [the longest x1 81.5 us: transport(): pl.pallas_call(functools.partial(middle_kernel, sub, parts), out_shape=(j...]
    ppermute x6 -> x9, starting transfers between devices: 12.7 us -> 17.8 us  [exchange(): lax.ppermute(array, axis, [(i, i ^ distance) for i in range(devices)])]
    all_to_all x1 -> x3, waiting for transfers between devices: 28.2 us -> 26 us  [the longest x2 26 us: per_device(): lax.all_to_all(sent, 'wave', split_axis=0, concat_axis=0, tiled=True)]
  transfers between devices with their start and end apart: 9 -> 14, of which waited for: 7 -> 5; matrix products, arithmetic and copies ran while one was open for 7% -> 11% of each run, Pallas kernels for 4% -> 20%
where the time goes in v2:
time: 304 us; the launch traced here: 303 us
  Pallas kernels  158 us (52%)
  waiting for transfers between devices  37 us (12%)
  starting transfers between devices  34.7 us (11%)
  local copies, waits for them, and re-layouts  31.2 us (10%)
  blocking collectives  29.2 us (10%)
  other arithmetic  12.2 us (4%)
    pallas_call x1, Pallas kernels, transport(): pl.pallas_call(functools.partial(middle_kernel, sub, parts), out_shape=(j...  81.5 us
    pallas_call x2, Pallas kernels, legendre_forward(): pl.pallas_call(functools.partial(forward_kernel, height, base), out_shape...  33.4 us
    pallas_call x2, Pallas kernels, legendre_backward(): pl.pallas_call(functools.partial(backward_kernel, height, base), out_shap...  29.4 us
    all_to_all x1, blocking collectives, per_device(): lax.all_to_all(leaving, 'wave', split_axis=0, concat_axis=0, tiled=True)  29.2 us
    all_to_all x2, waiting for transfers between devices, per_device(): lax.all_to_all(sent, 'wave', split_axis=0, concat_axis=0, tiled=True)  26 us
    ppermute x9, starting transfers between devices, exchange(): lax.ppermute(array, axis, [(i, i ^ distance) for i in range(devices)])  17.8 us
    pallas_call x1, Pallas kernels, angle_tables(): pl.pallas_call(table_kernel, out_shape=jax.ShapeDtypeStruct((shape[0], HA...  13.6 us
    ppermute x9, waiting for transfers between devices, exchange(): lax.ppermute(array, axis, [(i, i ^ distance) for i in range(devices)])  10.6 us
  transfers between devices with their start and end apart: 14, of which 5 were waited for; matrix products, arithmetic and copies ran while one was open for 11% of the time, Pallas kernels for 20%

profile of v2, /device:TPU:0, one launch (start us, length us, event | category | flops | bytes accessed | tf_op | source)
XLA Modules:
  0.0 303.2 jit_solution(15909559932861482553)
XLA Ops:
  0.6 3.0 collective-permute-start
  3.6 1.5 collective-permute-start.1
  5.2 0.8 reshape.235
  6.1 1.4 fusion.43
  14.7 8.2 %sine_multiply_fusion = (f32[2560,128]{1,0:T(8,128)}, f32[2560,128]{1,0:T(8,128)}) fusion(s32[2560]{0:T(1024)S(1)} %fusion.19, s32[2560]{0:T(1024)S(1)} %mul.95, f32[2560]{0:T(1024)S(1)} %mul.93), kind=kLoop, calls=%fused_computation.4 | loop fusion | flops 3932160 | bytes 2652160 | tf_op jit(solution)/shard_map/mul | solution.py:184
  23.3 0.8 dynamic_slice.48
  24.4 1.3 dynamic_slice.49.pair_ref
  25.9 0.4 broadcast_in_dim.71
  26.4 1.5 broadcast_in_dim.68.step_cos_ref
  27.9 1.5 broadcast_in_dim.69.step_sin_ref
  29.4 13.6 %angle_tables.1 = bf16[2560,2560]{1,0:T(8,128)(2,1)} custom-call(f32[2560,128]{1,0:T(8,128)} %get-tuple-element.57.cos_ref, f32[2560,128]{1,0:T(8,128)} %get-tuple-element.56.sin_ref, f32[2560,128]{1,0:T(8,128)} %broadcast_in_dim.68.step_cos_ref, f32[2560,128]{1,0:T(8,128)} %broadcast_in_dim.69.step_sin_ref), custom_call_target="tpu_custom_call" | custom-call | flops 39321600 | bytes 13107200 | tf_op jit(solution)/shard_map/angle_tables/pallas_call | solution.py:190
  42.9 0.6 add_convert_fusion.edge_ref
  43.5 0.5 pad_maximum_fusion
  44.2 2.5 concatenate.23.spec_ref
  46.7 0.7 broadcast_in_dim.73.taps_ref
  47.4 0.8 broadcast_in_dim.76.weight_ref
  48.1 0.6 broadcast_in_dim.72.scale_ref
  48.8 16.7 %legendre_forward.3 = bf16[8,5,40,256]{3,2,1,0:T(8,128)(2,1)} custom-call(s32[80]{0:T(128)} %dynamic_slice.49.pair_ref, bf16[80,8,1408]{2,1,0:T(8,128)(2,1)} %concatenate.23.spec_ref, bf16[80,320,1408]{2,1,0:T(8,128)(2,1)} %leg_ref.7), custom_call_target="tpu_custom_call" | custom-call | flops 1153433600 | bytes 36044800 | tf_op jit(solution)/shard_map/legendre_forward/pallas_call | solution.py:85
  65.5 5.3 %all-to-all-start = ((bf16[8,5,40,256]{3,2,1,0:T(8,128)(2,1)}), bf16[8,5,40,256]{3,2,1,0:T(8,128)(2,1)S(1)}, u32[]{:S(2)}, u32[]{:S(2)}) async-start(bf16[8,5,40,256]{3,2,1,0:T(8,128)(2,1)} %legendre_forward.3), calls=%async_computation | async-start | bytes 1638400 | tf_op jit(solution)/shard_map/all_to_all | solution.py:534
  70.8 16.7 %legendre_forward.2 = bf16[8,5,40,256]{3,2,1,0:T(8,128)(2,1)} custom-call(s32[80]{0:T(128)} %dynamic_slice.49.pair_ref, bf16[80,8,1408]{2,1,0:T(8,128)(2,1)} %concatenate.23.spec_ref, bf16[80,320,1408]{2,1,0:T(8,128)(2,1)} %leg_ref.7), custom_call_target="tpu_custom_call" | custom-call | flops 1153433600 | bytes 36044800 | tf_op jit(solution)/shard_map/legendre_forward/pallas_call | solution.py:85
  87.5 5.0 %all-to-all-done = bf16[8,5,40,256]{3,2,1,0:T(8,128)(2,1)S(1)} async-done(((bf16[8,5,40,256]{3,2,1,0:T(8,128)(2,1)}), bf16[8,5,40,256]{3,2,1,0:T(8,128)(2,1)S(1)}, u32[]{:S(2)}, u32[]{:S(2)}) %all-to-all-start) | async-done | bytes 819232 | tf_op jit(solution)/shard_map/all_to_all | solution.py:534
  92.5 3.5 %all-to-all-start.1 = ((bf16[8,5,40,256]{3,2,1,0:T(8,128)(2,1)}), bf16[8,5,40,256]{3,2,1,0:T(8,128)(2,1)S(1)}, u32[]{:S(2)}, u32[]{:S(2)}) async-start(bf16[8,5,40,256]{3,2,1,0:T(8,128)(2,1)} %legendre_forward.2), calls=%async_computation.1 | async-start | bytes 1638400 | tf_op jit(solution)/shard_map/all_to_all | solution.py:534
  96.0 0.5 slice.184
  96.6 21.1 %all-to-all-done.1 = bf16[8,5,40,256]{3,2,1,0:T(8,128)(2,1)S(1)} async-done(((bf16[8,5,40,256]{3,2,1,0:T(8,128)(2,1)}), bf16[8,5,40,256]{3,2,1,0:T(8,128)(2,1)S(1)}, u32[]{:S(2)}, u32[]{:S(2)}) %all-to-all-start.1) | async-done | bytes 819232 | tf_op jit(solution)/shard_map/all_to_all | solution.py:534
  117.6 0.5 slice.185
  118.3 1.3 collective-permute-start.4
  119.6 1.2 slice.187
  120.7 1.2 slice.188
  122.0 3.2 %collective-permute-start.3 = (bf16[80,3,256]{2,1,0:T(4,128)(2,1)S(1)}, bf16[80,3,256]{2,1,0:T(4,128)(2,1)S(1)}, u32[]{:S(2)}, u32[]{:S(2)}) collective-permute-start(bf16[80,3,256]{2,1,0:T(4,128)(2,1)S(1)} %pad_maximum_fusion.5), channel_id=1, source_target_pairs={{0,1},{1,2},{2,3},{3,4},{4,5},{5,6},{6,7},{7,8},{8,9},{9,10},{10,1... | collective-permute-start | bytes 368648 | tf_op jit(solution)/shard_map/ppermute | solution.py:541
  125.3 0.5 broadcast_select_fusion
  126.1 0.5 broadcast_select_fusion.3
  126.6 3.1 %stack.197 = bf16[80,8,256]{2,1,0:T(8,128)(2,1)} concatenate(bf16[80,1,256]{2,1,0:T(2,128)(2,1)S(1)} %get-tuple-element.55, bf16[80,1,256]{2,1,0:T(2,128)(2,1)S(1)} %get-tuple-element.54, bf16[80,1,256]{2,1,0:T(2,128)(2,1)S(1)} %get-tuple-element.53, bf16[80,1,256]{2,1,0:T(2,128)(2,1)S(1)} %get-tuple-element.52, bf16[80,1,256]{2,1,0:T(2,128)(2,1)S(1)} %get-tuple-element.51, ...), dimensions={1} | concatenate | bytes 655360 | tf_op jit(solution)/shard_map/stack | solution.py:546
  129.7 81.5 %transport.1 = (bf16[4,2,40,5120]{3,2,1,0:T(8,128)(2,1)}, bf16[1600,256]{1,0:T(8,128)(2,1)}, bf16[1600,256]{1,0:T(8,128)(2,1)}) custom-call(s32[2]{0:T(128)} %add_convert_fusion.edge_ref, bf16[640,256]{1,0:T(8,128)(2,1)} %bitcast.86, bf16[256,256]{1,0:T(8,128)(2,1)} %constant.117.clone.perm_ref, f32[28,8,128]{2,1,0:T(8,128)} %broadcast_in_dim.73.taps_ref, ...), custom_call_target="tpu_custom_call" | custom-call | flops 10066329600 | bytes 19660800 | tf_op jit(solution)/shard_map/transport/pallas_call | solution.py:416
  211.2 29.2 %all_to_all.20.coef_ref = bf16[8,5,40,256]{3,2,1,0:T(8,128)(2,1)} all-to-all(bf16[8,5,40,256]{3,2,1,0:T(8,128)(2,1)} %bitcast.78), channel_id=1, replica_groups=mesh['band'=4,'wave'=8] {'wave'}, dimensions={0} | all-to-all | bytes 1638400 | tf_op jit(solution)/shard_map/all_to_all | solution.py:576
  240.3 3.5 %all-to-all-start.3 = ((bf16[8,5,40,256]{3,2,1,0:T(8,128)(2,1)}), bf16[8,5,40,256]{3,2,1,0:T(8,128)(2,1)S(1)}, u32[]{:S(2)}, u32[]{:S(2)}) async-start(bf16[8,5,40,256]{3,2,1,0:T(8,128)(2,1)} %bitcast.22), calls=%async_computation.3 | async-start | bytes 1638400 | tf_op jit(solution)/shard_map/all_to_all | solution.py:576
  243.9 14.7 %legendre_backward.2 = bf16[320,1408]{1,0:T(8,128)(2,1)} custom-call(s32[80]{0:T(128)} %dynamic_slice.49.pair_ref, bf16[256,256]{1,0:T(8,128)(2,1)} %constant.117.clone.perm_ref, bf16[8,5,40,256]{3,2,1,0:T(8,128)(2,1)} %all_to_all.20.coef_ref, bf16[80,320,1408]{2,1,0:T(8,128)(2,1)} %leg_ref.7), custom_call_target="tpu_custom_call" | custom-call | flops 1153433600 | bytes 36044800 | tf_op jit(solution)/shard_map/legendre_backward/pallas_call | solution.py:135
  258.6 1.7 slice_bitcast_fusion.7
  260.6 5.1 %collective-permute-start.5 = (bf16[40,8,352]{2,1,0:T(8,128)(2,1)S(1)}, bf16[40,8,352]{2,1,0:T(8,128)(2,1)S(1)}, u32[]{:S(2)}, u32[]{:S(2)}) collective-permute-start(bf16[40,8,352]{2,1,0:T(8,128)(2,1)S(1)} %get-tuple-element.36), channel_id=1, source_target_pairs={{0,8},{8,0},{16,24},{24,16},{1,9},{9,1},{17,25},{25,17},{2,10},{10... | collective-permute-start | bytes 675848 | tf_op jit(solution)/shard_map/ppermute | solution.py:467
  265.7 1.9 collective-permute-start.6
  267.6 1.4 collective-permute-start.7
  269.0 0.9 copy-done
  269.9 14.7 %legendre_backward.3 = bf16[320,1408]{1,0:T(8,128)(2,1)} custom-call(s32[80]{0:T(128)} %dynamic_slice.49.pair_ref, bf16[256,256]{1,0:T(8,128)(2,1)} %constant.117.clone.perm_ref, bf16[8,5,40,256]{3,2,1,0:T(8,128)(2,1)} %copy-done, bf16[80,320,1408]{2,1,0:T(8,128)(2,1)} %leg_ref.7), custom_call_target="tpu_custom_call" | custom-call | flops 1153433600 | bytes 36044800 | tf_op jit(solution)/shard_map/legendre_backward/pallas_call | solution.py:135
  284.6 1.7 slice_bitcast_fusion.3
  286.6 2.5 collective-permute-start.10
  289.1 2.3 collective-permute-start.8
  291.6 4.8 %collective-permute-done.10 = bf16[40,8,352]{2,1,0:T(8,128)(2,1)S(1)} collective-permute-done((bf16[40,8,352]{2,1,0:T(8,128)(2,1)S(1)}, bf16[40,8,352]{2,1,0:T(8,128)(2,1)S(1)}, u32[]{:S(2)}, u32[]{:S(2)}) %collective-permute-start.10) | collective-permute-done | bytes 225312 | tf_op jit(solution)/shard_map/ppermute | solution.py:467
  296.4 5.8 %collective-permute-done.8 = bf16[40,8,352]{2,1,0:T(8,128)(2,1)S(1)} collective-permute-done((bf16[40,8,352]{2,1,0:T(8,128)(2,1)S(1)}, bf16[40,8,352]{2,1,0:T(8,128)(2,1)S(1)}, u32[]{:S(2)}, u32[]{:S(2)}) %collective-permute-start.8) | collective-permute-done | bytes 225312 | tf_op jit(solution)/shard_map/ppermute | solution.py:467
  302.4 0.9 pad_maximum_fusion.3
  (128 shorter events, 9.9 us)
Async XLA Ops:
  0.6 42.9 %collective-permute-start = (bf16[80,8,352]{2,1,0:T(8,128)(2,1)}, bf16[80,8,352]{2,1,0:T(8,128)(2,1)S(1)}, u32[]{:S(2)}, u32[]{:S(2)}) collective-permute-start(bf16[80,8,352]{2,1,0:T(8,128)(2,1)} %bitcast.79), channel_id=1, source_target_pairs={{0,8},{8,0},{16,24},{24,16},{1,9},{9,1},{17,25},{25,17},{2,10},{10... | collective-permute-start | bytes 1351688 | tf_op jit(solution)/shard_map/ppermute | solution.py:467
  3.6 39.9 %collective-permute-start.1 = (bf16[80,8,352]{2,1,0:T(8,128)(2,1)}, bf16[80,8,352]{2,1,0:T(8,128)(2,1)S(1)}, u32[]{:S(2)}, u32[]{:S(2)}) collective-permute-start(bf16[80,8,352]{2,1,0:T(8,128)(2,1)} %bitcast.80), channel_id=1, source_target_pairs={{0,16},{8,24},{16,0},{24,8},{1,17},{9,25},{17,1},{25,9},{2,18},{10... | collective-permute-start | bytes 1351688 | tf_op jit(solution)/shard_map/ppermute | solution.py:467
  5.2 38.4 %collective-permute-start.2 = (bf16[80,8,352]{2,1,0:T(8,128)(2,1)}, bf16[80,8,352]{2,1,0:T(8,128)(2,1)S(1)}, u32[]{:S(2)}, u32[]{:S(2)}) collective-permute-start(bf16[80,8,352]{2,1,0:T(8,128)(2,1)} %bitcast.81), channel_id=1, source_target_pairs={{0,24},{8,16},{16,8},{24,0},{1,25},{9,17},{17,9},{25,1},{2,26},{10... | collective-permute-start | bytes 1351688 | tf_op jit(solution)/shard_map/ppermute | solution.py:467
  29.4 14.2 %copy-start.3 = (bf16[80,352,8]{1,2,0:T(8,128)(2,1)S(1)}, bf16[80,352,8]{1,2,0:T(8,128)(2,1)}, u32[]{:S(2)}) copy-start(bf16[80,352,8]{1,2,0:T(8,128)(2,1)} %param.8) | copy-start | bytes 1351684
  65.5 27.0 %all-to-all-start = ((bf16[8,5,40,256]{3,2,1,0:T(8,128)(2,1)}), bf16[8,5,40,256]{3,2,1,0:T(8,128)(2,1)S(1)}, u32[]{:S(2)}, u32[]{:S(2)}) async-start(bf16[8,5,40,256]{3,2,1,0:T(8,128)(2,1)} %legendre_forward.3), calls=%async_computation | async-start | bytes 1638400 | tf_op jit(solution)/shard_map/all_to_all | solution.py:534
  92.5 29.4 %copy-start.1 = (bf16[8,5,40,256]{3,2,1,0:T(8,128)(2,1)}, bf16[8,5,40,256]{3,2,1,0:T(8,128)(2,1)S(1)}, u32[]{:S(2)}) copy-start(bf16[8,5,40,256]{3,2,1,0:T(8,128)(2,1)S(1)} %all-to-all-done) | copy-start | bytes 2457604
  92.5 25.2 %all-to-all-start.1 = ((bf16[8,5,40,256]{3,2,1,0:T(8,128)(2,1)}), bf16[8,5,40,256]{3,2,1,0:T(8,128)(2,1)S(1)}, u32[]{:S(2)}, u32[]{:S(2)}) async-start(bf16[8,5,40,256]{3,2,1,0:T(8,128)(2,1)} %legendre_forward.2), calls=%async_computation.1 | async-start | bytes 1638400 | tf_op jit(solution)/shard_map/all_to_all | solution.py:534
  117.6 12.0 %copy-start.2 = (bf16[8,5,40,256]{3,2,1,0:T(8,128)(2,1)}, bf16[8,5,40,256]{3,2,1,0:T(8,128)(2,1)S(1)}, u32[]{:S(2)}) copy-start(bf16[8,5,40,256]{3,2,1,0:T(8,128)(2,1)S(1)} %all-to-all-done.1) | copy-start | bytes 2457604
  118.3 7.0 %collective-permute-start.4 = (bf16[80,3,256]{2,1,0:T(4,128)(2,1)S(1)}, bf16[80,3,256]{2,1,0:T(4,128)(2,1)S(1)}, u32[]{:S(2)}, u32[]{:S(2)}) collective-permute-start(bf16[80,3,256]{2,1,0:T(4,128)(2,1)S(1)} %pad_maximum_fusion.4), channel_id=1, source_target_pairs={{1,0},{2,1},{3,2},{4,3},{5,4},{6,5},{7,6},{8,7},{9,8},{10,9},{11,1... | collective-permute-start | bytes 368648 | tf_op jit(solution)/shard_map/ppermute | solution.py:542
  122.0 4.0 %collective-permute-start.3 = (bf16[80,3,256]{2,1,0:T(4,128)(2,1)S(1)}, bf16[80,3,256]{2,1,0:T(4,128)(2,1)S(1)}, u32[]{:S(2)}, u32[]{:S(2)}) collective-permute-start(bf16[80,3,256]{2,1,0:T(4,128)(2,1)S(1)} %pad_maximum_fusion.5), channel_id=1, source_target_pairs={{0,1},{1,2},{2,3},{3,4},{4,5},{5,6},{6,7},{7,8},{8,9},{9,10},{10,1... | collective-permute-start | bytes 368648 | tf_op jit(solution)/shard_map/ppermute | solution.py:541
  240.3 28.7 %all-to-all-start.3 = ((bf16[8,5,40,256]{3,2,1,0:T(8,128)(2,1)}), bf16[8,5,40,256]{3,2,1,0:T(8,128)(2,1)S(1)}, u32[]{:S(2)}, u32[]{:S(2)}) async-start(bf16[8,5,40,256]{3,2,1,0:T(8,128)(2,1)} %bitcast.22), calls=%async_computation.3 | async-start | bytes 1638400 | tf_op jit(solution)/shard_map/all_to_all | solution.py:576
  260.6 30.9 %collective-permute-start.5 = (bf16[40,8,352]{2,1,0:T(8,128)(2,1)S(1)}, bf16[40,8,352]{2,1,0:T(8,128)(2,1)S(1)}, u32[]{:S(2)}, u32[]{:S(2)}) collective-permute-start(bf16[40,8,352]{2,1,0:T(8,128)(2,1)S(1)} %get-tuple-element.36), channel_id=1, source_target_pairs={{0,8},{8,0},{16,24},{24,16},{1,9},{9,1},{17,25},{25,17},{2,10},{10... | collective-permute-start | bytes 675848 | tf_op jit(solution)/shard_map/ppermute | solution.py:467
  265.7 25.8 %collective-permute-start.6 = (bf16[40,8,352]{2,1,0:T(8,128)(2,1)S(1)}, bf16[40,8,352]{2,1,0:T(8,128)(2,1)S(1)}, u32[]{:S(2)}, u32[]{:S(2)}) collective-permute-start(bf16[40,8,352]{2,1,0:T(8,128)(2,1)S(1)} %get-tuple-element.38), channel_id=1, source_target_pairs={{0,16},{8,24},{16,0},{24,8},{1,17},{9,25},{17,1},{25,9},{2,18},{10... | collective-permute-start | bytes 675848 | tf_op jit(solution)/shard_map/ppermute | solution.py:467
  267.6 23.9 %collective-permute-start.7 = (bf16[40,8,352]{2,1,0:T(8,128)(2,1)S(1)}, bf16[40,8,352]{2,1,0:T(8,128)(2,1)S(1)}, u32[]{:S(2)}, u32[]{:S(2)}) collective-permute-start(bf16[40,8,352]{2,1,0:T(8,128)(2,1)S(1)} %get-tuple-element.37), channel_id=1, source_target_pairs={{0,24},{8,16},{16,8},{24,0},{1,25},{9,17},{17,9},{25,1},{2,26},{10... | collective-permute-start | bytes 675848 | tf_op jit(solution)/shard_map/ppermute | solution.py:467
  269.0 0.9 copy-start
  286.6 9.8 %collective-permute-start.10 = (bf16[40,8,352]{2,1,0:T(8,128)(2,1)S(1)}, bf16[40,8,352]{2,1,0:T(8,128)(2,1)S(1)}, u32[]{:S(2)}, u32[]{:S(2)}) collective-permute-start(bf16[40,8,352]{2,1,0:T(8,128)(2,1)S(1)} %get-tuple-element.40), channel_id=1, source_target_pairs={{0,24},{8,16},{16,8},{24,0},{1,25},{9,17},{17,9},{25,1},{2,26},{10... | collective-permute-start | bytes 675848 | tf_op jit(solution)/shard_map/ppermute | solution.py:467
  289.1 13.1 %collective-permute-start.8 = (bf16[40,8,352]{2,1,0:T(8,128)(2,1)S(1)}, bf16[40,8,352]{2,1,0:T(8,128)(2,1)S(1)}, u32[]{:S(2)}, u32[]{:S(2)}) collective-permute-start(bf16[40,8,352]{2,1,0:T(8,128)(2,1)S(1)} %get-tuple-element.39), channel_id=1, source_target_pairs={{0,8},{8,0},{16,24},{24,16},{1,9},{9,1},{17,25},{25,17},{2,10},{10... | collective-permute-start | bytes 675848 | tf_op jit(solution)/shard_map/ppermute | solution.py:467
  291.5 10.8 %collective-permute-start.9 = (bf16[40,8,352]{2,1,0:T(8,128)(2,1)S(1)}, bf16[40,8,352]{2,1,0:T(8,128)(2,1)S(1)}, u32[]{:S(2)}, u32[]{:S(2)}) collective-permute-start(bf16[40,8,352]{2,1,0:T(8,128)(2,1)S(1)} %get-tuple-element.41), channel_id=1, source_target_pairs={{0,16},{8,24},{16,0},{24,8},{1,17},{9,25},{17,1},{25,9},{2,18},{10... | collective-permute-start | bytes 675848 | tf_op jit(solution)/shard_map/ppermute | solution.py:467

commit v3 on v2

--- a/solution.py
+++ b/solution.py
@@ -21,8 +21,11 @@
 RUN = 5
 SUB = 8
 REACH = RUN + 2 * RIM
-BLOCKS = NLON // 128
 TILES = 10
+CHUNK = 512
+FINE = CHUNK // 128
+CHUNKS = NLON // CHUNK
+STEP = 4
 F32 = jnp.float32
 BF16 = jnp.bfloat16
 VMEM_LIMIT = 60 * 2**20
@@ -33,10 +36,18 @@
 
 
 def lane_order():
-    index = np.arange(WIDE).reshape(GROUP, 2, 2, FIELDS, 2).transpose(1, 2, 3, 0, 4).reshape(-1)
+    index = np.arange(WIDE).reshape(GROUP, 2, 2, FIELDS, 2).transpose(1, 2, 3, 4, 0).reshape(-1)
     matrix = np.zeros((WIDE, WIDE), np.float32)
     matrix[index, np.arange(WIDE)] = 1.0
     return jnp.asarray(matrix, BF16)
+
+
+def longitude_order():
+    position = np.arange(CHUNK)
+    longitude = FINE * (position % 128) + position // 128
+    matrix = np.zeros((CHUNK, CHUNK), np.float32)
+    matrix[longitude, position] = 1.0
+    return jnp.asarray(np.stack([matrix, matrix.T]), BF16)
 
 
 def row_masks(pair, rows):
@@ -53,28 +64,31 @@
 
 
 def forward_kernel(height, base, pair_ref, spec_ref, leg_ref, out_ref, acc_ref):
-    group = pl.program_id(0) + base
+    group, step = pl.program_id(0) + base, pl.program_id(1)
     rows = spec_ref.shape[2]
     sub = height // RUN
 
     pieces = []
-    for u in range(GROUP):
-        even, odd, sign = row_masks(pair_ref[group * GROUP + u], rows)
+    for u in range(STEP):
+        even, odd, sign = row_masks(pair_ref[group * GROUP + step * STEP + u], rows)
         spec = spec_ref[u].astype(F32)
         south = spec * sign
         parts = [spec * even, south * even, spec * odd, south * odd]
         masked = jnp.concatenate(parts, axis=0).astype(BF16)
         pieces.append(dot_nt(leg_ref[u], masked))
-        if u % 4 == 3:
-            acc_ref[u // 4] = jnp.concatenate(pieces[-4:], axis=1)
-    for dest in range(out_ref.shape[0]):
-        halves = []
-        for half in range(2):
-            pieces = [
-                acc_ref[half, pl.ds(dest * height + k, sub, stride=RUN), :] for k in range(RUN)
-            ]
-            halves.append(jnp.concatenate(pieces, axis=0))
-        out_ref[dest, 0] = jnp.concatenate(halves, axis=1).astype(BF16)
+    acc_ref[step] = jnp.concatenate(pieces, axis=1)
+
+    @pl.when(step == GROUP // STEP - 1)
+    def _():
+        for dest in range(out_ref.shape[0]):
+            halves = []
+            for half in range(2):
+                pieces = [
+                    acc_ref[half, pl.ds(dest * height + k, sub, stride=RUN), :]
+                    for k in range(RUN)
+                ]
+                halves.append(jnp.concatenate(pieces, axis=0))
+            out_ref[dest, 0] = jnp.concatenate(halves, axis=1).astype(BF16)
 
 
 def legendre_forward(pairs, spec, legendre, waves, part, parts):
@@ -85,13 +99,13 @@
     return pl.pallas_call(
         functools.partial(forward_kernel, height, base),
         out_shape=jax.ShapeDtypeStruct((waves, groups, height, WIDE), BF16),
-        grid=(groups,),
+        grid=(groups, GROUP // STEP),
         in_specs=[
             pl.BlockSpec(memory_space=pltpu.SMEM),
-            pl.BlockSpec((GROUP, COLS, rows), lambda g: (g + base, 0, 0)),
-            pl.BlockSpec((GROUP, lats, rows), lambda g: (g + base, 0, 0)),
+            pl.BlockSpec((STEP, COLS, rows), lambda g, t: (2 * (g + base) + t, 0, 0)),
+            pl.BlockSpec((STEP, lats, rows), lambda g, t: (2 * (g + base) + t, 0, 0)),
         ],
-        out_specs=pl.BlockSpec((waves, 1, height, WIDE), lambda g: (0, g, 0, 0)),
+        out_specs=pl.BlockSpec((waves, 1, height, WIDE), lambda g, t: (0, g, 0, 0)),
         scratch_shapes=[pltpu.VMEM((2, lats, 128), F32)],
         compiler_params=pltpu.CompilerParams(vmem_limit_bytes=VMEM_LIMIT),
         cost_estimate=pl.CostEstimate(
@@ -103,28 +117,34 @@
     )(pairs, spec, legendre)
 
 
-def backward_kernel(height, base, pair_ref, perm_ref, coef_ref, leg_ref, out_ref, rows_ref):
-    group = pl.program_id(0) + base
+def backward_kernel(
+    height, base, pair_ref, perm_ref, coef_ref, leg_ref, out_ref, rows_ref, turned_ref
+):
+    group, step = pl.program_id(0) + base, pl.program_id(1)
     rows = leg_ref.shape[2]
     sub = height // RUN
-    for source in range(coef_ref.shape[0]):
-        block = coef_ref[source, 0].astype(F32)
-        for k in range(RUN):
-            for half in range(2):
-                rows_ref[half, pl.ds(source * height + k, sub, stride=RUN), :] = block[
-                    k * sub : (k + 1) * sub, 128 * half : 128 * half + 128
-                ]
-    natural = jnp.concatenate([rows_ref[0], rows_ref[1]], axis=1).astype(BF16)
-    turned = dot_nt(perm_ref[...], natural).astype(BF16)
+
+    @pl.when(step == 0)
+    def _():
+        for source in range(coef_ref.shape[0]):
+            block = coef_ref[source, 0].astype(F32)
+            for k in range(RUN):
+                for half in range(2):
+                    rows_ref[half, pl.ds(source * height + k, sub, stride=RUN), :] = block[
+                        k * sub : (k + 1) * sub, 128 * half : 128 * half + 128
+                    ]
+        natural = jnp.concatenate([rows_ref[0], rows_ref[1]], axis=1).astype(BF16)
+        turned_ref[...] = dot_nt(perm_ref[...], natural).astype(BF16)
+
     sums = []
-    for u in range(GROUP):
-        even, odd, sign = row_masks(pair_ref[group * GROUP + u], rows)
-        raw = jnp.dot(turned[32 * u : 32 * u + 32], leg_ref[u], preferred_element_type=F32)
+    for u in range(STEP):
+        even, odd, sign = row_masks(pair_ref[group * GROUP + step * STEP + u], rows)
+        at = pl.ds(pl.multiple_of(step * (32 * STEP) + 32 * u, 32), 32)
+        raw = jnp.dot(turned_ref[at, :], leg_ref[u], preferred_element_type=F32)
         low = raw[0:8] + sign * raw[8:16]
         high = raw[16:24] + sign * raw[24:32]
         sums.append(low * even + high * odd)
-        if u % 2 == 1:
-            out_ref[8 * (u - 1) : 8 * (u + 1), :] = jnp.concatenate(sums[-2:], axis=0).astype(BF16)
+    out_ref[...] = jnp.concatenate(sums, axis=0).astype(BF16)
 
 
 def legendre_backward(pairs, perm, coefs, legendre, part):
@@ -135,15 +155,15 @@
     return pl.pallas_call(
         functools.partial(backward_kernel, height, base),
         out_shape=jax.ShapeDtypeStruct((slots * COLS, rows), BF16),
-        grid=(groups,),
+        grid=(groups, GROUP // STEP),
         in_specs=[
             pl.BlockSpec(memory_space=pltpu.SMEM),
-            pl.BlockSpec((WIDE, WIDE), lambda g: (0, 0)),
-            pl.BlockSpec((waves, 1, height, WIDE), lambda g: (0, g, 0, 0)),
-            pl.BlockSpec((GROUP, lats, rows), lambda g: (g + base, 0, 0)),
+            pl.BlockSpec((WIDE, WIDE), lambda g, t: (0, 0)),
+            pl.BlockSpec((waves, 1, height, WIDE), lambda g, t: (0, g, 0, 0)),
+            pl.BlockSpec((STEP, lats, rows), lambda g, t: (2 * (g + base) + t, 0, 0)),
         ],
-        out_specs=pl.BlockSpec((GROUP * COLS, rows), lambda g: (g, 0)),
-        scratch_shapes=[pltpu.VMEM((2, lats, 128), F32)],
+        out_specs=pl.BlockSpec((STEP * COLS, rows), lambda g, t: (2 * g + t, 0)),
+        scratch_shapes=[pltpu.VMEM((2, lats, 128), F32), pltpu.VMEM((WIDE, lats), BF16)],
         compiler_params=pltpu.CompilerParams(vmem_limit_bytes=VMEM_LIMIT),
         cost_estimate=pl.CostEstimate(
             flops=2 * slots * lats * rows * 32,
@@ -154,53 +174,65 @@
     )(pairs, perm, coefs, legendre)
 
 
-def table_kernel(cos_ref, sin_ref, step_cos_ref, step_sin_ref, out_ref):
+def table_kernel(cos_ref, sin_ref, step_ref, out_ref):
+    def rotate(c, s, step_c, step_s):
+        return c * step_c - s * step_s, s * step_c + c * step_s
+
     def body(i, carry):
-        rows = pl.ds(pl.multiple_of(i * 16, 16), 16)
-        c, s = cos_ref[rows, :], sin_ref[rows, :]
-        step_c, step_s = step_cos_ref[rows, :], step_sin_ref[rows, :]
-        for tile in range(HALF // 128):
-            out_ref[rows, 128 * tile : 128 * tile + 128] = c.astype(BF16)
-            if tile < HALF // 128 - 1:
-                c, s = c * step_c - s * step_s, s * step_c + c * step_s
+        rows = pl.ds(pl.multiple_of(i * GROUP, GROUP), GROUP)
+        to = pl.ds(pl.multiple_of(i * 2 * GROUP, 2 * GROUP), 2 * GROUP)
+        steps = step_ref[rows, :]
+        steps = [jnp.broadcast_to(steps[:, n : n + 1], (GROUP, 128)) for n in range(4)]
+        first = cos_ref[rows, :], sin_ref[rows, :]
+        for j in range(FINE):
+            c, s = first
+            for chunk in range(HALF // CHUNK):
+                at = chunk * CHUNK + j * 128
+                out_ref[to, at : at + 128] = jnp.concatenate([c, -s], axis=0).astype(BF16)
+                if chunk < HALF // CHUNK - 1:
+                    c, s = rotate(c, s, *steps[2:])
+            if j < FINE - 1:
+                first = rotate(*first, *steps[:2])
         return carry
 
-    lax.fori_loop(0, out_ref.shape[0] // 16, body, 0)
+    lax.fori_loop(0, cos_ref.shape[0] // GROUP, body, 0)
 
 
 def angle_tables(slot_pair):
     flipped = M - 1 - slot_pair
     odd = slot_pair % 2 == 1
-    waves = jnp.stack([jnp.where(odd, flipped, slot_pair), jnp.where(odd, slot_pair, flipped)])
+    waves = jnp.concatenate([jnp.where(odd, flipped, slot_pair), jnp.where(odd, slot_pair, flipped)])
     factor = jnp.where(waves == 0, 1.0, 2.0).astype(F32)
-    waves2 = jnp.broadcast_to(waves[..., None], waves.shape + (2,)).reshape(-1)
-    factor2 = jnp.broadcast_to(factor[..., None], factor.shape + (2,)).reshape(-1)
-    part = jnp.arange(waves2.shape[0], dtype=jnp.int32) % 2
-    column = jnp.arange(128, dtype=jnp.int32)
     unit = 2.0 * math.pi / NLON
-    turn = (waves2[:, None] * column[None, :] + (NLON // 4) * part[:, None]) % NLON
-    angle = turn.astype(F32) * unit
-    first_cos = factor2[:, None] * jnp.cos(angle)
-    first_sin = factor2[:, None] * jnp.sin(angle)
-    step = ((waves2 * 128) % NLON).astype(F32) * unit
-    shape = (waves2.shape[0], 128)
-    step_cos = jnp.broadcast_to(jnp.cos(step)[:, None], shape)
-    step_sin = jnp.broadcast_to(jnp.sin(step)[:, None], shape)
-    spec = pl.BlockSpec((256, 128), lambda i: (i, 0))
+
+    def angle(columns):
+        columns = jnp.asarray(columns, jnp.int32)
+        return (waves[:, None] * columns[None, :] % NLON).astype(F32) * unit
+
+    lanes = angle(FINE * np.arange(128))
+    first_cos = factor[:, None] * jnp.cos(lanes)
+    first_sin = factor[:, None] * jnp.sin(lanes)
+    moves = angle([1, 1, CHUNK, CHUNK])
+    steps = jnp.where(jnp.arange(4) % 2 == 0, jnp.cos(moves), jnp.sin(moves))
+    count = waves.shape[0]
     table = pl.pallas_call(
         table_kernel,
-        out_shape=jax.ShapeDtypeStruct((shape[0], HALF), BF16),
-        grid=(shape[0] // 256,),
-        in_specs=[spec] * 4,
+        out_shape=jax.ShapeDtypeStruct((2 * count, HALF), BF16),
+        grid=(count // 128,),
+        in_specs=[
+            pl.BlockSpec((128, 128), lambda i: (i, 0)),
+            pl.BlockSpec((128, 128), lambda i: (i, 0)),
+            pl.BlockSpec((128, 4), lambda i: (i, 0)),
+        ],
         out_specs=pl.BlockSpec((256, HALF), lambda i: (i, 0)),
         cost_estimate=pl.CostEstimate(
-            flops=6 * shape[0] * HALF, bytes_accessed=2 * shape[0] * HALF, transcendentals=0
+            flops=6 * count * HALF, bytes_accessed=4 * count * HALF, transcendentals=0
         ),
         name="angle_tables",
-    )(first_cos, first_sin, step_cos, step_sin)
-    scale = 1.0 / (factor * math.sqrt(NLON))
-    scale2 = jnp.broadcast_to(scale[:, None, :, None], (2, 8) + (scale.shape[1], 2))
-    return table.reshape(2, shape[0] // 2, HALF), scale2.reshape(2, 8, -1)
+    )(first_cos, first_sin, steps)
+    scale = (1.0 / (factor * math.sqrt(NLON))).reshape(2, 1, -1, 1, GROUP)
+    scale = jnp.broadcast_to(scale, (2, 8, count // 2 // GROUP, 2, GROUP))
+    return table.reshape(2, count, HALF), scale.reshape(2, 8, count)
 
 
 def swap_blocks(tiles, lane):
@@ -217,13 +249,13 @@
 
 
 def middle_kernel(
-    sub, parts, edge_ref, halo_ref, perm_ref, taps_ref, scale_ref, weight_ref,
+    sub, parts, edge_ref, halo_ref, perm_ref, order_ref, taps_ref, scale_ref, weight_ref,
     table_hbm, depart_hbm, pick_hbm, *refs,
 ):
     recv_refs, arrival_ref, coef_refs = refs[:parts], refs[parts], refs[parts + 1 : 2 * parts + 1]
     (
-    table_ref, depart_ref, pick_ref, left_ref, plus_ref, minus_ref, grid_ref, shift_ref,
-    stage_ref, code_ref, moved_ref, pair_ref, sums_ref, sems,
+        table_ref, depart_ref, pick_ref, left_ref, plus_ref, minus_ref, grid_ref, near_ref,
+        stage_ref, code_ref, moved_ref, pair_ref, sums_ref, sems,
     ) = refs[2 * parts + 1 :]
     per_part = TILES // parts
     copies = [
@@ -277,7 +309,7 @@
         minus_ref[...] = even - odd
         place = lax.broadcasted_iota(jnp.int32, (8, 256), 0)
         for side, ref in enumerate((plus_ref, minus_ref)):
-            to = pl.ds(pl.multiple_of(128 + side * HALF + tile * 256, 128), 256)
+            to = pl.ds(pl.multiple_of(side * HALF + tile * 256, 256), 256)
             for f in range(FIELDS):
                 for k in range(RUN):
                     at = (f * RUN + k) * 16
@@ -302,62 +334,95 @@
         return carry
 
     lax.fori_loop(0, HALF // 256, to_grid, 0)
-    grid_ref[:, :, 0:128] = grid_ref[:, :, NLON : NLON + 128]
-    grid_ref[:, :, NLON + 128 : NLON + 256] = grid_ref[:, :, 128:256]
     copies[1].wait()
     copies[2].wait()
 
-    def interpolate(tile, carry):
-        lanes = pl.ds(pl.multiple_of(tile * 128, 128), 128)
-        window = pl.ds(pl.multiple_of(tile * 128, 128), 384)
-        for row in range(FIELDS * REACH):
-            wide = grid_ref[row, :, window]
-            for c in range(-RIM, RIM + 1):
-                shift_ref[c + RIM, row] = wide[:, 128 + c : 256 + c]
-        for h in range(2):
-            code_ref[h] = pick_ref[h, :, lanes] * 16 + depart_ref[h, :, lanes]
-        for k in range(RUN):
-            index, column = [], []
-            for h in range(2):
-                code = code_ref[h, pl.ds(k, SUB, stride=RUN), :]
-                index.append(code >> 2)
-                column.append(code & 3)
-            column = jnp.concatenate(column, axis=0).astype(F32).astype(BF16)
-            hits = [column == jnp.asarray(d, BF16) for d in range(4)]
-            totals = [jnp.zeros((16, 128), F32) for _ in range(FIELDS)]
-            for r in range(7):
-                weights = []
-                for b in range(4):
-                    entry = taps_ref[r * 4 + b]
-                    found = [jnp.take_along_axis(entry, index[h], axis=1) for h in range(2)]
-                    weights.append(jnp.concatenate(found, axis=0).astype(BF16))
-                factors = []
-                for c in range(-RIM, RIM + 1):
-                    factor = jnp.zeros((16, 128), BF16)
-                    for d in range(4):
-                        b = c - (d - 2) + 1
-                        if 0 <= b < 4:
-                            factor = jnp.where(hits[d], weights[b], factor)
-                    factors.append(factor)
+    def interpolate(chunk, carry):
+        lanes = pl.ds(pl.multiple_of(chunk * CHUNK, CHUNK), CHUNK)
+        lane = lax.broadcasted_iota(jnp.int32, (16, 128), 1)
+        previous = jnp.where(chunk == 0, CHUNKS - 1, chunk - 1)
+        following = jnp.where(chunk == CHUNKS - 1, 0, chunk + 1)
+
+        def neighbours(row, carry):
+            for j in range(FINE):
+                here = grid_ref[row, :, pl.ds(pl.multiple_of(chunk * CHUNK + j * 128, 128), 128)]
+                near_ref[row, :, (RIM + j) * 128 : (RIM + j + 1) * 128] = here
+                here = here.astype(F32)
+                if j >= FINE - RIM:
+                    at = pl.ds(pl.multiple_of(previous * CHUNK + j * 128, 128), 128)
+                    there = grid_ref[row, :, at].astype(F32)
+                    mixed = pltpu.roll(jnp.where(lane == 127, there, here), 1, 1)
+                    slot = j - (FINE - RIM)
+                    near_ref[row, :, slot * 128 : slot * 128 + 128] = mixed.astype(BF16)
+                if j < RIM:
+                    at = pl.ds(pl.multiple_of(following * CHUNK + j * 128, 128), 128)
+                    there = grid_ref[row, :, at].astype(F32)
+                    mixed = pltpu.roll(jnp.where(lane == 0, there, here), 127, 1)
+                    slot = RIM + FINE + j
+                    near_ref[row, :, slot * 128 : slot * 128 + 128] = mixed.astype(BF16)
+            return carry
+
+        lax.fori_loop(0, FIELDS * REACH, neighbours, 0, unroll=4)
+        code = pick_ref[:, :, lanes] * 16 + depart_ref[:, :, lanes]
+        code = code.reshape(2 * RUN * SUB, CHUNK).astype(F32).astype(BF16)
+        code = jnp.dot(code, order_ref[0], preferred_element_type=F32).astype(jnp.int32)
+        for j in range(FINE):
+            code_ref[j] = code[:, 128 * j : 128 * j + 128]
+
+        def points(j, carry):
+            at_lanes = pl.ds(pl.multiple_of(chunk * CHUNK + j * 128, 128), 128)
+            for k in range(RUN):
+                index, column = [], []
+                for h in range(2):
+                    code = code_ref[j, pl.ds(h * RUN * SUB + k, SUB, stride=RUN), :]
+                    index.append(code >> 2)
+                    column.append(code & 3)
+                column = jnp.concatenate(column, axis=0).astype(F32).astype(BF16)
+                hits = [column == jnp.asarray(d, BF16) for d in range(4)]
+                totals = [jnp.zeros((16, 128), F32) for _ in range(FIELDS)]
+                for r in range(7):
+                    weights = []
+                    for b in range(4):
+                        entry = taps_ref[r * 4 + b]
+                        found = [jnp.take_along_axis(entry, index[h], axis=1) for h in range(2)]
+                        weights.append(jnp.concatenate(found, axis=0).astype(BF16))
+                    factors = []
+                    for c in range(-RIM, RIM + 1):
+                        factor = jnp.zeros((16, 128), BF16)
+                        for d in range(4):
+                            b = c - (d - 2) + 1
+                            if 0 <= b < 4:
+                                factor = jnp.where(hits[d], weights[b], factor)
+                        factors.append(factor)
+                    for f in range(FIELDS):
+                        row = f * REACH + k + r
+                        part = None
+                        for c in range(7):
+                            near = near_ref[row, :, pl.ds(pl.multiple_of((j + c) * 128, 128), 128)]
+                            part = factors[c] * near if part is None else part + factors[c] * near
+                        totals[f] = totals[f] + part.astype(F32)
                 for f in range(FIELDS):
-                    row = f * REACH + k + r
-                    part = factors[0] * shift_ref[0, row]
-                    for c in range(1, 7):
-                        part = part + factors[c] * shift_ref[c, row]
-                    totals[f] = totals[f] + part.astype(F32)
+                    at = (f * RUN + k) * 16
+                    moved_ref[at : at + 16, at_lanes] = totals[f].astype(BF16)
+            return carry
+
+        lax.fori_loop(0, FINE, points, 0)
+        natural = jnp.dot(moved_ref[:, lanes], order_ref[1], preferred_element_type=F32)
+        for j in range(FINE):
             for f in range(FIELDS):
-                at = (f * RUN + k) * 16
-                moved_ref[at : at + 16, lanes] = totals[f].astype(BF16)
-                for h in range(2):
-                    stage_ref[f * 2 + h, pl.ds(k, SUB, stride=RUN), :] = totals[f][
-                        8 * h : 8 * h + 8
-                    ]
+                for k in range(RUN):
+                    for h in range(2):
+                        at = (f * RUN + k) * 16 + 8 * h
+                        stage_ref[j, f * 2 + h, pl.ds(k, SUB, stride=RUN), :] = natural[
+                            at : at + 8, 128 * j : 128 * j + 128
+                        ]
         for f in range(FIELDS):
             for h in range(2):
-                arrival_ref[f, h, :, lanes] = stage_ref[f * 2 + h].astype(BF16)
+                rows = [stage_ref[j, f * 2 + h] for j in range(FINE)]
+                arrival_ref[f, h, :, lanes] = jnp.concatenate(rows, axis=1).astype(BF16)
         return carry
 
-    lax.fori_loop(0, BLOCKS, interpolate, 0)
+    lax.fori_loop(0, CHUNKS, interpolate, 0)
 
     def fold(tile, carry):
         lanes = pl.ds(pl.multiple_of(tile * 128, 128), 128)
@@ -404,7 +469,7 @@
         lax.fori_loop(0, per_part, functools.partial(scatter_rows, part), 0)
 
 
-def transport(sub, edge, recv, halo, perm, taps, scale, weight, table, depart, pick):
+def transport(sub, edge, recv, halo, perm, order, taps, scale, weight, table, depart, pick):
     parts = len(recv)
     rows, width = recv[0].shape
     lats = RUN * SUB
@@ -419,7 +484,7 @@
             jax.ShapeDtypeStruct((FIELDS, 2, lats, NLON), BF16),
             *[jax.ShapeDtypeStruct((rows, width), BF16)] * parts,
         ),
-        in_specs=[pl.BlockSpec(memory_space=pltpu.SMEM)] + [vmem] * 5 + [anywhere] * 3 + [vmem] * parts,
+        in_specs=[pl.BlockSpec(memory_space=pltpu.SMEM)] + [vmem] * 6 + [anywhere] * 3 + [vmem] * parts,
         out_specs=(vmem,) * (parts + 1),
         scratch_shapes=[
             pltpu.VMEM((2, slots2, HALF), BF16),
@@ -428,10 +493,10 @@
             pltpu.VMEM((2, left, slots2), BF16),
             pltpu.VMEM((left, 256), F32),
             pltpu.VMEM((left, 256), F32),
-            pltpu.VMEM((FIELDS * REACH, 16, NLON + 256), BF16),
-            pltpu.VMEM((7, FIELDS * REACH, 16, 128), BF16),
-            pltpu.VMEM((FIELDS * 2, lats, 128), F32),
-            pltpu.VMEM((2, lats, 128), jnp.int32),
+            pltpu.VMEM((FIELDS * REACH, 16, NLON), BF16),
+            pltpu.VMEM((FIELDS * REACH, 16, CHUNK + 2 * RIM * 128), BF16),
+            pltpu.VMEM((FINE, FIELDS * 2, lats, 128), F32),
+            pltpu.VMEM((FINE, 2 * lats, 128), jnp.int32),
             pltpu.VMEM((own, NLON), BF16),
             pltpu.VMEM((2, own, HALF), BF16),
             pltpu.VMEM((2, TILES, own, 128), F32),
@@ -444,21 +509,19 @@
             transcendentals=0,
         ),
         name="transport",
-    )(edge, halo, perm, taps, scale, weight, table, depart, pick, *recv)
+    )(edge, halo, perm, order, taps, scale, weight, table, depart, pick, *recv)
 
 
 def tap_tables(stencil_weight):
-    zero = jnp.zeros((NSTEN,), F32)
-    rows = []
-    for r in range(-3, 4):
-        for b in range(4):
-            picks = []
-            for dy in range(-2, 2):
-                a = r - dy + 1
-                picks.append(stencil_weight[:, 4 * a + b] if 0 <= a < 4 else zero)
-            rows.append(jnp.stack(picks, axis=1).reshape(-1))
-    table = jnp.stack(rows)
-    table = jnp.concatenate([table, jnp.zeros_like(table)], axis=1)
+    choose = np.zeros((16, 7, 4, 4), np.float32)
+    for r in range(7):
+        for d in range(4):
+            a = (r - 3) - (d - 2) + 1
+            if 0 <= a < 4:
+                for b in range(4):
+                    choose[4 * a + b, r, b, d] = 1.0
+    table = jnp.einsum("tw,wnd->ntd", stencil_weight, choose.reshape(16, 28, 4), precision="highest")
+    table = jnp.pad(table.reshape(28, 4 * NSTEN), ((0, 0), (0, 128 - 4 * NSTEN)))
     return jnp.broadcast_to(table[:, None, :], (28, 8, 128))
 
 
@@ -558,6 +621,7 @@
         [r.reshape(-1, WIDE) for r in recv],
         halo,
         perm,
+        longitude_order(),
         taps,
         scale,
         weight,

time: 304 us -> 290 us (0.954)
  local copies, waits for them, and re-layouts: 31.2 us -> 19.5 us
  starting transfers between devices: 34.7 us -> 27.5 us
  blocking collectives: 29.2 us -> 34 us
    pallas_call x1, Pallas kernels: 81.5 us -> 68.2 us  [transport(): pl.pallas_call(functools.partial(middle_kernel, sub, parts), out_shape=(j...]
    ppermute x9, starting transfers between devices: 17.8 us -> 12.1 us  [exchange(): lax.ppermute(array, axis, [(i, i ^ distance) for i in range(devices)])]
    pallas_call x2, Pallas kernels: 29.4 us -> 34.4 us  [legendre_backward(): pl.pallas_call(functools.partial(backward_kernel, height, base), out_shap...]
    another operation x59 -> x0, local copies, waits for them, and re-layouts: 4.95 us -> none  [the longest x29 2.61 us: tap_tables(): table = jnp.stack(rows)]
    all_to_all x1, blocking collectives: 29.2 us -> 34 us  [per_device(): lax.all_to_all(leaving, 'wave', split_axis=0, concat_axis=0, tiled=True)]
    pallas_call x1, Pallas kernels: 13.6 us -> 18.4 us  [angle_tables(): pl.pallas_call(table_kernel, out_shape=jax.ShapeDtypeStruct((2 * count, H...]
    pallas_call x2, Pallas kernels: 33.4 us -> 38.1 us  [legendre_forward(): pl.pallas_call(functools.partial(forward_kernel, height, base), out_shape...]
    mul x2 -> x1, other arithmetic: 8.18 us -> 4.19 us  [angle_tables(): first_sin = factor[:, None] * jnp.sin(lanes)]
  transfers between devices with their start and end apart: 14 -> 14, of which waited for: 5 -> 6; matrix products, arithmetic and copies ran while one was open for 11% -> 7% of each run, Pallas kernels for 20% -> 25%
where the time goes in v3:
time: 290 us; the launch traced here: 289 us
  Pallas kernels  159 us (55%)
  waiting for transfers between devices  35.4 us (12%)
  blocking collectives  34 us (12%)
  starting transfers between devices  27.5 us (9%)
  local copies, waits for them, and re-layouts  19.5 us (7%)
  other arithmetic  12 us (4%)
    pallas_call x1, Pallas kernels, transport(): pl.pallas_call(functools.partial(middle_kernel, sub, parts), out_shape=(j...  68.2 us
    pallas_call x2, Pallas kernels, legendre_forward(): pl.pallas_call(functools.partial(forward_kernel, height, base), out_shape...  38.1 us
    pallas_call x2, Pallas kernels, legendre_backward(): pl.pallas_call(functools.partial(backward_kernel, height, base), out_shap...  34.4 us
    all_to_all x1, blocking collectives, per_device(): lax.all_to_all(leaving, 'wave', split_axis=0, concat_axis=0, tiled=True)  34 us
    all_to_all x2, waiting for transfers between devices, per_device(): lax.all_to_all(sent, 'wave', split_axis=0, concat_axis=0, tiled=True)  23 us
    pallas_call x1, Pallas kernels, angle_tables(): pl.pallas_call(table_kernel, out_shape=jax.ShapeDtypeStruct((2 * count, H...  18.4 us
    ppermute x9, starting transfers between devices, exchange(): lax.ppermute(array, axis, [(i, i ^ distance) for i in range(devices)])  12.1 us
    ppermute x9, waiting for transfers between devices, exchange(): lax.ppermute(array, axis, [(i, i ^ distance) for i in range(devices)])  10.9 us
  transfers between devices with their start and end apart: 14, of which 6 were waited for; matrix products, arithmetic and copies ran while one was open for 7% of the time, Pallas kernels for 25%

profile of v3, /device:TPU:0, one launch (start us, length us, event | category | flops | bytes accessed | tf_op | source)
XLA Modules:
  0.0 289.3 jit_solution(10411350670643590246)
XLA Ops:
  0.7 3.0 %collective-permute-start.1 = (bf16[80,8,352]{2,1,0:T(8,128)(2,1)}, bf16[80,8,352]{2,1,0:T(8,128)(2,1)S(1)}, u32[]{:S(2)}, u32[]{:S(2)}) collective-permute-start(bf16[80,8,352]{2,1,0:T(8,128)(2,1)} %bitcast.87), channel_id=1, source_target_pairs={{0,16},{8,24},{16,0},{24,8},{1,17},{9,25},{17,1},{25,9},{2,18},{10... | collective-permute-start | bytes 1351688 | tf_op jit(solution)/shard_map/ppermute | solution.py:530
  3.7 1.5 collective-permute-start
  5.2 0.8 reshape.146
  6.2 1.3 dynamic_slice.49.pair_ref
  7.5 0.8 dynamic_slice.48
  8.5 0.9 convolution_bitcast_fusion
  10.2 4.2 %sine_multiply_fusion = (f32[1280,128]{1,0:T(8,128)}, f32[1280,128]{1,0:T(8,128)}) fusion(s32[128]{0:T(128)S(1)} %iota_multiply_fusion, s32[1280]{0:T(1024)S(1)} %pad_add_fusion, f32[1280]{0:T(1024)S(1)} %compare_select_fusion), kind=kLoop, calls=%fused_computation.14 | loop fusion | flops 1802240 | bytes 1321472 | tf_op jit(solution)/shard_map/mul | solution.py:214
  14.4 3.8 %sine_select_fusion.step_ref = f32[1280,4]{1,0:T(8,128)} fusion(s32[1280]{0:T(1024)S(1)} %pad_add_fusion, s32[4]{0:T(128)S(1)} %copy-done.5, pred[4]{0:T(512)(128)(4,1)S(1)} %fusion.29), kind=kLoop, calls=%fused_computation.10 | loop fusion | flops 51200 | bytes 25620 | tf_op jit(solution)/shard_map/jit(_where)/select_n | solution.py:216
  18.2 18.4 %angle_tables.1 = bf16[2560,2560]{1,0:T(8,128)(2,1)} custom-call(f32[1280,128]{1,0:T(8,128)} %get-tuple-element.57.cos_ref, f32[1280,128]{1,0:T(8,128)} %get-tuple-element.56.sin_ref, f32[1280,4]{1,0:T(8,128)} %sine_select_fusion.step_ref), custom_call_target="tpu_custom_call" | custom-call | flops 19660800 | bytes 13107200 | tf_op jit(solution)/shard_map/angle_tables/pallas_call | solution.py:218
  36.5 0.7 add_convert_fusion.edge_ref
  37.9 2.5 concatenate.25.spec_ref
  40.4 0.6 broadcast_in_dim.57.scale_ref
  41.1 0.7 broadcast_in_dim.58.taps_ref
  41.7 0.8 broadcast_in_dim.61.weight_ref
  42.5 19.0 %legendre_forward.3 = bf16[8,5,40,256]{3,2,1,0:T(8,128)(2,1)} custom-call(s32[80]{0:T(128)} %dynamic_slice.49.pair_ref, bf16[80,8,1408]{2,1,0:T(8,128)(2,1)} %concatenate.25.spec_ref, bf16[80,320,1408]{2,1,0:T(8,128)(2,1)} %leg_ref.7), custom_call_target="tpu_custom_call" | custom-call | flops 1153433600 | bytes 36044800 | tf_op jit(solution)/shard_map/legendre_forward/pallas_call | solution.py:99
  61.5 5.3 %all-to-all-start = ((bf16[8,5,40,256]{3,2,1,0:T(8,128)(2,1)}), bf16[8,5,40,256]{3,2,1,0:T(8,128)(2,1)S(1)}, u32[]{:S(2)}, u32[]{:S(2)}) async-start(bf16[8,5,40,256]{3,2,1,0:T(8,128)(2,1)} %legendre_forward.3), calls=%async_computation | async-start | bytes 1638400 | tf_op jit(solution)/shard_map/all_to_all | solution.py:597
  66.8 19.1 %legendre_forward.2 = bf16[8,5,40,256]{3,2,1,0:T(8,128)(2,1)} custom-call(s32[80]{0:T(128)} %dynamic_slice.49.pair_ref, bf16[80,8,1408]{2,1,0:T(8,128)(2,1)} %concatenate.25.spec_ref, bf16[80,320,1408]{2,1,0:T(8,128)(2,1)} %leg_ref.7), custom_call_target="tpu_custom_call" | custom-call | flops 1153433600 | bytes 36044800 | tf_op jit(solution)/shard_map/legendre_forward/pallas_call | solution.py:99
  85.9 2.6 all-to-all-done
  88.5 3.5 %all-to-all-start.1 = ((bf16[8,5,40,256]{3,2,1,0:T(8,128)(2,1)}), bf16[8,5,40,256]{3,2,1,0:T(8,128)(2,1)S(1)}, u32[]{:S(2)}, u32[]{:S(2)}) async-start(bf16[8,5,40,256]{3,2,1,0:T(8,128)(2,1)} %legendre_forward.2), calls=%async_computation.1 | async-start | bytes 1638400 | tf_op jit(solution)/shard_map/all_to_all | solution.py:597
  92.0 1.2 slice.75
  93.2 20.4 %all-to-all-done.1 = bf16[8,5,40,256]{3,2,1,0:T(8,128)(2,1)S(1)} async-done(((bf16[8,5,40,256]{3,2,1,0:T(8,128)(2,1)}), bf16[8,5,40,256]{3,2,1,0:T(8,128)(2,1)S(1)}, u32[]{:S(2)}, u32[]{:S(2)}) %all-to-all-start.1) | async-done | bytes 819232 | tf_op jit(solution)/shard_map/all_to_all | solution.py:597
  113.6 1.1 slice.76
  114.9 1.6 collective-permute-start.3
  116.4 0.5 slice.72
  117.0 0.5 slice.73
  117.6 1.3 collective-permute-start.4
  118.9 0.5 broadcast_select_fusion.3
  119.4 1.5 collective-permute-done.4
  120.9 0.5 broadcast_select_fusion
  121.5 3.1 %stack.75 = bf16[80,8,256]{2,1,0:T(8,128)(2,1)} concatenate(bf16[80,1,256]{2,1,0:T(2,128)(2,1)S(1)} %get-tuple-element.53, bf16[80,1,256]{2,1,0:T(2,128)(2,1)S(1)} %get-tuple-element.52, bf16[80,1,256]{2,1,0:T(2,128)(2,1)S(1)} %get-tuple-element.51, bf16[80,1,256]{2,1,0:T(2,128)(2,1)S(1)} %get-tuple-element.50, bf16[80,1,256]{2,1,0:T(2,128)(2,1)S(1)} %get-tuple-element.49, ...), dimensions={1} | concatenate | bytes 655360 | tf_op jit(solution)/shard_map/stack | solution.py:609
  124.5 68.2 %transport.1 = (bf16[4,2,40,5120]{3,2,1,0:T(8,128)(2,1)}, bf16[1600,256]{1,0:T(8,128)(2,1)}, bf16[1600,256]{1,0:T(8,128)(2,1)}) custom-call(s32[2]{0:T(128)} %add_convert_fusion.edge_ref, bf16[640,256]{1,0:T(8,128)(2,1)} %bitcast.94, bf16[256,256]{1,0:T(8,128)(2,1)} %constant.124.clone.perm_ref, bf16[2,512,512]{2,1,0:T(8,128)(2,1)} %constant.128.clone.order_ref, ...), custom_call_target="tpu_custom_call" | custom-call | flops 10066329600 | bytes 19660800 | tf_op jit(solution)/shard_map/transport/pallas_call | solution.py:481
  192.7 34.0 %all_to_all.20.coef_ref = bf16[8,5,40,256]{3,2,1,0:T(8,128)(2,1)} all-to-all(bf16[8,5,40,256]{3,2,1,0:T(8,128)(2,1)} %bitcast.86), channel_id=1, replica_groups=mesh['band'=4,'wave'=8] {'wave'}, dimensions={0} | all-to-all | bytes 1638400 | tf_op jit(solution)/shard_map/all_to_all | solution.py:640
  226.7 3.7 %all-to-all-start.3 = ((bf16[8,5,40,256]{3,2,1,0:T(8,128)(2,1)}), bf16[8,5,40,256]{3,2,1,0:T(8,128)(2,1)S(1)}, u32[]{:S(2)}, u32[]{:S(2)}) async-start(bf16[8,5,40,256]{3,2,1,0:T(8,128)(2,1)} %bitcast.85), calls=%async_computation.3 | async-start | bytes 1638400 | tf_op jit(solution)/shard_map/all_to_all | solution.py:640
  230.4 17.2 %legendre_backward.2 = bf16[320,1408]{1,0:T(8,128)(2,1)} custom-call(s32[80]{0:T(128)} %dynamic_slice.49.pair_ref, bf16[256,256]{1,0:T(8,128)(2,1)} %constant.124.clone.perm_ref, bf16[8,5,40,256]{3,2,1,0:T(8,128)(2,1)} %all_to_all.20.coef_ref, bf16[80,320,1408]{2,1,0:T(8,128)(2,1)} %leg_ref.7), custom_call_target="tpu_custom_call" | custom-call | flops 1153433600 | bytes 36044800 | tf_op jit(solution)/shard_map/legendre_backward/pallas_call | solution.py:155
  247.6 1.7 slice_bitcast_fusion.7
  249.6 2.4 collective-permute-start.5
  252.1 0.6 collective-permute-start.7
  252.7 1.0 collective-permute-start.6
  253.6 0.9 copy-done.1
  254.5 17.2 %legendre_backward.3 = bf16[320,1408]{1,0:T(8,128)(2,1)} custom-call(s32[80]{0:T(128)} %dynamic_slice.49.pair_ref, bf16[256,256]{1,0:T(8,128)(2,1)} %constant.124.clone.perm_ref, bf16[8,5,40,256]{3,2,1,0:T(8,128)(2,1)} %copy-done.1, bf16[80,320,1408]{2,1,0:T(8,128)(2,1)} %leg_ref.7), custom_call_target="tpu_custom_call" | custom-call | flops 1153433600 | bytes 36044800 | tf_op jit(solution)/shard_map/legendre_backward/pallas_call | solution.py:155
  271.7 1.7 slice_bitcast_fusion.3
  273.7 2.0 collective-permute-start.8
  275.7 0.6 collective-permute-start.10
  276.3 1.0 collective-permute-start.9
  277.4 5.2 %collective-permute-done.8 = bf16[40,8,352]{2,1,0:T(8,128)(2,1)S(1)} collective-permute-done((bf16[40,8,352]{2,1,0:T(8,128)(2,1)S(1)}, bf16[40,8,352]{2,1,0:T(8,128)(2,1)S(1)}, u32[]{:S(2)}, u32[]{:S(2)}) %collective-permute-start.8) | collective-permute-done | bytes 225312 | tf_op jit(solution)/shard_map/ppermute | solution.py:530
  282.6 4.2 %collective-permute-done.10 = bf16[40,8,352]{2,1,0:T(8,128)(2,1)S(1)} collective-permute-done((bf16[40,8,352]{2,1,0:T(8,128)(2,1)S(1)}, bf16[40,8,352]{2,1,0:T(8,128)(2,1)S(1)}, u32[]{:S(2)}, u32[]{:S(2)}) %collective-permute-start.10) | collective-permute-done | bytes 225312 | tf_op jit(solution)/shard_map/ppermute | solution.py:530
  286.9 1.4 collective-permute-done.9
  288.4 0.9 pad_maximum_fusion.3
  (53 shorter events, 3.1 us)
Async XLA Ops:
  0.6 7.9 %copy-start = (f32[16,16]{1,0:T(8,128)S(1)}, f32[16,16]{1,0:T(8,128)}, u32[]{:S(2)}) copy-start(f32[16,16]{1,0:T(8,128)} %param.18) | copy-start | bytes 3076
  0.6 13.8 %copy-start.5 = (s32[4]{0:T(128)S(1)}, s32[4]{0:T(128)}, u32[]{:S(2)}) copy-start(s32[4]{0:T(128)} %constant.126.clone) | copy-start | bytes 52
  0.7 36.6 %collective-permute-start.1 = (bf16[80,8,352]{2,1,0:T(8,128)(2,1)}, bf16[80,8,352]{2,1,0:T(8,128)(2,1)S(1)}, u32[]{:S(2)}, u32[]{:S(2)}) collective-permute-start(bf16[80,8,352]{2,1,0:T(8,128)(2,1)} %bitcast.87), channel_id=1, source_target_pairs={{0,16},{8,24},{16,0},{24,8},{1,17},{9,25},{17,1},{25,9},{2,18},{10... | collective-permute-start | bytes 1351688 | tf_op jit(solution)/shard_map/ppermute | solution.py:530
  3.7 33.5 %collective-permute-start = (bf16[80,8,352]{2,1,0:T(8,128)(2,1)}, bf16[80,8,352]{2,1,0:T(8,128)(2,1)S(1)}, u32[]{:S(2)}, u32[]{:S(2)}) collective-permute-start(bf16[80,8,352]{2,1,0:T(8,128)(2,1)} %bitcast.88), channel_id=1, source_target_pairs={{0,8},{8,0},{16,24},{24,16},{1,9},{9,1},{17,25},{25,17},{2,10},{10... | collective-permute-start | bytes 1351688 | tf_op jit(solution)/shard_map/ppermute | solution.py:530
  5.2 32.0 %collective-permute-start.2 = (bf16[80,8,352]{2,1,0:T(8,128)(2,1)}, bf16[80,8,352]{2,1,0:T(8,128)(2,1)S(1)}, u32[]{:S(2)}, u32[]{:S(2)}) collective-permute-start(bf16[80,8,352]{2,1,0:T(8,128)(2,1)} %bitcast.89), channel_id=1, source_target_pairs={{0,24},{8,16},{16,8},{24,0},{1,25},{9,17},{17,9},{25,1},{2,26},{10... | collective-permute-start | bytes 1351688 | tf_op jit(solution)/shard_map/ppermute | solution.py:530
  18.2 19.1 %copy-start.4 = (bf16[80,352,8]{1,2,0:T(8,128)(2,1)S(1)}, bf16[80,352,8]{1,2,0:T(8,128)(2,1)}, u32[]{:S(2)}) copy-start(bf16[80,352,8]{1,2,0:T(8,128)(2,1)} %param.12) | copy-start | bytes 1351684
  61.5 27.0 %all-to-all-start = ((bf16[8,5,40,256]{3,2,1,0:T(8,128)(2,1)}), bf16[8,5,40,256]{3,2,1,0:T(8,128)(2,1)S(1)}, u32[]{:S(2)}, u32[]{:S(2)}) async-start(bf16[8,5,40,256]{3,2,1,0:T(8,128)(2,1)} %legendre_forward.3), calls=%async_computation | async-start | bytes 1638400 | tf_op jit(solution)/shard_map/all_to_all | solution.py:597
  88.5 32.9 %copy-start.2 = (bf16[8,5,40,256]{3,2,1,0:T(8,128)(2,1)}, bf16[8,5,40,256]{3,2,1,0:T(8,128)(2,1)S(1)}, u32[]{:S(2)}) copy-start(bf16[8,5,40,256]{3,2,1,0:T(8,128)(2,1)S(1)} %all-to-all-done) | copy-start | bytes 2457604
  88.5 25.2 %all-to-all-start.1 = ((bf16[8,5,40,256]{3,2,1,0:T(8,128)(2,1)}), bf16[8,5,40,256]{3,2,1,0:T(8,128)(2,1)S(1)}, u32[]{:S(2)}, u32[]{:S(2)}) async-start(bf16[8,5,40,256]{3,2,1,0:T(8,128)(2,1)} %legendre_forward.2), calls=%async_computation.1 | async-start | bytes 1638400 | tf_op jit(solution)/shard_map/all_to_all | solution.py:597
  113.6 10.9 %copy-start.3 = (bf16[8,5,40,256]{3,2,1,0:T(8,128)(2,1)}, bf16[8,5,40,256]{3,2,1,0:T(8,128)(2,1)S(1)}, u32[]{:S(2)}) copy-start(bf16[8,5,40,256]{3,2,1,0:T(8,128)(2,1)S(1)} %all-to-all-done.1) | copy-start | bytes 2457604
  114.9 4.0 %collective-permute-start.3 = (bf16[80,3,256]{2,1,0:T(4,128)(2,1)S(1)}, bf16[80,3,256]{2,1,0:T(4,128)(2,1)S(1)}, u32[]{:S(2)}, u32[]{:S(2)}) collective-permute-start(bf16[80,3,256]{2,1,0:T(4,128)(2,1)S(1)} %pad_maximum_fusion.5), channel_id=1, source_target_pairs={{0,1},{1,2},{2,3},{3,4},{4,5},{5,6},{6,7},{7,8},{8,9},{9,10},{10,1... | collective-permute-start | bytes 368648 | tf_op jit(solution)/shard_map/ppermute | solution.py:604
  117.6 3.3 %collective-permute-start.4 = (bf16[80,3,256]{2,1,0:T(4,128)(2,1)S(1)}, bf16[80,3,256]{2,1,0:T(4,128)(2,1)S(1)}, u32[]{:S(2)}, u32[]{:S(2)}) collective-permute-start(bf16[80,3,256]{2,1,0:T(4,128)(2,1)S(1)} %pad_maximum_fusion.4), channel_id=1, source_target_pairs={{1,0},{2,1},{3,2},{4,3},{5,4},{6,5},{7,6},{8,7},{9,8},{10,9},{11,1... | collective-permute-start | bytes 368648 | tf_op jit(solution)/shard_map/ppermute | solution.py:605
  226.7 26.9 %all-to-all-start.3 = ((bf16[8,5,40,256]{3,2,1,0:T(8,128)(2,1)}), bf16[8,5,40,256]{3,2,1,0:T(8,128)(2,1)S(1)}, u32[]{:S(2)}, u32[]{:S(2)}) async-start(bf16[8,5,40,256]{3,2,1,0:T(8,128)(2,1)} %bitcast.85), calls=%async_computation.3 | async-start | bytes 1638400 | tf_op jit(solution)/shard_map/all_to_all | solution.py:640
  249.6 26.7 %collective-permute-start.5 = (bf16[40,8,352]{2,1,0:T(8,128)(2,1)S(1)}, bf16[40,8,352]{2,1,0:T(8,128)(2,1)S(1)}, u32[]{:S(2)}, u32[]{:S(2)}) collective-permute-start(bf16[40,8,352]{2,1,0:T(8,128)(2,1)S(1)} %get-tuple-element.34), channel_id=1, source_target_pairs={{0,8},{8,0},{16,24},{24,16},{1,9},{9,1},{17,25},{25,17},{2,10},{10... | collective-permute-start | bytes 675848 | tf_op jit(solution)/shard_map/ppermute | solution.py:530
  252.1 25.2 %collective-permute-start.7 = (bf16[40,8,352]{2,1,0:T(8,128)(2,1)S(1)}, bf16[40,8,352]{2,1,0:T(8,128)(2,1)S(1)}, u32[]{:S(2)}, u32[]{:S(2)}) collective-permute-start(bf16[40,8,352]{2,1,0:T(8,128)(2,1)S(1)} %get-tuple-element.35), channel_id=1, source_target_pairs={{0,24},{8,16},{16,8},{24,0},{1,25},{9,17},{17,9},{25,1},{2,26},{10... | collective-permute-start | bytes 675848 | tf_op jit(solution)/shard_map/ppermute | solution.py:530
  252.7 24.6 %collective-permute-start.6 = (bf16[40,8,352]{2,1,0:T(8,128)(2,1)S(1)}, bf16[40,8,352]{2,1,0:T(8,128)(2,1)S(1)}, u32[]{:S(2)}, u32[]{:S(2)}) collective-permute-start(bf16[40,8,352]{2,1,0:T(8,128)(2,1)S(1)} %get-tuple-element.36), channel_id=1, source_target_pairs={{0,16},{8,24},{16,0},{24,8},{1,17},{9,25},{17,1},{25,9},{2,18},{10... | collective-permute-start | bytes 675848 | tf_op jit(solution)/shard_map/ppermute | solution.py:530
  253.6 0.9 copy-start.1
  273.7 8.9 %collective-permute-start.8 = (bf16[40,8,352]{2,1,0:T(8,128)(2,1)S(1)}, bf16[40,8,352]{2,1,0:T(8,128)(2,1)S(1)}, u32[]{:S(2)}, u32[]{:S(2)}) collective-permute-start(bf16[40,8,352]{2,1,0:T(8,128)(2,1)S(1)} %get-tuple-element.37), channel_id=1, source_target_pairs={{0,8},{8,0},{16,24},{24,16},{1,9},{9,1},{17,25},{25,17},{2,10},{10... | collective-permute-start | bytes 675848 | tf_op jit(solution)/shard_map/ppermute | solution.py:530
  275.7 11.2 %collective-permute-start.10 = (bf16[40,8,352]{2,1,0:T(8,128)(2,1)S(1)}, bf16[40,8,352]{2,1,0:T(8,128)(2,1)S(1)}, u32[]{:S(2)}, u32[]{:S(2)}) collective-permute-start(bf16[40,8,352]{2,1,0:T(8,128)(2,1)S(1)} %get-tuple-element.38), channel_id=1, source_target_pairs={{0,24},{8,16},{16,8},{24,0},{1,25},{9,17},{17,9},{25,1},{2,26},{10... | collective-permute-start | bytes 675848 | tf_op jit(solution)/shard_map/ppermute | solution.py:530
  276.3 11.9 %collective-permute-start.9 = (bf16[40,8,352]{2,1,0:T(8,128)(2,1)S(1)}, bf16[40,8,352]{2,1,0:T(8,128)(2,1)S(1)}, u32[]{:S(2)}, u32[]{:S(2)}) collective-permute-start(bf16[40,8,352]{2,1,0:T(8,128)(2,1)S(1)} %get-tuple-element.39), channel_id=1, source_target_pairs={{0,16},{8,24},{16,0},{24,8},{1,17},{9,25},{17,1},{25,9},{2,18},{10... | collective-permute-start | bytes 675848 | tf_op jit(solution)/shard_map/ppermute | solution.py:530

commit v4 on v3

--- a/solution.py
+++ b/solution.py
@@ -25,7 +25,8 @@
 CHUNK = 512
 FINE = CHUNK // 128
 CHUNKS = NLON // CHUNK
-STEP = 4
+STEP = 8
+REACH_TAPS = (2 * RIM + 1) ** 2
 F32 = jnp.float32
 BF16 = jnp.bfloat16
 VMEM_LIMIT = 60 * 2**20
@@ -47,7 +48,7 @@
     longitude = FINE * (position % 128) + position // 128
     matrix = np.zeros((CHUNK, CHUNK), np.float32)
     matrix[longitude, position] = 1.0
-    return jnp.asarray(np.stack([matrix, matrix.T]), BF16)
+    return jnp.asarray(matrix, BF16), jnp.asarray(matrix.T, BF16)
 
 
 def row_masks(pair, rows):
@@ -76,7 +77,8 @@
         parts = [spec * even, south * even, spec * odd, south * odd]
         masked = jnp.concatenate(parts, axis=0).astype(BF16)
         pieces.append(dot_nt(leg_ref[u], masked))
-    acc_ref[step] = jnp.concatenate(pieces, axis=1)
+    for half in range(STEP // 4):
+        acc_ref[step * (STEP // 4) + half] = jnp.concatenate(pieces[4 * half : 4 * half + 4], axis=1)
 
     @pl.when(step == GROUP // STEP - 1)
     def _():
@@ -102,8 +104,8 @@
         grid=(groups, GROUP // STEP),
         in_specs=[
             pl.BlockSpec(memory_space=pltpu.SMEM),
-            pl.BlockSpec((STEP, COLS, rows), lambda g, t: (2 * (g + base) + t, 0, 0)),
-            pl.BlockSpec((STEP, lats, rows), lambda g, t: (2 * (g + base) + t, 0, 0)),
+            pl.BlockSpec((STEP, COLS, rows), lambda g, t: (GROUP // STEP * (g + base) + t, 0, 0)),
+            pl.BlockSpec((STEP, lats, rows), lambda g, t: (GROUP // STEP * (g + base) + t, 0, 0)),
         ],
         out_specs=pl.BlockSpec((waves, 1, height, WIDE), lambda g, t: (0, g, 0, 0)),
         scratch_shapes=[pltpu.VMEM((2, lats, 128), F32)],
@@ -160,9 +162,9 @@
             pl.BlockSpec(memory_space=pltpu.SMEM),
             pl.BlockSpec((WIDE, WIDE), lambda g, t: (0, 0)),
             pl.BlockSpec((waves, 1, height, WIDE), lambda g, t: (0, g, 0, 0)),
-            pl.BlockSpec((STEP, lats, rows), lambda g, t: (2 * (g + base) + t, 0, 0)),
+            pl.BlockSpec((STEP, lats, rows), lambda g, t: (GROUP // STEP * (g + base) + t, 0, 0)),
         ],
-        out_specs=pl.BlockSpec((STEP * COLS, rows), lambda g, t: (2 * g + t, 0)),
+        out_specs=pl.BlockSpec((STEP * COLS, rows), lambda g, t: (GROUP // STEP * g + t, 0)),
         scratch_shapes=[pltpu.VMEM((2, lats, 128), F32), pltpu.VMEM((WIDE, lats), BF16)],
         compiler_params=pltpu.CompilerParams(vmem_limit_bytes=VMEM_LIMIT),
         cost_estimate=pl.CostEstimate(
@@ -175,27 +177,32 @@
 
 
 def table_kernel(cos_ref, sin_ref, step_ref, out_ref):
+    batch = 4 * GROUP
+
     def rotate(c, s, step_c, step_s):
         return c * step_c - s * step_s, s * step_c + c * step_s
 
     def body(i, carry):
-        rows = pl.ds(pl.multiple_of(i * GROUP, GROUP), GROUP)
-        to = pl.ds(pl.multiple_of(i * 2 * GROUP, 2 * GROUP), 2 * GROUP)
+        rows = pl.ds(pl.multiple_of(i * batch, batch), batch)
         steps = step_ref[rows, :]
-        steps = [jnp.broadcast_to(steps[:, n : n + 1], (GROUP, 128)) for n in range(4)]
+        steps = [jnp.broadcast_to(steps[:, n : n + 1], (batch, 128)) for n in range(4)]
         first = cos_ref[rows, :], sin_ref[rows, :]
         for j in range(FINE):
             c, s = first
             for chunk in range(HALF // CHUNK):
                 at = chunk * CHUNK + j * 128
-                out_ref[to, at : at + 128] = jnp.concatenate([c, -s], axis=0).astype(BF16)
+                parts = []
+                for g in range(batch // GROUP):
+                    parts += [c[GROUP * g : GROUP * g + GROUP], -s[GROUP * g : GROUP * g + GROUP]]
+                to = pl.ds(pl.multiple_of(i * 2 * batch, 2 * batch), 2 * batch)
+                out_ref[to, at : at + 128] = jnp.concatenate(parts, axis=0).astype(BF16)
                 if chunk < HALF // CHUNK - 1:
                     c, s = rotate(c, s, *steps[2:])
             if j < FINE - 1:
                 first = rotate(*first, *steps[:2])
         return carry
 
-    lax.fori_loop(0, cos_ref.shape[0] // GROUP, body, 0)
+    lax.fori_loop(0, cos_ref.shape[0] // batch, body, 0)
 
 
 def angle_tables(slot_pair):
@@ -249,22 +256,18 @@
 
 
 def middle_kernel(
-    sub, parts, edge_ref, halo_ref, perm_ref, order_ref, taps_ref, scale_ref, weight_ref,
-    table_hbm, depart_hbm, pick_hbm, *refs,
+    sub, parts, edge_ref, halo_ref, perm_ref, order_ref, scale_ref, weight_ref,
+    table_hbm, factor_hbm, *refs,
 ):
     recv_refs, arrival_ref, coef_refs = refs[:parts], refs[parts], refs[parts + 1 : 2 * parts + 1]
     (
-        table_ref, depart_ref, pick_ref, left_ref, plus_ref, minus_ref, grid_ref, near_ref,
-        stage_ref, code_ref, moved_ref, pair_ref, sums_ref, sems,
+        table_ref, factor_ref, left_ref, plus_ref, minus_ref, grid_ref, near_ref,
+        stage_ref, moved_ref, pair_ref, sums_ref, table_sem, factor_sems,
     ) = refs[2 * parts + 1 :]
     per_part = TILES // parts
-    copies = [
-        pltpu.make_async_copy(table_hbm, table_ref, sems.at[0]),
-        pltpu.make_async_copy(depart_hbm, depart_ref, sems.at[1]),
-        pltpu.make_async_copy(pick_hbm, pick_ref, sems.at[2]),
-    ]
-    for copy in copies:
-        copy.start()
+    table_copy = pltpu.make_async_copy(table_hbm, table_ref, table_sem)
+    table_copy.start()
+    pltpu.make_async_copy(factor_hbm.at[0], factor_ref.at[0], factor_sems.at[0]).start()
     own = FIELDS * RUN * 16
     is_first, is_last = edge_ref[0], edge_ref[1]
 
@@ -299,7 +302,7 @@
 
     for part in range(parts):
         lax.fori_loop(0, per_part, functools.partial(gather_rows, part), 0)
-    copies[0].wait()
+    table_copy.wait()
 
     def to_grid(tile, carry):
         cols = pl.ds(pl.multiple_of(tile * 256, 256), 256)
@@ -334,14 +337,21 @@
         return carry
 
     lax.fori_loop(0, HALF // 256, to_grid, 0)
-    copies[1].wait()
-    copies[2].wait()
+    def fetch(chunk, slot):
+        return pltpu.make_async_copy(
+            factor_hbm.at[chunk], factor_ref.at[slot], factor_sems.at[slot]
+        )
 
     def interpolate(chunk, carry):
         lanes = pl.ds(pl.multiple_of(chunk * CHUNK, CHUNK), CHUNK)
         lane = lax.broadcasted_iota(jnp.int32, (16, 128), 1)
         previous = jnp.where(chunk == 0, CHUNKS - 1, chunk - 1)
         following = jnp.where(chunk == CHUNKS - 1, 0, chunk + 1)
+        slot = lax.rem(chunk, 2)
+
+        @pl.when(chunk + 1 < CHUNKS)
+        def _():
+            fetch(chunk + 1, 1 - slot).start()
 
         def neighbours(row, carry):
             for j in range(FINE):
@@ -352,62 +362,40 @@
                     at = pl.ds(pl.multiple_of(previous * CHUNK + j * 128, 128), 128)
                     there = grid_ref[row, :, at].astype(F32)
                     mixed = pltpu.roll(jnp.where(lane == 127, there, here), 1, 1)
-                    slot = j - (FINE - RIM)
-                    near_ref[row, :, slot * 128 : slot * 128 + 128] = mixed.astype(BF16)
+                    to = (j - (FINE - RIM)) * 128
+                    near_ref[row, :, to : to + 128] = mixed.astype(BF16)
                 if j < RIM:
                     at = pl.ds(pl.multiple_of(following * CHUNK + j * 128, 128), 128)
                     there = grid_ref[row, :, at].astype(F32)
                     mixed = pltpu.roll(jnp.where(lane == 0, there, here), 127, 1)
-                    slot = RIM + FINE + j
-                    near_ref[row, :, slot * 128 : slot * 128 + 128] = mixed.astype(BF16)
+                    to = (RIM + FINE + j) * 128
+                    near_ref[row, :, to : to + 128] = mixed.astype(BF16)
             return carry
 
         lax.fori_loop(0, FIELDS * REACH, neighbours, 0, unroll=4)
-        code = pick_ref[:, :, lanes] * 16 + depart_ref[:, :, lanes]
-        code = code.reshape(2 * RUN * SUB, CHUNK).astype(F32).astype(BF16)
-        code = jnp.dot(code, order_ref[0], preferred_element_type=F32).astype(jnp.int32)
-        for j in range(FINE):
-            code_ref[j] = code[:, 128 * j : 128 * j + 128]
+        fetch(chunk, slot).wait()
 
         def points(j, carry):
             at_lanes = pl.ds(pl.multiple_of(chunk * CHUNK + j * 128, 128), 128)
             for k in range(RUN):
-                index, column = [], []
-                for h in range(2):
-                    code = code_ref[j, pl.ds(h * RUN * SUB + k, SUB, stride=RUN), :]
-                    index.append(code >> 2)
-                    column.append(code & 3)
-                column = jnp.concatenate(column, axis=0).astype(F32).astype(BF16)
-                hits = [column == jnp.asarray(d, BF16) for d in range(4)]
-                totals = [jnp.zeros((16, 128), F32) for _ in range(FIELDS)]
+                totals = [None] * FIELDS
                 for r in range(7):
-                    weights = []
-                    for b in range(4):
-                        entry = taps_ref[r * 4 + b]
-                        found = [jnp.take_along_axis(entry, index[h], axis=1) for h in range(2)]
-                        weights.append(jnp.concatenate(found, axis=0).astype(BF16))
-                    factors = []
-                    for c in range(-RIM, RIM + 1):
-                        factor = jnp.zeros((16, 128), BF16)
-                        for d in range(4):
-                            b = c - (d - 2) + 1
-                            if 0 <= b < 4:
-                                factor = jnp.where(hits[d], weights[b], factor)
-                        factors.append(factor)
+                    factors = [factor_ref[slot, j, k, r * 7 + c] for c in range(7)]
                     for f in range(FIELDS):
                         row = f * REACH + k + r
                         part = None
                         for c in range(7):
                             near = near_ref[row, :, pl.ds(pl.multiple_of((j + c) * 128, 128), 128)]
                             part = factors[c] * near if part is None else part + factors[c] * near
-                        totals[f] = totals[f] + part.astype(F32)
+                        part = part.astype(F32)
+                        totals[f] = part if totals[f] is None else totals[f] + part
                 for f in range(FIELDS):
                     at = (f * RUN + k) * 16
                     moved_ref[at : at + 16, at_lanes] = totals[f].astype(BF16)
             return carry
 
         lax.fori_loop(0, FINE, points, 0)
-        natural = jnp.dot(moved_ref[:, lanes], order_ref[1], preferred_element_type=F32)
+        natural = jnp.dot(moved_ref[:, lanes], order_ref[...], preferred_element_type=F32)
         for j in range(FINE):
             for f in range(FIELDS):
                 for k in range(RUN):
@@ -469,7 +457,7 @@
         lax.fori_loop(0, per_part, functools.partial(scatter_rows, part), 0)
 
 
-def transport(sub, edge, recv, halo, perm, order, taps, scale, weight, table, depart, pick):
+def transport(sub, edge, recv, halo, perm, order, scale, weight, table, factors):
     parts = len(recv)
     rows, width = recv[0].shape
     lats = RUN * SUB
@@ -484,23 +472,22 @@
             jax.ShapeDtypeStruct((FIELDS, 2, lats, NLON), BF16),
             *[jax.ShapeDtypeStruct((rows, width), BF16)] * parts,
         ),
-        in_specs=[pl.BlockSpec(memory_space=pltpu.SMEM)] + [vmem] * 6 + [anywhere] * 3 + [vmem] * parts,
+        in_specs=[pl.BlockSpec(memory_space=pltpu.SMEM)] + [vmem] * 5 + [anywhere] * 2 + [vmem] * parts,
         out_specs=(vmem,) * (parts + 1),
         scratch_shapes=[
             pltpu.VMEM((2, slots2, HALF), BF16),
-            pltpu.VMEM((2, lats, NLON), jnp.int32),
-            pltpu.VMEM((2, lats, NLON), jnp.int32),
+            pltpu.VMEM((2,) + factors.shape[1:], BF16),
             pltpu.VMEM((2, left, slots2), BF16),
             pltpu.VMEM((left, 256), F32),
             pltpu.VMEM((left, 256), F32),
             pltpu.VMEM((FIELDS * REACH, 16, NLON), BF16),
             pltpu.VMEM((FIELDS * REACH, 16, CHUNK + 2 * RIM * 128), BF16),
             pltpu.VMEM((FINE, FIELDS * 2, lats, 128), F32),
-            pltpu.VMEM((FINE, 2 * lats, 128), jnp.int32),
             pltpu.VMEM((own, NLON), BF16),
             pltpu.VMEM((2, own, HALF), BF16),
             pltpu.VMEM((2, TILES, own, 128), F32),
-            pltpu.SemaphoreType.DMA((3,)),
+            pltpu.SemaphoreType.DMA,
+            pltpu.SemaphoreType.DMA((2,)),
         ],
         compiler_params=pltpu.CompilerParams(vmem_limit_bytes=VMEM_LIMIT),
         cost_estimate=pl.CostEstimate(
@@ -509,7 +496,68 @@
             transcendentals=0,
         ),
         name="transport",
-    )(edge, halo, perm, order, taps, scale, weight, table, depart, pick, *recv)
+    )(edge, halo, perm, order, scale, weight, table, factors, *recv)
+
+
+def factor_kernel(depart_ref, pick_ref, order_ref, taps_ref, out_ref, code_ref):
+    code = pick_ref[...] * 16 + depart_ref[...]
+    code = code.reshape(2 * RUN * SUB, CHUNK).astype(F32).astype(BF16)
+    code = jnp.dot(code, order_ref[...], preferred_element_type=F32).astype(jnp.int32)
+    for j in range(FINE):
+        code_ref[j] = code[:, 128 * j : 128 * j + 128]
+
+    def points(j, carry):
+        for k in range(RUN):
+            index, column = [], []
+            for h in range(2):
+                code = code_ref[j, pl.ds(h * RUN * SUB + k, SUB, stride=RUN), :]
+                index.append(code >> 2)
+                column.append(code & 3)
+            column = jnp.concatenate(column, axis=0).astype(F32).astype(BF16)
+            hits = [column == jnp.asarray(d, BF16) for d in range(4)]
+            for r in range(2 * RIM + 1):
+                weights = []
+                for b in range(4):
+                    entry = taps_ref[r * 4 + b]
+                    found = [jnp.take_along_axis(entry, index[h], axis=1) for h in range(2)]
+                    weights.append(jnp.concatenate(found, axis=0).astype(BF16))
+                for c in range(-RIM, RIM + 1):
+                    factor = jnp.zeros((16, 128), BF16)
+                    for d in range(4):
+                        b = c - (d - 2) + 1
+                        if 0 <= b < 4:
+                            factor = jnp.where(hits[d], weights[b], factor)
+                    out_ref[0, j, k, r * 7 + c + RIM] = factor
+        return carry
+
+    lax.fori_loop(0, FINE, points, 0)
+
+
+def stencil_factors(depart, pick, order, taps):
+    hemispheres, lats, longitudes = depart.shape
+    chunks = longitudes // CHUNK
+    shape = (FINE, RUN, REACH_TAPS, 16, 128)
+    code = pl.BlockSpec((hemispheres, lats, CHUNK), lambda i: (0, 0, i))
+    return pl.pallas_call(
+        factor_kernel,
+        out_shape=jax.ShapeDtypeStruct((chunks,) + shape, BF16),
+        grid=(chunks,),
+        in_specs=[
+            code,
+            code,
+            pl.BlockSpec(order.shape, lambda i: (0, 0)),
+            pl.BlockSpec(taps.shape, lambda i: (0, 0, 0)),
+        ],
+        out_specs=pl.BlockSpec((1,) + shape, lambda i: (i, 0, 0, 0, 0, 0)),
+        scratch_shapes=[pltpu.VMEM((FINE, 2 * lats, 128), jnp.int32)],
+        compiler_params=pltpu.CompilerParams(vmem_limit_bytes=VMEM_LIMIT),
+        cost_estimate=pl.CostEstimate(
+            flops=2 * REACH_TAPS * 4 * depart.size,
+            bytes_accessed=2 * REACH_TAPS * depart.size,
+            transcendentals=0,
+        ),
+        name="stencil_factors",
+    )(depart, pick, order, taps)
 
 
 def tap_tables(stencil_weight):
@@ -588,11 +636,20 @@
     spec, table, scale, taps, weight, edge, my_pairs = lax.optimization_barrier(
         (spec, table, scale, taps, weight, edge, my_pairs)
     )
+    depart, pick = depart_code[0], stencil_pick[0]
+    if sub != SUB:
+        gap = SUB - sub
+        depart = jnp.pad(depart, ((0, 0), (0, RUN * gap), (0, 0)))
+        pick = jnp.pad(pick, ((0, 0), (0, RUN * gap), (0, 0)))
+    to_lanes, to_longitudes = longitude_order()
     received = []
     for part in range(parts):
         sent = legendre_forward(my_pairs, spec, legendre, waves, part, parts)
         if received:
             sent, received[-1] = lax.optimization_barrier((sent, received[-1]))
+        if part == parts - 1:
+            sent, depart = lax.optimization_barrier((sent, depart))
+            factors = stencil_factors(depart, pick, to_lanes, taps)
         received.append(
             lax.all_to_all(sent, "wave", split_axis=0, concat_axis=0, tiled=True)
         )
@@ -608,26 +665,20 @@
     halo += [jnp.zeros_like(halo[0])] * (8 - 2 * RIM)
     halo = jnp.stack(halo, axis=1).reshape(blocks * 8, WIDE)
 
-    depart, pick = depart_code[0], stencil_pick[0]
     if sub != SUB:
-        gap = SUB - sub
         recv = [r.reshape(-1, RUN, sub, WIDE) for r in recv]
         recv = [jnp.pad(r, ((0, 0), (0, 0), (0, gap), (0, 0))) for r in recv]
-        depart = jnp.pad(depart, ((0, 0), (0, RUN * gap), (0, 0)))
-        pick = jnp.pad(pick, ((0, 0), (0, RUN * gap), (0, 0)))
     arrival, *coefs = transport(
         sub,
         edge,
         [r.reshape(-1, WIDE) for r in recv],
         halo,
         perm,
-        longitude_order(),
-        taps,
+        to_longitudes,
         scale,
         weight,
         table,
-        depart,
-        pick,
+        factors,
     )
     arrival = arrival[None, :, :, :height]
     coefs = [c.reshape(-1, RUN, SUB, WIDE)[:, :, :sub] for c in coefs]

time: 290 us -> 309 us (1.066)
  Pallas kernels: 159 us -> 174 us
  waiting for transfers between devices: 35.4 us -> 38.7 us
    pallas_call x0 -> x1, Pallas kernels: none -> 20.9 us  [stencil_factors(): pl.pallas_call(factor_kernel, out_shape=jax.ShapeDtypeStruct((chunks,) +...]
    pallas_call x1, Pallas kernels: 68.2 us -> 79 us  [transport(): pl.pallas_call(functools.partial(middle_kernel, sub, parts), out_shape=(j...]
    pallas_call x1, Pallas kernels: 18.4 us -> 11.2 us  [angle_tables(): pl.pallas_call(table_kernel, out_shape=jax.ShapeDtypeStruct((2 * count, H...]
    pallas_call x2, Pallas kernels: 34.4 us -> 29.4 us  [legendre_backward(): pl.pallas_call(functools.partial(backward_kernel, height, base), out_shap...]
    pallas_call x2, Pallas kernels: 38.1 us -> 33.4 us  [legendre_forward(): pl.pallas_call(functools.partial(forward_kernel, height, base), out_shape...]
  transfers between devices with their start and end apart: 14 -> 14, of which waited for: 6 -> 7; matrix products, arithmetic and copies ran while one was open for 7% -> 7% of each run, Pallas kernels for 25% -> 25%
where the time goes in v4:
time: 309 us; the launch traced here: 308 us
  Pallas kernels  174 us (56%)
  waiting for transfers between devices  38.7 us (13%)
  blocking collectives  33.9 us (11%)
  starting transfers between devices  28 us (9%)
  local copies, waits for them, and re-layouts  19.5 us (6%)
  other arithmetic  11.9 us (4%)
    pallas_call x1, Pallas kernels, transport(): pl.pallas_call(functools.partial(middle_kernel, sub, parts), out_shape=(j...  79 us
    all_to_all x1, blocking collectives, per_device(): lax.all_to_all(leaving, 'wave', split_axis=0, concat_axis=0, tiled=True)  33.9 us
    pallas_call x2, Pallas kernels, legendre_forward(): pl.pallas_call(functools.partial(forward_kernel, height, base), out_shape...  33.4 us
    pallas_call x2, Pallas kernels, legendre_backward(): pl.pallas_call(functools.partial(backward_kernel, height, base), out_shap...  29.4 us
    all_to_all x2, waiting for transfers between devices, per_device(): lax.all_to_all(sent, 'wave', split_axis=0, concat_axis=0, tiled=True)  25.4 us
    pallas_call x1, Pallas kernels, stencil_factors(): pl.pallas_call(factor_kernel, out_shape=jax.ShapeDtypeStruct((chunks,) +...  20.9 us
    ppermute x9, starting transfers between devices, exchange(): lax.ppermute(array, axis, [(i, i ^ distance) for i in range(devices)])  12.6 us
    pallas_call x1, Pallas kernels, angle_tables(): pl.pallas_call(table_kernel, out_shape=jax.ShapeDtypeStruct((2 * count, H...  11.2 us
  transfers between devices with their start and end apart: 14, of which 7 were waited for; matrix products, arithmetic and copies ran while one was open for 7% of the time, Pallas kernels for 25%

profile of v4, /device:TPU:0, one launch (start us, length us, event | category | flops | bytes accessed | tf_op | source)
XLA Modules:
  0.0 307.8 jit_solution(1465541299233935506)
XLA Ops:
  0.7 3.0 collective-permute-start.1
  3.7 1.5 collective-permute-start
  5.2 0.8 reshape.146
  6.2 1.3 dynamic_slice.49.pair_ref
  7.6 0.8 dynamic_slice.48
  8.6 0.9 convolution_bitcast_fusion
  10.3 4.2 %sine_multiply_fusion = (f32[1280,128]{1,0:T(8,128)}, f32[1280,128]{1,0:T(8,128)}) fusion(s32[128]{0:T(128)S(1)} %iota_multiply_fusion, s32[1280]{0:T(1024)S(1)} %pad_add_fusion, f32[1280]{0:T(1024)S(1)} %compare_select_fusion), kind=kLoop, calls=%fused_computation.14 | loop fusion | flops 1802240 | bytes 1321472 | tf_op jit(solution)/shard_map/mul | solution.py:221
  14.5 3.8 %sine_select_fusion.step_ref = f32[1280,4]{1,0:T(8,128)} fusion(s32[1280]{0:T(1024)S(1)} %pad_add_fusion, s32[4]{0:T(128)S(1)} %copy-done.6, pred[4]{0:T(512)(128)(4,1)S(1)} %fusion.29), kind=kLoop, calls=%fused_computation.10 | loop fusion | flops 51200 | bytes 25620 | tf_op jit(solution)/shard_map/jit(_where)/select_n | solution.py:223
  18.2 11.2 %angle_tables.1 = bf16[2560,2560]{1,0:T(8,128)(2,1)} custom-call(f32[1280,128]{1,0:T(8,128)} %get-tuple-element.61.cos_ref, f32[1280,128]{1,0:T(8,128)} %get-tuple-element.60.sin_ref, f32[1280,4]{1,0:T(8,128)} %sine_select_fusion.step_ref), custom_call_target="tpu_custom_call" | custom-call | flops 19660800 | bytes 13107200 | tf_op jit(solution)/shard_map/angle_tables/pallas_call | solution.py:225
  29.5 0.6 add_convert_fusion.edge_ref
  30.8 2.5 concatenate.25.spec_ref
  33.3 0.6 broadcast_in_dim.57.scale_ref
  33.9 0.7 broadcast_in_dim.58.taps_ref
  34.5 0.8 broadcast_in_dim.61.weight_ref
  35.3 16.7 %legendre_forward.3 = bf16[8,5,40,256]{3,2,1,0:T(8,128)(2,1)} custom-call(s32[80]{0:T(128)} %dynamic_slice.49.pair_ref, bf16[80,8,1408]{2,1,0:T(8,128)(2,1)} %concatenate.25.spec_ref, bf16[80,320,1408]{2,1,0:T(8,128)(2,1)} %leg_ref.7), custom_call_target="tpu_custom_call" | custom-call | flops 1153433600 | bytes 36044800 | tf_op jit(solution)/shard_map/legendre_forward/pallas_call | solution.py:101
  52.0 5.3 %all-to-all-start = ((bf16[8,5,40,256]{3,2,1,0:T(8,128)(2,1)}), bf16[8,5,40,256]{3,2,1,0:T(8,128)(2,1)S(1)}, u32[]{:S(2)}, u32[]{:S(2)}) async-start(bf16[8,5,40,256]{3,2,1,0:T(8,128)(2,1)} %legendre_forward.3), calls=%async_computation | async-start | bytes 1638400 | tf_op jit(solution)/shard_map/all_to_all | solution.py:654
  57.3 16.7 %legendre_forward.2 = bf16[8,5,40,256]{3,2,1,0:T(8,128)(2,1)} custom-call(s32[80]{0:T(128)} %dynamic_slice.49.pair_ref, bf16[80,8,1408]{2,1,0:T(8,128)(2,1)} %concatenate.25.spec_ref, bf16[80,320,1408]{2,1,0:T(8,128)(2,1)} %leg_ref.7), custom_call_target="tpu_custom_call" | custom-call | flops 1153433600 | bytes 36044800 | tf_op jit(solution)/shard_map/legendre_forward/pallas_call | solution.py:101
  74.0 5.0 %all-to-all-done = bf16[8,5,40,256]{3,2,1,0:T(8,128)(2,1)S(1)} async-done(((bf16[8,5,40,256]{3,2,1,0:T(8,128)(2,1)}), bf16[8,5,40,256]{3,2,1,0:T(8,128)(2,1)S(1)}, u32[]{:S(2)}, u32[]{:S(2)}) %all-to-all-start) | async-done | bytes 819232 | tf_op jit(solution)/shard_map/all_to_all | solution.py:654
  79.0 3.5 %all-to-all-start.1 = ((bf16[8,5,40,256]{3,2,1,0:T(8,128)(2,1)}), bf16[8,5,40,256]{3,2,1,0:T(8,128)(2,1)S(1)}, u32[]{:S(2)}, u32[]{:S(2)}) async-start(bf16[8,5,40,256]{3,2,1,0:T(8,128)(2,1)} %legendre_forward.2), calls=%async_computation.1 | async-start | bytes 1638400 | tf_op jit(solution)/shard_map/all_to_all | solution.py:654
  82.5 1.2 slice.75
  83.7 20.4 %all-to-all-done.1 = bf16[8,5,40,256]{3,2,1,0:T(8,128)(2,1)S(1)} async-done(((bf16[8,5,40,256]{3,2,1,0:T(8,128)(2,1)}), bf16[8,5,40,256]{3,2,1,0:T(8,128)(2,1)S(1)}, u32[]{:S(2)}, u32[]{:S(2)}) %all-to-all-start.1) | async-done | bytes 819232 | tf_op jit(solution)/shard_map/all_to_all | solution.py:654
  104.1 1.1 slice.76
  105.4 1.6 collective-permute-start.3
  106.9 20.9 %stencil_factors.1.factor_hbm = bf16[10,4,5,49,16,128]{5,4,3,2,1,0:T(8,128)(2,1)} custom-call(s32[2,40,5120]{2,1,0:T(8,128)} %bitcast.85, s32[2,40,5120]{2,1,0:T(8,128)} %bitcast.86, bf16[512,512]{1,0:T(8,128)(2,1)} %constant.130.clone.order_ref, f32[28,8,128]{2,1,0:T(8,128)} %broadcast_in_dim.58.taps_ref), custom_call_target="tpu_custom_call" | custom-call | flops 160563200 | bytes 40140800 | tf_op jit(solution)/shard_map/stencil_factors/pallas_call | solution.py:541
  127.8 0.5 slice.72
  128.3 0.5 slice.73
  129.0 1.5 collective-permute-start.4
  131.0 1.3 collective-permute-done.4
  132.8 3.1 stack.75
  135.9 79.0 %transport.1 = (bf16[4,2,40,5120]{3,2,1,0:T(8,128)(2,1)}, bf16[1600,256]{1,0:T(8,128)(2,1)}, bf16[1600,256]{1,0:T(8,128)(2,1)}) custom-call(s32[2]{0:T(128)} %add_convert_fusion.edge_ref, bf16[640,256]{1,0:T(8,128)(2,1)} %bitcast.87, bf16[256,256]{1,0:T(8,128)(2,1)} %constant.126.clone.perm_ref, bf16[512,512]{1,0:T(8,128)(2,1)} %constant.131.clone.order_ref, ...), custom_call_target="tpu_custom_call" | custom-call | flops 10066329600 | bytes 19660800 | tf_op jit(solution)/shard_map/transport/pallas_call | solution.py:469
  214.9 33.9 %all_to_all.20.coef_ref = bf16[8,5,40,256]{3,2,1,0:T(8,128)(2,1)} all-to-all(bf16[8,5,40,256]{3,2,1,0:T(8,128)(2,1)} %bitcast.89), channel_id=1, replica_groups=mesh['band'=4,'wave'=8] {'wave'}, dimensions={0} | all-to-all | bytes 1638400 | tf_op jit(solution)/shard_map/all_to_all | solution.py:691
  248.8 3.5 %all-to-all-start.3 = ((bf16[8,5,40,256]{3,2,1,0:T(8,128)(2,1)}), bf16[8,5,40,256]{3,2,1,0:T(8,128)(2,1)S(1)}, u32[]{:S(2)}, u32[]{:S(2)}) async-start(bf16[8,5,40,256]{3,2,1,0:T(8,128)(2,1)} %bitcast.88), calls=%async_computation.3 | async-start | bytes 1638400 | tf_op jit(solution)/shard_map/all_to_all | solution.py:691
  252.4 14.7 %legendre_backward.2 = bf16[320,1408]{1,0:T(8,128)(2,1)} custom-call(s32[80]{0:T(128)} %dynamic_slice.49.pair_ref, bf16[256,256]{1,0:T(8,128)(2,1)} %constant.126.clone.perm_ref, bf16[8,5,40,256]{3,2,1,0:T(8,128)(2,1)} %all_to_all.20.coef_ref, bf16[80,320,1408]{2,1,0:T(8,128)(2,1)} %leg_ref.7), custom_call_target="tpu_custom_call" | custom-call | flops 1153433600 | bytes 36044800 | tf_op jit(solution)/shard_map/legendre_backward/pallas_call | solution.py:157
  267.1 1.7 slice_bitcast_fusion.7
  269.1 2.5 collective-permute-start.5
  271.6 0.6 collective-permute-start.7
  272.2 0.9 collective-permute-start.6
  273.1 0.9 all-to-all-done.3.coef_ref
  274.0 0.9 copy-done.4
  274.9 14.7 %legendre_backward.3 = bf16[320,1408]{1,0:T(8,128)(2,1)} custom-call(s32[80]{0:T(128)} %dynamic_slice.49.pair_ref, bf16[256,256]{1,0:T(8,128)(2,1)} %constant.126.clone.perm_ref, bf16[8,5,40,256]{3,2,1,0:T(8,128)(2,1)} %copy-done.4, bf16[80,320,1408]{2,1,0:T(8,128)(2,1)} %leg_ref.7), custom_call_target="tpu_custom_call" | custom-call | flops 1153433600 | bytes 36044800 | tf_op jit(solution)/shard_map/legendre_backward/pallas_call | solution.py:157
  289.6 1.7 slice_bitcast_fusion.3
  291.6 2.5 collective-permute-start.8
  294.0 0.6 collective-permute-start.10
  294.6 1.0 collective-permute-start.9
  295.7 5.1 %collective-permute-done.8 = bf16[40,8,352]{2,1,0:T(8,128)(2,1)S(1)} collective-permute-done((bf16[40,8,352]{2,1,0:T(8,128)(2,1)S(1)}, bf16[40,8,352]{2,1,0:T(8,128)(2,1)S(1)}, u32[]{:S(2)}, u32[]{:S(2)}) %collective-permute-start.8) | collective-permute-done | bytes 225312 | tf_op jit(solution)/shard_map/ppermute | solution.py:578
  300.8 4.6 %collective-permute-done.10 = bf16[40,8,352]{2,1,0:T(8,128)(2,1)S(1)} collective-permute-done((bf16[40,8,352]{2,1,0:T(8,128)(2,1)S(1)}, bf16[40,8,352]{2,1,0:T(8,128)(2,1)S(1)}, u32[]{:S(2)}, u32[]{:S(2)}) %collective-permute-start.10) | collective-permute-done | bytes 225312 | tf_op jit(solution)/shard_map/ppermute | solution.py:578
  305.5 1.4 collective-permute-done.9
  307.0 0.9 pad_maximum_fusion.3
  (56 shorter events, 4.1 us)
Async XLA Ops:
  0.6 8.0 %copy-start = (f32[16,16]{1,0:T(8,128)S(1)}, f32[16,16]{1,0:T(8,128)}, u32[]{:S(2)}) copy-start(f32[16,16]{1,0:T(8,128)} %param.19) | copy-start | bytes 3076
  0.6 13.8 %copy-start.6 = (s32[4]{0:T(128)S(1)}, s32[4]{0:T(128)}, u32[]{:S(2)}) copy-start(s32[4]{0:T(128)} %constant.128.clone) | copy-start | bytes 52
  0.7 29.4 %collective-permute-start.1 = (bf16[80,8,352]{2,1,0:T(8,128)(2,1)}, bf16[80,8,352]{2,1,0:T(8,128)(2,1)S(1)}, u32[]{:S(2)}, u32[]{:S(2)}) collective-permute-start(bf16[80,8,352]{2,1,0:T(8,128)(2,1)} %bitcast.90), channel_id=1, source_target_pairs={{0,16},{8,24},{16,0},{24,8},{1,17},{9,25},{17,1},{25,9},{2,18},{10... | collective-permute-start | bytes 1351688 | tf_op jit(solution)/shard_map/ppermute | solution.py:578
  3.7 26.4 %collective-permute-start = (bf16[80,8,352]{2,1,0:T(8,128)(2,1)}, bf16[80,8,352]{2,1,0:T(8,128)(2,1)S(1)}, u32[]{:S(2)}, u32[]{:S(2)}) collective-permute-start(bf16[80,8,352]{2,1,0:T(8,128)(2,1)} %bitcast.91), channel_id=1, source_target_pairs={{0,8},{8,0},{16,24},{24,16},{1,9},{9,1},{17,25},{25,17},{2,10},{10... | collective-permute-start | bytes 1351688 | tf_op jit(solution)/shard_map/ppermute | solution.py:578
  5.2 24.9 %collective-permute-start.2 = (bf16[80,8,352]{2,1,0:T(8,128)(2,1)}, bf16[80,8,352]{2,1,0:T(8,128)(2,1)S(1)}, u32[]{:S(2)}, u32[]{:S(2)}) collective-permute-start(bf16[80,8,352]{2,1,0:T(8,128)(2,1)} %bitcast.92), channel_id=1, source_target_pairs={{0,24},{8,16},{16,8},{24,0},{1,25},{9,17},{17,9},{25,1},{2,26},{10... | collective-permute-start | bytes 1351688 | tf_op jit(solution)/shard_map/ppermute | solution.py:578
  18.2 11.8 %copy-start.5 = (bf16[80,352,8]{1,2,0:T(8,128)(2,1)S(1)}, bf16[80,352,8]{1,2,0:T(8,128)(2,1)}, u32[]{:S(2)}) copy-start(bf16[80,352,8]{1,2,0:T(8,128)(2,1)} %param.13) | copy-start | bytes 1351684
  52.0 27.0 %all-to-all-start = ((bf16[8,5,40,256]{3,2,1,0:T(8,128)(2,1)}), bf16[8,5,40,256]{3,2,1,0:T(8,128)(2,1)S(1)}, u32[]{:S(2)}, u32[]{:S(2)}) async-start(bf16[8,5,40,256]{3,2,1,0:T(8,128)(2,1)} %legendre_forward.3), calls=%async_computation | async-start | bytes 1638400 | tf_op jit(solution)/shard_map/all_to_all | solution.py:654
  79.0 48.8 %copy-start.2 = (bf16[8,5,40,256]{3,2,1,0:T(8,128)(2,1)}, bf16[8,5,40,256]{3,2,1,0:T(8,128)(2,1)S(1)}, u32[]{:S(2)}) copy-start(bf16[8,5,40,256]{3,2,1,0:T(8,128)(2,1)S(1)} %all-to-all-done) | copy-start | bytes 2457604
  79.0 25.2 %all-to-all-start.1 = ((bf16[8,5,40,256]{3,2,1,0:T(8,128)(2,1)}), bf16[8,5,40,256]{3,2,1,0:T(8,128)(2,1)S(1)}, u32[]{:S(2)}, u32[]{:S(2)}) async-start(bf16[8,5,40,256]{3,2,1,0:T(8,128)(2,1)} %legendre_forward.2), calls=%async_computation.1 | async-start | bytes 1638400 | tf_op jit(solution)/shard_map/all_to_all | solution.py:654
  104.1 24.2 %copy-start.3 = (bf16[8,5,40,256]{3,2,1,0:T(8,128)(2,1)}, bf16[8,5,40,256]{3,2,1,0:T(8,128)(2,1)S(1)}, u32[]{:S(2)}) copy-start(bf16[8,5,40,256]{3,2,1,0:T(8,128)(2,1)S(1)} %all-to-all-done.1) | copy-start | bytes 2457604
  105.4 25.1 %collective-permute-start.3 = (bf16[80,3,256]{2,1,0:T(4,128)(2,1)S(1)}, bf16[80,3,256]{2,1,0:T(4,128)(2,1)S(1)}, u32[]{:S(2)}, u32[]{:S(2)}) collective-permute-start(bf16[80,3,256]{2,1,0:T(4,128)(2,1)S(1)} %pad_maximum_fusion.5), channel_id=1, source_target_pairs={{0,1},{1,2},{2,3},{3,4},{4,5},{5,6},{6,7},{7,8},{8,9},{9,10},{10,1... | collective-permute-start | bytes 368648 | tf_op jit(solution)/shard_map/ppermute | solution.py:661
  129.0 3.3 %collective-permute-start.4 = (bf16[80,3,256]{2,1,0:T(4,128)(2,1)S(1)}, bf16[80,3,256]{2,1,0:T(4,128)(2,1)S(1)}, u32[]{:S(2)}, u32[]{:S(2)}) collective-permute-start(bf16[80,3,256]{2,1,0:T(4,128)(2,1)S(1)} %pad_maximum_fusion.4), channel_id=1, source_target_pairs={{1,0},{2,1},{3,2},{4,3},{5,4},{6,5},{7,6},{8,7},{9,8},{10,9},{11,1... | collective-permute-start | bytes 368648 | tf_op jit(solution)/shard_map/ppermute | solution.py:662
  248.8 25.2 %all-to-all-start.3 = ((bf16[8,5,40,256]{3,2,1,0:T(8,128)(2,1)}), bf16[8,5,40,256]{3,2,1,0:T(8,128)(2,1)S(1)}, u32[]{:S(2)}, u32[]{:S(2)}) async-start(bf16[8,5,40,256]{3,2,1,0:T(8,128)(2,1)} %bitcast.88), calls=%async_computation.3 | async-start | bytes 1638400 | tf_op jit(solution)/shard_map/all_to_all | solution.py:691
  269.1 25.5 %collective-permute-start.5 = (bf16[40,8,352]{2,1,0:T(8,128)(2,1)S(1)}, bf16[40,8,352]{2,1,0:T(8,128)(2,1)S(1)}, u32[]{:S(2)}, u32[]{:S(2)}) collective-permute-start(bf16[40,8,352]{2,1,0:T(8,128)(2,1)S(1)} %get-tuple-element.38), channel_id=1, source_target_pairs={{0,8},{8,0},{16,24},{24,16},{1,9},{9,1},{17,25},{25,17},{2,10},{10... | collective-permute-start | bytes 675848 | tf_op jit(solution)/shard_map/ppermute | solution.py:578
  271.6 24.0 %collective-permute-start.7 = (bf16[40,8,352]{2,1,0:T(8,128)(2,1)S(1)}, bf16[40,8,352]{2,1,0:T(8,128)(2,1)S(1)}, u32[]{:S(2)}, u32[]{:S(2)}) collective-permute-start(bf16[40,8,352]{2,1,0:T(8,128)(2,1)S(1)} %get-tuple-element.39), channel_id=1, source_target_pairs={{0,24},{8,16},{16,8},{24,0},{1,25},{9,17},{17,9},{25,1},{2,26},{10... | collective-permute-start | bytes 675848 | tf_op jit(solution)/shard_map/ppermute | solution.py:578
  272.2 23.4 %collective-permute-start.6 = (bf16[40,8,352]{2,1,0:T(8,128)(2,1)S(1)}, bf16[40,8,352]{2,1,0:T(8,128)(2,1)S(1)}, u32[]{:S(2)}, u32[]{:S(2)}) collective-permute-start(bf16[40,8,352]{2,1,0:T(8,128)(2,1)S(1)} %get-tuple-element.40), channel_id=1, source_target_pairs={{0,16},{8,24},{16,0},{24,8},{1,17},{9,25},{17,1},{25,9},{2,18},{10... | collective-permute-start | bytes 675848 | tf_op jit(solution)/shard_map/ppermute | solution.py:578
  274.0 0.9 copy-start.4
  291.5 16.4 %copy-start.1 = (f32[16,16]{1,0:T(8,128)S(1)}, f32[16,16]{1,0:T(8,128)}, u32[]{:S(2)}) copy-start(f32[16,16]{1,0:T(8,128)} %param.19) | copy-start | bytes 3076
  291.6 9.3 %collective-permute-start.8 = (bf16[40,8,352]{2,1,0:T(8,128)(2,1)S(1)}, bf16[40,8,352]{2,1,0:T(8,128)(2,1)S(1)}, u32[]{:S(2)}, u32[]{:S(2)}) collective-permute-start(bf16[40,8,352]{2,1,0:T(8,128)(2,1)S(1)} %get-tuple-element.41), channel_id=1, source_target_pairs={{0,8},{8,0},{16,24},{24,16},{1,9},{9,1},{17,25},{25,17},{2,10},{10... | collective-permute-start | bytes 675848 | tf_op jit(solution)/shard_map/ppermute | solution.py:578
  294.0 11.4 %collective-permute-start.10 = (bf16[40,8,352]{2,1,0:T(8,128)(2,1)S(1)}, bf16[40,8,352]{2,1,0:T(8,128)(2,1)S(1)}, u32[]{:S(2)}, u32[]{:S(2)}) collective-permute-start(bf16[40,8,352]{2,1,0:T(8,128)(2,1)S(1)} %get-tuple-element.42), channel_id=1, source_target_pairs={{0,24},{8,16},{16,8},{24,0},{1,25},{9,17},{17,9},{25,1},{2,26},{10... | collective-permute-start | bytes 675848 | tf_op jit(solution)/shard_map/ppermute | solution.py:578
  294.6 12.2 %collective-permute-start.9 = (bf16[40,8,352]{2,1,0:T(8,128)(2,1)S(1)}, bf16[40,8,352]{2,1,0:T(8,128)(2,1)S(1)}, u32[]{:S(2)}, u32[]{:S(2)}) collective-permute-start(bf16[40,8,352]{2,1,0:T(8,128)(2,1)S(1)} %get-tuple-element.43), channel_id=1, source_target_pairs={{0,16},{8,24},{16,0},{24,8},{1,17},{9,25},{17,1},{25,9},{2,18},{10... | collective-permute-start | bytes 675848 | tf_op jit(solution)/shard_map/ppermute | solution.py:578

commit v5 on v3

--- a/solution.py
+++ b/solution.py
@@ -25,7 +25,7 @@
 CHUNK = 512
 FINE = CHUNK // 128
 CHUNKS = NLON // CHUNK
-STEP = 4
+STEP = 8
 F32 = jnp.float32
 BF16 = jnp.bfloat16
 VMEM_LIMIT = 60 * 2**20
@@ -76,7 +76,8 @@
         parts = [spec * even, south * even, spec * odd, south * odd]
         masked = jnp.concatenate(parts, axis=0).astype(BF16)
         pieces.append(dot_nt(leg_ref[u], masked))
-    acc_ref[step] = jnp.concatenate(pieces, axis=1)
+    for half in range(STEP // 4):
+        acc_ref[step * (STEP // 4) + half] = jnp.concatenate(pieces[4 * half : 4 * half + 4], axis=1)
 
     @pl.when(step == GROUP // STEP - 1)
     def _():
@@ -102,8 +103,8 @@
         grid=(groups, GROUP // STEP),
         in_specs=[
             pl.BlockSpec(memory_space=pltpu.SMEM),
-            pl.BlockSpec((STEP, COLS, rows), lambda g, t: (2 * (g + base) + t, 0, 0)),
-            pl.BlockSpec((STEP, lats, rows), lambda g, t: (2 * (g + base) + t, 0, 0)),
+            pl.BlockSpec((STEP, COLS, rows), lambda g, t: (GROUP // STEP * (g + base) + t, 0, 0)),
+            pl.BlockSpec((STEP, lats, rows), lambda g, t: (GROUP // STEP * (g + base) + t, 0, 0)),
         ],
         out_specs=pl.BlockSpec((waves, 1, height, WIDE), lambda g, t: (0, g, 0, 0)),
         scratch_shapes=[pltpu.VMEM((2, lats, 128), F32)],
@@ -160,9 +161,9 @@
             pl.BlockSpec(memory_space=pltpu.SMEM),
             pl.BlockSpec((WIDE, WIDE), lambda g, t: (0, 0)),
             pl.BlockSpec((waves, 1, height, WIDE), lambda g, t: (0, g, 0, 0)),
-            pl.BlockSpec((STEP, lats, rows), lambda g, t: (2 * (g + base) + t, 0, 0)),
+            pl.BlockSpec((STEP, lats, rows), lambda g, t: (GROUP // STEP * (g + base) + t, 0, 0)),
         ],
-        out_specs=pl.BlockSpec((STEP * COLS, rows), lambda g, t: (2 * g + t, 0)),
+        out_specs=pl.BlockSpec((STEP * COLS, rows), lambda g, t: (GROUP // STEP * g + t, 0)),
         scratch_shapes=[pltpu.VMEM((2, lats, 128), F32), pltpu.VMEM((WIDE, lats), BF16)],
         compiler_params=pltpu.CompilerParams(vmem_limit_bytes=VMEM_LIMIT),
         cost_estimate=pl.CostEstimate(
@@ -175,27 +176,32 @@
 
 
 def table_kernel(cos_ref, sin_ref, step_ref, out_ref):
+    batch = 4 * GROUP
+
     def rotate(c, s, step_c, step_s):
         return c * step_c - s * step_s, s * step_c + c * step_s
 
     def body(i, carry):
-        rows = pl.ds(pl.multiple_of(i * GROUP, GROUP), GROUP)
-        to = pl.ds(pl.multiple_of(i * 2 * GROUP, 2 * GROUP), 2 * GROUP)
+        rows = pl.ds(pl.multiple_of(i * batch, batch), batch)
         steps = step_ref[rows, :]
-        steps = [jnp.broadcast_to(steps[:, n : n + 1], (GROUP, 128)) for n in range(4)]
+        steps = [jnp.broadcast_to(steps[:, n : n + 1], (batch, 128)) for n in range(4)]
         first = cos_ref[rows, :], sin_ref[rows, :]
         for j in range(FINE):
             c, s = first
             for chunk in range(HALF // CHUNK):
                 at = chunk * CHUNK + j * 128
-                out_ref[to, at : at + 128] = jnp.concatenate([c, -s], axis=0).astype(BF16)
+                parts = []
+                for g in range(batch // GROUP):
+                    parts += [c[GROUP * g : GROUP * g + GROUP], -s[GROUP * g : GROUP * g + GROUP]]
+                to = pl.ds(pl.multiple_of(i * 2 * batch, 2 * batch), 2 * batch)
+                out_ref[to, at : at + 128] = jnp.concatenate(parts, axis=0).astype(BF16)
                 if chunk < HALF // CHUNK - 1:
                     c, s = rotate(c, s, *steps[2:])
             if j < FINE - 1:
                 first = rotate(*first, *steps[:2])
         return carry
 
-    lax.fori_loop(0, cos_ref.shape[0] // GROUP, body, 0)
+    lax.fori_loop(0, cos_ref.shape[0] // batch, body, 0)
 
 
 def angle_tables(slot_pair):
@@ -313,7 +319,7 @@
             for f in range(FIELDS):
                 for k in range(RUN):
                     at = (f * RUN + k) * 16
-                    grid_ref[f * REACH + RIM + k, :, to] = ref[at : at + 16, :].astype(BF16)
+                    grid_ref[f * REACH + RIM + k, :, to] = ref[at : at + 16, :]
                 for k in range(RIM):
                     before, after = [], []
                     for h in range(2):
@@ -327,10 +333,8 @@
                         after.append(
                             jnp.where(place == sub - 1, ref[end + k : end + k + 1, :], rolled)
                         )
-                    grid_ref[f * REACH + k, :, to] = jnp.concatenate(before, 0).astype(BF16)
-                    grid_ref[f * REACH + RIM + RUN + k, :, to] = jnp.concatenate(after, 0).astype(
-                        BF16
-                    )
+                    grid_ref[f * REACH + k, :, to] = jnp.concatenate(before, 0)
+                    grid_ref[f * REACH + RIM + RUN + k, :, to] = jnp.concatenate(after, 0)
         return carry
 
     lax.fori_loop(0, HALF // 256, to_grid, 0)
@@ -347,19 +351,16 @@
             for j in range(FINE):
                 here = grid_ref[row, :, pl.ds(pl.multiple_of(chunk * CHUNK + j * 128, 128), 128)]
                 near_ref[row, :, (RIM + j) * 128 : (RIM + j + 1) * 128] = here
-                here = here.astype(F32)
                 if j >= FINE - RIM:
                     at = pl.ds(pl.multiple_of(previous * CHUNK + j * 128, 128), 128)
-                    there = grid_ref[row, :, at].astype(F32)
-                    mixed = pltpu.roll(jnp.where(lane == 127, there, here), 1, 1)
-                    slot = j - (FINE - RIM)
-                    near_ref[row, :, slot * 128 : slot * 128 + 128] = mixed.astype(BF16)
+                    mixed = pltpu.roll(jnp.where(lane == 127, grid_ref[row, :, at], here), 1, 1)
+                    to = (j - (FINE - RIM)) * 128
+                    near_ref[row, :, to : to + 128] = mixed
                 if j < RIM:
                     at = pl.ds(pl.multiple_of(following * CHUNK + j * 128, 128), 128)
-                    there = grid_ref[row, :, at].astype(F32)
-                    mixed = pltpu.roll(jnp.where(lane == 0, there, here), 127, 1)
-                    slot = RIM + FINE + j
-                    near_ref[row, :, slot * 128 : slot * 128 + 128] = mixed.astype(BF16)
+                    mixed = pltpu.roll(jnp.where(lane == 0, grid_ref[row, :, at], here), 127, 1)
+                    to = (RIM + FINE + j) * 128
+                    near_ref[row, :, to : to + 128] = mixed
             return carry
 
         lax.fori_loop(0, FIELDS * REACH, neighbours, 0, unroll=4)
@@ -371,39 +372,46 @@
 
         def points(j, carry):
             at_lanes = pl.ds(pl.multiple_of(chunk * CHUNK + j * 128, 128), 128)
-            for k in range(RUN):
-                index, column = [], []
-                for h in range(2):
-                    code = code_ref[j, pl.ds(h * RUN * SUB + k, SUB, stride=RUN), :]
-                    index.append(code >> 2)
-                    column.append(code & 3)
-                column = jnp.concatenate(column, axis=0).astype(F32).astype(BF16)
-                hits = [column == jnp.asarray(d, BF16) for d in range(4)]
-                totals = [jnp.zeros((16, 128), F32) for _ in range(FIELDS)]
-                for r in range(7):
-                    weights = []
-                    for b in range(4):
-                        entry = taps_ref[r * 4 + b]
-                        found = [jnp.take_along_axis(entry, index[h], axis=1) for h in range(2)]
-                        weights.append(jnp.concatenate(found, axis=0).astype(BF16))
-                    factors = []
-                    for c in range(-RIM, RIM + 1):
-                        factor = jnp.zeros((16, 128), BF16)
-                        for d in range(4):
-                            b = c - (d - 2) + 1
-                            if 0 <= b < 4:
-                                factor = jnp.where(hits[d], weights[b], factor)
-                        factors.append(factor)
+            for ks in ((0, 1), (2, 3), (4,)):
+                index, hits = {}, {}
+                for k in ks:
+                    codes = [
+                        code_ref[j, pl.ds(h * RUN * SUB + k, SUB, stride=RUN), :] for h in range(2)
+                    ]
+                    index[k] = [code >> 2 for code in codes]
+                    column = jnp.concatenate(codes, axis=0) & 3
+                    hits[k] = [column == d for d in range(4)]
+                totals = {}
+                for row in range(ks[0], ks[-1] + 7):
+                    factors = {}
+                    for k in ks:
+                        r = row - k
+                        if not 0 <= r < 7:
+                            continue
+                        weights = []
+                        for b in range(4):
+                            entry = taps_ref[r * 4 + b]
+                            found = [jnp.take_along_axis(entry, index[k][h], axis=1) for h in range(2)]
+                            weights.append(jnp.concatenate(found, axis=0))
+                        factors[k] = []
+                        for c in range(-RIM, RIM + 1):
+                            factor = jnp.zeros((16, 128), F32)
+                            for d in range(4):
+                                b = c - (d - 2) + 1
+                                if 0 <= b < 4:
+                                    factor = jnp.where(hits[k][d], weights[b], factor)
+                            factors[k].append(factor)
                     for f in range(FIELDS):
-                        row = f * REACH + k + r
-                        part = None
                         for c in range(7):
-                            near = near_ref[row, :, pl.ds(pl.multiple_of((j + c) * 128, 128), 128)]
-                            part = factors[c] * near if part is None else part + factors[c] * near
-                        totals[f] = totals[f] + part.astype(F32)
+                            lanes_c = pl.ds(pl.multiple_of((j + c) * 128, 128), 128)
+                            near = near_ref[f * REACH + row, :, lanes_c]
+                            for k in factors:
+                                term = factors[k][c] * near
+                                totals[f, k] = totals[f, k] + term if (f, k) in totals else term
                 for f in range(FIELDS):
-                    at = (f * RUN + k) * 16
-                    moved_ref[at : at + 16, at_lanes] = totals[f].astype(BF16)
+                    for k in ks:
+                        at = (f * RUN + k) * 16
+                        moved_ref[at : at + 16, at_lanes] = totals[f, k].astype(BF16)
             return carry
 
         lax.fori_loop(0, FINE, points, 0)
@@ -493,8 +501,8 @@
             pltpu.VMEM((2, left, slots2), BF16),
             pltpu.VMEM((left, 256), F32),
             pltpu.VMEM((left, 256), F32),
-            pltpu.VMEM((FIELDS * REACH, 16, NLON), BF16),
-            pltpu.VMEM((FIELDS * REACH, 16, CHUNK + 2 * RIM * 128), BF16),
+            pltpu.VMEM((FIELDS * REACH, 16, NLON), F32),
+            pltpu.VMEM((FIELDS * REACH, 16, CHUNK + 2 * RIM * 128), F32),
             pltpu.VMEM((FINE, FIELDS * 2, lats, 128), F32),
             pltpu.VMEM((FINE, 2 * lats, 128), jnp.int32),
             pltpu.VMEM((own, NLON), BF16),

time: 290 us -> 294 us (1.014)
  waiting for transfers between devices: 35.4 us -> 38.7 us
    pallas_call x1, Pallas kernels: 68.2 us -> 84.2 us  [transport(): pl.pallas_call(functools.partial(middle_kernel, sub, parts), out_shape=(j...]
    pallas_call x1, Pallas kernels: 18.4 us -> 11.4 us  [angle_tables(): pl.pallas_call(table_kernel, out_shape=jax.ShapeDtypeStruct((2 * count, H...]
    pallas_call x2, Pallas kernels: 34.4 us -> 29.4 us  [legendre_backward(): pl.pallas_call(functools.partial(backward_kernel, height, base), out_shap...]
    pallas_call x2, Pallas kernels: 38.1 us -> 33.4 us  [legendre_forward(): pl.pallas_call(functools.partial(forward_kernel, height, base), out_shape...]
  transfers between devices with their start and end apart: 14 -> 14, of which waited for: 6 -> 7; matrix products, arithmetic and copies ran while one was open for 7% -> 7% of each run, Pallas kernels for 25% -> 20%
where the time goes in v5:
time: 294 us; the launch traced here: 292 us
  Pallas kernels  158 us (54%)
  waiting for transfers between devices  38.7 us (13%)
  blocking collectives  33.9 us (12%)
  starting transfers between devices  28 us (10%)
  local copies, waits for them, and re-layouts  19.5 us (7%)
  other arithmetic  12 us (4%)
    pallas_call x1, Pallas kernels, transport(): pl.pallas_call(functools.partial(middle_kernel, sub, parts), out_shape=(j...  84.2 us
    all_to_all x1, blocking collectives, per_device(): lax.all_to_all(leaving, 'wave', split_axis=0, concat_axis=0, tiled=True)  33.9 us
    pallas_call x2, Pallas kernels, legendre_forward(): pl.pallas_call(functools.partial(forward_kernel, height, base), out_shape...  33.4 us
    pallas_call x2, Pallas kernels, legendre_backward(): pl.pallas_call(functools.partial(backward_kernel, height, base), out_shap...  29.4 us
    all_to_all x2, waiting for transfers between devices, per_device(): lax.all_to_all(sent, 'wave', split_axis=0, concat_axis=0, tiled=True)  25.4 us
    ppermute x9, starting transfers between devices, exchange(): lax.ppermute(array, axis, [(i, i ^ distance) for i in range(devices)])  12.6 us
    pallas_call x1, Pallas kernels, angle_tables(): pl.pallas_call(table_kernel, out_shape=jax.ShapeDtypeStruct((2 * count, H...  11.4 us
    ppermute x9, waiting for transfers between devices, exchange(): lax.ppermute(array, axis, [(i, i ^ distance) for i in range(devices)])  11.1 us
  transfers between devices with their start and end apart: 14, of which 7 were waited for; matrix products, arithmetic and copies ran while one was open for 7% of the time, Pallas kernels for 20%

profile of v5, /device:TPU:0, one launch (start us, length us, event | category | flops | bytes accessed | tf_op | source)
XLA Modules:
  0.0 292.3 jit_solution(16517573384576329027)
XLA Ops:
  0.7 3.0 %collective-permute-start.1 = (bf16[80,8,352]{2,1,0:T(8,128)(2,1)}, bf16[80,8,352]{2,1,0:T(8,128)(2,1)S(1)}, u32[]{:S(2)}, u32[]{:S(2)}) collective-permute-start(bf16[80,8,352]{2,1,0:T(8,128)(2,1)} %bitcast.87), channel_id=1, source_target_pairs={{0,16},{8,24},{16,0},{24,8},{1,17},{9,25},{17,1},{25,9},{2,18},{10... | collective-permute-start | bytes 1351688 | tf_op jit(solution)/shard_map/ppermute | solution.py:538
  3.7 1.5 collective-permute-start
  5.2 0.8 reshape.146
  6.2 1.3 dynamic_slice.49.pair_ref
  7.5 0.8 dynamic_slice.48
  8.5 0.9 convolution_bitcast_fusion
  10.2 4.2 %sine_multiply_fusion = (f32[1280,128]{1,0:T(8,128)}, f32[1280,128]{1,0:T(8,128)}) fusion(s32[128]{0:T(128)S(1)} %iota_multiply_fusion, s32[1280]{0:T(1024)S(1)} %pad_add_fusion, f32[1280]{0:T(1024)S(1)} %compare_select_fusion), kind=kLoop, calls=%fused_computation.14 | loop fusion | flops 1802240 | bytes 1321472 | tf_op jit(solution)/shard_map/mul | solution.py:220
  14.4 3.8 %sine_select_fusion.step_ref = f32[1280,4]{1,0:T(8,128)} fusion(s32[1280]{0:T(1024)S(1)} %pad_add_fusion, s32[4]{0:T(128)S(1)} %copy-done.5, pred[4]{0:T(512)(128)(4,1)S(1)} %fusion.29), kind=kLoop, calls=%fused_computation.10 | loop fusion | flops 51200 | bytes 25620 | tf_op jit(solution)/shard_map/jit(_where)/select_n | solution.py:222
  18.2 11.4 %angle_tables.1 = bf16[2560,2560]{1,0:T(8,128)(2,1)} custom-call(f32[1280,128]{1,0:T(8,128)} %get-tuple-element.57.cos_ref, f32[1280,128]{1,0:T(8,128)} %get-tuple-element.56.sin_ref, f32[1280,4]{1,0:T(8,128)} %sine_select_fusion.step_ref), custom_call_target="tpu_custom_call" | custom-call | flops 19660800 | bytes 13107200 | tf_op jit(solution)/shard_map/angle_tables/pallas_call | solution.py:224
  29.6 0.7 add_convert_fusion.edge_ref
  30.9 2.5 concatenate.25.spec_ref
  33.4 0.6 broadcast_in_dim.57.scale_ref
  34.1 0.7 broadcast_in_dim.58.taps_ref
  34.7 0.8 broadcast_in_dim.61.weight_ref
  35.5 16.7 %legendre_forward.3 = bf16[8,5,40,256]{3,2,1,0:T(8,128)(2,1)} custom-call(s32[80]{0:T(128)} %dynamic_slice.49.pair_ref, bf16[80,8,1408]{2,1,0:T(8,128)(2,1)} %concatenate.25.spec_ref, bf16[80,320,1408]{2,1,0:T(8,128)(2,1)} %leg_ref.7), custom_call_target="tpu_custom_call" | custom-call | flops 1153433600 | bytes 36044800 | tf_op jit(solution)/shard_map/legendre_forward/pallas_call | solution.py:100
  52.2 5.3 %all-to-all-start = ((bf16[8,5,40,256]{3,2,1,0:T(8,128)(2,1)}), bf16[8,5,40,256]{3,2,1,0:T(8,128)(2,1)S(1)}, u32[]{:S(2)}, u32[]{:S(2)}) async-start(bf16[8,5,40,256]{3,2,1,0:T(8,128)(2,1)} %legendre_forward.3), calls=%async_computation | async-start | bytes 1638400 | tf_op jit(solution)/shard_map/all_to_all | solution.py:605
  57.5 16.7 %legendre_forward.2 = bf16[8,5,40,256]{3,2,1,0:T(8,128)(2,1)} custom-call(s32[80]{0:T(128)} %dynamic_slice.49.pair_ref, bf16[80,8,1408]{2,1,0:T(8,128)(2,1)} %concatenate.25.spec_ref, bf16[80,320,1408]{2,1,0:T(8,128)(2,1)} %leg_ref.7), custom_call_target="tpu_custom_call" | custom-call | flops 1153433600 | bytes 36044800 | tf_op jit(solution)/shard_map/legendre_forward/pallas_call | solution.py:100
  74.2 5.0 %all-to-all-done = bf16[8,5,40,256]{3,2,1,0:T(8,128)(2,1)S(1)} async-done(((bf16[8,5,40,256]{3,2,1,0:T(8,128)(2,1)}), bf16[8,5,40,256]{3,2,1,0:T(8,128)(2,1)S(1)}, u32[]{:S(2)}, u32[]{:S(2)}) %all-to-all-start) | async-done | bytes 819232 | tf_op jit(solution)/shard_map/all_to_all | solution.py:605
  79.2 3.5 %all-to-all-start.1 = ((bf16[8,5,40,256]{3,2,1,0:T(8,128)(2,1)}), bf16[8,5,40,256]{3,2,1,0:T(8,128)(2,1)S(1)}, u32[]{:S(2)}, u32[]{:S(2)}) async-start(bf16[8,5,40,256]{3,2,1,0:T(8,128)(2,1)} %legendre_forward.2), calls=%async_computation.1 | async-start | bytes 1638400 | tf_op jit(solution)/shard_map/all_to_all | solution.py:605
  82.7 1.2 slice.75
  83.9 20.4 %all-to-all-done.1 = bf16[8,5,40,256]{3,2,1,0:T(8,128)(2,1)S(1)} async-done(((bf16[8,5,40,256]{3,2,1,0:T(8,128)(2,1)}), bf16[8,5,40,256]{3,2,1,0:T(8,128)(2,1)S(1)}, u32[]{:S(2)}, u32[]{:S(2)}) %all-to-all-start.1) | async-done | bytes 819232 | tf_op jit(solution)/shard_map/all_to_all | solution.py:605
  104.3 1.1 slice.76
  105.6 1.6 collective-permute-start.3
  107.1 0.5 slice.72
  107.7 0.5 slice.73
  108.3 1.5 collective-permute-start.4
  109.8 0.5 broadcast_select_fusion.3
  110.3 1.3 collective-permute-done.4
  112.2 3.1 %stack.75 = bf16[80,8,256]{2,1,0:T(8,128)(2,1)} concatenate(bf16[80,1,256]{2,1,0:T(2,128)(2,1)S(1)} %get-tuple-element.53, bf16[80,1,256]{2,1,0:T(2,128)(2,1)S(1)} %get-tuple-element.52, bf16[80,1,256]{2,1,0:T(2,128)(2,1)S(1)} %get-tuple-element.51, bf16[80,1,256]{2,1,0:T(2,128)(2,1)S(1)} %get-tuple-element.50, bf16[80,1,256]{2,1,0:T(2,128)(2,1)S(1)} %get-tuple-element.49, ...), dimensions={1} | concatenate | bytes 655360 | tf_op jit(solution)/shard_map/stack | solution.py:617
  115.2 84.2 %transport.1 = (bf16[4,2,40,5120]{3,2,1,0:T(8,128)(2,1)}, bf16[1600,256]{1,0:T(8,128)(2,1)}, bf16[1600,256]{1,0:T(8,128)(2,1)}) custom-call(s32[2]{0:T(128)} %add_convert_fusion.edge_ref, bf16[640,256]{1,0:T(8,128)(2,1)} %bitcast.94, bf16[256,256]{1,0:T(8,128)(2,1)} %constant.124.clone.perm_ref, bf16[2,512,512]{2,1,0:T(8,128)(2,1)} %constant.128.clone.order_ref, ...), custom_call_target="tpu_custom_call" | custom-call | flops 10066329600 | bytes 19660800 | tf_op jit(solution)/shard_map/transport/pallas_call | solution.py:489
  199.4 33.9 %all_to_all.20.coef_ref = bf16[8,5,40,256]{3,2,1,0:T(8,128)(2,1)} all-to-all(bf16[8,5,40,256]{3,2,1,0:T(8,128)(2,1)} %bitcast.86), channel_id=1, replica_groups=mesh['band'=4,'wave'=8] {'wave'}, dimensions={0} | all-to-all | bytes 1638400 | tf_op jit(solution)/shard_map/all_to_all | solution.py:648
  233.3 3.5 %all-to-all-start.3 = ((bf16[8,5,40,256]{3,2,1,0:T(8,128)(2,1)}), bf16[8,5,40,256]{3,2,1,0:T(8,128)(2,1)S(1)}, u32[]{:S(2)}, u32[]{:S(2)}) async-start(bf16[8,5,40,256]{3,2,1,0:T(8,128)(2,1)} %bitcast.85), calls=%async_computation.3 | async-start | bytes 1638400 | tf_op jit(solution)/shard_map/all_to_all | solution.py:648
  236.9 14.7 %legendre_backward.2 = bf16[320,1408]{1,0:T(8,128)(2,1)} custom-call(s32[80]{0:T(128)} %dynamic_slice.49.pair_ref, bf16[256,256]{1,0:T(8,128)(2,1)} %constant.124.clone.perm_ref, bf16[8,5,40,256]{3,2,1,0:T(8,128)(2,1)} %all_to_all.20.coef_ref, bf16[80,320,1408]{2,1,0:T(8,128)(2,1)} %leg_ref.7), custom_call_target="tpu_custom_call" | custom-call | flops 1153433600 | bytes 36044800 | tf_op jit(solution)/shard_map/legendre_backward/pallas_call | solution.py:156
  251.6 1.7 slice_bitcast_fusion.7
  253.6 2.5 collective-permute-start.5
  256.1 0.6 collective-permute-start.7
  256.7 0.9 collective-permute-start.6
  257.6 0.9 all-to-all-done.3.coef_ref
  258.5 0.9 copy-done.1
  259.4 14.7 %legendre_backward.3 = bf16[320,1408]{1,0:T(8,128)(2,1)} custom-call(s32[80]{0:T(128)} %dynamic_slice.49.pair_ref, bf16[256,256]{1,0:T(8,128)(2,1)} %constant.124.clone.perm_ref, bf16[8,5,40,256]{3,2,1,0:T(8,128)(2,1)} %copy-done.1, bf16[80,320,1408]{2,1,0:T(8,128)(2,1)} %leg_ref.7), custom_call_target="tpu_custom_call" | custom-call | flops 1153433600 | bytes 36044800 | tf_op jit(solution)/shard_map/legendre_backward/pallas_call | solution.py:156
  274.1 1.7 slice_bitcast_fusion.3
  276.1 2.5 collective-permute-start.8
  278.5 0.6 collective-permute-start.10
  279.1 1.0 collective-permute-start.9
  280.2 5.1 %collective-permute-done.8 = bf16[40,8,352]{2,1,0:T(8,128)(2,1)S(1)} collective-permute-done((bf16[40,8,352]{2,1,0:T(8,128)(2,1)S(1)}, bf16[40,8,352]{2,1,0:T(8,128)(2,1)S(1)}, u32[]{:S(2)}, u32[]{:S(2)}) %collective-permute-start.8) | collective-permute-done | bytes 225312 | tf_op jit(solution)/shard_map/ppermute | solution.py:538
  285.4 4.6 %collective-permute-done.10 = bf16[40,8,352]{2,1,0:T(8,128)(2,1)S(1)} collective-permute-done((bf16[40,8,352]{2,1,0:T(8,128)(2,1)S(1)}, bf16[40,8,352]{2,1,0:T(8,128)(2,1)S(1)}, u32[]{:S(2)}, u32[]{:S(2)}) %collective-permute-start.10) | collective-permute-done | bytes 225312 | tf_op jit(solution)/shard_map/ppermute | solution.py:538
  290.0 1.4 collective-permute-done.9
  291.5 0.9 pad_maximum_fusion.3
  (53 shorter events, 3.6 us)
Async XLA Ops:
  0.6 7.9 %copy-start = (f32[16,16]{1,0:T(8,128)S(1)}, f32[16,16]{1,0:T(8,128)}, u32[]{:S(2)}) copy-start(f32[16,16]{1,0:T(8,128)} %param.18) | copy-start | bytes 3076
  0.6 13.8 %copy-start.5 = (s32[4]{0:T(128)S(1)}, s32[4]{0:T(128)}, u32[]{:S(2)}) copy-start(s32[4]{0:T(128)} %constant.126.clone) | copy-start | bytes 52
  0.7 29.6 %collective-permute-start.1 = (bf16[80,8,352]{2,1,0:T(8,128)(2,1)}, bf16[80,8,352]{2,1,0:T(8,128)(2,1)S(1)}, u32[]{:S(2)}, u32[]{:S(2)}) collective-permute-start(bf16[80,8,352]{2,1,0:T(8,128)(2,1)} %bitcast.87), channel_id=1, source_target_pairs={{0,16},{8,24},{16,0},{24,8},{1,17},{9,25},{17,1},{25,9},{2,18},{10... | collective-permute-start | bytes 1351688 | tf_op jit(solution)/shard_map/ppermute | solution.py:538
  3.7 26.5 %collective-permute-start = (bf16[80,8,352]{2,1,0:T(8,128)(2,1)}, bf16[80,8,352]{2,1,0:T(8,128)(2,1)S(1)}, u32[]{:S(2)}, u32[]{:S(2)}) collective-permute-start(bf16[80,8,352]{2,1,0:T(8,128)(2,1)} %bitcast.88), channel_id=1, source_target_pairs={{0,8},{8,0},{16,24},{24,16},{1,9},{9,1},{17,25},{25,17},{2,10},{10... | collective-permute-start | bytes 1351688 | tf_op jit(solution)/shard_map/ppermute | solution.py:538
  5.2 25.1 %collective-permute-start.2 = (bf16[80,8,352]{2,1,0:T(8,128)(2,1)}, bf16[80,8,352]{2,1,0:T(8,128)(2,1)S(1)}, u32[]{:S(2)}, u32[]{:S(2)}) collective-permute-start(bf16[80,8,352]{2,1,0:T(8,128)(2,1)} %bitcast.89), channel_id=1, source_target_pairs={{0,24},{8,16},{16,8},{24,0},{1,25},{9,17},{17,9},{25,1},{2,26},{10... | collective-permute-start | bytes 1351688 | tf_op jit(solution)/shard_map/ppermute | solution.py:538
  18.2 12.1 %copy-start.4 = (bf16[80,352,8]{1,2,0:T(8,128)(2,1)S(1)}, bf16[80,352,8]{1,2,0:T(8,128)(2,1)}, u32[]{:S(2)}) copy-start(bf16[80,352,8]{1,2,0:T(8,128)(2,1)} %param.12) | copy-start | bytes 1351684
  52.2 27.0 %all-to-all-start = ((bf16[8,5,40,256]{3,2,1,0:T(8,128)(2,1)}), bf16[8,5,40,256]{3,2,1,0:T(8,128)(2,1)S(1)}, u32[]{:S(2)}, u32[]{:S(2)}) async-start(bf16[8,5,40,256]{3,2,1,0:T(8,128)(2,1)} %legendre_forward.3), calls=%async_computation | async-start | bytes 1638400 | tf_op jit(solution)/shard_map/all_to_all | solution.py:605
  79.2 32.9 %copy-start.2 = (bf16[8,5,40,256]{3,2,1,0:T(8,128)(2,1)}, bf16[8,5,40,256]{3,2,1,0:T(8,128)(2,1)S(1)}, u32[]{:S(2)}) copy-start(bf16[8,5,40,256]{3,2,1,0:T(8,128)(2,1)S(1)} %all-to-all-done) | copy-start | bytes 2457604
  79.2 25.2 %all-to-all-start.1 = ((bf16[8,5,40,256]{3,2,1,0:T(8,128)(2,1)}), bf16[8,5,40,256]{3,2,1,0:T(8,128)(2,1)S(1)}, u32[]{:S(2)}, u32[]{:S(2)}) async-start(bf16[8,5,40,256]{3,2,1,0:T(8,128)(2,1)} %legendre_forward.2), calls=%async_computation.1 | async-start | bytes 1638400 | tf_op jit(solution)/shard_map/all_to_all | solution.py:605
  104.3 10.9 %copy-start.3 = (bf16[8,5,40,256]{3,2,1,0:T(8,128)(2,1)}, bf16[8,5,40,256]{3,2,1,0:T(8,128)(2,1)S(1)}, u32[]{:S(2)}) copy-start(bf16[8,5,40,256]{3,2,1,0:T(8,128)(2,1)S(1)} %all-to-all-done.1) | copy-start | bytes 2457604
  105.6 4.2 %collective-permute-start.3 = (bf16[80,3,256]{2,1,0:T(4,128)(2,1)S(1)}, bf16[80,3,256]{2,1,0:T(4,128)(2,1)S(1)}, u32[]{:S(2)}, u32[]{:S(2)}) collective-permute-start(bf16[80,3,256]{2,1,0:T(4,128)(2,1)S(1)} %pad_maximum_fusion.5), channel_id=1, source_target_pairs={{0,1},{1,2},{2,3},{3,4},{4,5},{5,6},{6,7},{7,8},{8,9},{9,10},{10,1... | collective-permute-start | bytes 368648 | tf_op jit(solution)/shard_map/ppermute | solution.py:612
  108.3 3.3 %collective-permute-start.4 = (bf16[80,3,256]{2,1,0:T(4,128)(2,1)S(1)}, bf16[80,3,256]{2,1,0:T(4,128)(2,1)S(1)}, u32[]{:S(2)}, u32[]{:S(2)}) collective-permute-start(bf16[80,3,256]{2,1,0:T(4,128)(2,1)S(1)} %pad_maximum_fusion.4), channel_id=1, source_target_pairs={{1,0},{2,1},{3,2},{4,3},{5,4},{6,5},{7,6},{8,7},{9,8},{10,9},{11,1... | collective-permute-start | bytes 368648 | tf_op jit(solution)/shard_map/ppermute | solution.py:613
  233.3 25.2 %all-to-all-start.3 = ((bf16[8,5,40,256]{3,2,1,0:T(8,128)(2,1)}), bf16[8,5,40,256]{3,2,1,0:T(8,128)(2,1)S(1)}, u32[]{:S(2)}, u32[]{:S(2)}) async-start(bf16[8,5,40,256]{3,2,1,0:T(8,128)(2,1)} %bitcast.85), calls=%async_computation.3 | async-start | bytes 1638400 | tf_op jit(solution)/shard_map/all_to_all | solution.py:648
  253.6 25.5 %collective-permute-start.5 = (bf16[40,8,352]{2,1,0:T(8,128)(2,1)S(1)}, bf16[40,8,352]{2,1,0:T(8,128)(2,1)S(1)}, u32[]{:S(2)}, u32[]{:S(2)}) collective-permute-start(bf16[40,8,352]{2,1,0:T(8,128)(2,1)S(1)} %get-tuple-element.34), channel_id=1, source_target_pairs={{0,8},{8,0},{16,24},{24,16},{1,9},{9,1},{17,25},{25,17},{2,10},{10... | collective-permute-start | bytes 675848 | tf_op jit(solution)/shard_map/ppermute | solution.py:538
  256.1 24.0 %collective-permute-start.7 = (bf16[40,8,352]{2,1,0:T(8,128)(2,1)S(1)}, bf16[40,8,352]{2,1,0:T(8,128)(2,1)S(1)}, u32[]{:S(2)}, u32[]{:S(2)}) collective-permute-start(bf16[40,8,352]{2,1,0:T(8,128)(2,1)S(1)} %get-tuple-element.35), channel_id=1, source_target_pairs={{0,24},{8,16},{16,8},{24,0},{1,25},{9,17},{17,9},{25,1},{2,26},{10... | collective-permute-start | bytes 675848 | tf_op jit(solution)/shard_map/ppermute | solution.py:538
  256.7 23.4 %collective-permute-start.6 = (bf16[40,8,352]{2,1,0:T(8,128)(2,1)S(1)}, bf16[40,8,352]{2,1,0:T(8,128)(2,1)S(1)}, u32[]{:S(2)}, u32[]{:S(2)}) collective-permute-start(bf16[40,8,352]{2,1,0:T(8,128)(2,1)S(1)} %get-tuple-element.36), channel_id=1, source_target_pairs={{0,16},{8,24},{16,0},{24,8},{1,17},{9,25},{17,1},{25,9},{2,18},{10... | collective-permute-start | bytes 675848 | tf_op jit(solution)/shard_map/ppermute | solution.py:538
  258.5 0.9 copy-start.1
  276.1 9.3 %collective-permute-start.8 = (bf16[40,8,352]{2,1,0:T(8,128)(2,1)S(1)}, bf16[40,8,352]{2,1,0:T(8,128)(2,1)S(1)}, u32[]{:S(2)}, u32[]{:S(2)}) collective-permute-start(bf16[40,8,352]{2,1,0:T(8,128)(2,1)S(1)} %get-tuple-element.37), channel_id=1, source_target_pairs={{0,8},{8,0},{16,24},{24,16},{1,9},{9,1},{17,25},{25,17},{2,10},{10... | collective-permute-start | bytes 675848 | tf_op jit(solution)/shard_map/ppermute | solution.py:538
  278.5 11.4 %collective-permute-start.10 = (bf16[40,8,352]{2,1,0:T(8,128)(2,1)S(1)}, bf16[40,8,352]{2,1,0:T(8,128)(2,1)S(1)}, u32[]{:S(2)}, u32[]{:S(2)}) collective-permute-start(bf16[40,8,352]{2,1,0:T(8,128)(2,1)S(1)} %get-tuple-element.38), channel_id=1, source_target_pairs={{0,24},{8,16},{16,8},{24,0},{1,25},{9,17},{17,9},{25,1},{2,26},{10... | collective-permute-start | bytes 675848 | tf_op jit(solution)/shard_map/ppermute | solution.py:538
  279.1 12.2 %collective-permute-start.9 = (bf16[40,8,352]{2,1,0:T(8,128)(2,1)S(1)}, bf16[40,8,352]{2,1,0:T(8,128)(2,1)S(1)}, u32[]{:S(2)}, u32[]{:S(2)}) collective-permute-start(bf16[40,8,352]{2,1,0:T(8,128)(2,1)S(1)} %get-tuple-element.39), channel_id=1, source_target_pairs={{0,16},{8,24},{16,0},{24,8},{1,17},{9,25},{17,1},{25,9},{2,18},{10... | collective-permute-start | bytes 675848 | tf_op jit(solution)/shard_map/ppermute | solution.py:538

commit v6 on v3

--- a/solution.py
+++ b/solution.py
@@ -25,7 +25,7 @@
 CHUNK = 512
 FINE = CHUNK // 128
 CHUNKS = NLON // CHUNK
-STEP = 4
+STEP = 8
 F32 = jnp.float32
 BF16 = jnp.bfloat16
 VMEM_LIMIT = 60 * 2**20
@@ -76,7 +76,8 @@
         parts = [spec * even, south * even, spec * odd, south * odd]
         masked = jnp.concatenate(parts, axis=0).astype(BF16)
         pieces.append(dot_nt(leg_ref[u], masked))
-    acc_ref[step] = jnp.concatenate(pieces, axis=1)
+    for half in range(STEP // 4):
+        acc_ref[step * (STEP // 4) + half] = jnp.concatenate(pieces[4 * half : 4 * half + 4], axis=1)
 
     @pl.when(step == GROUP // STEP - 1)
     def _():
@@ -102,8 +103,8 @@
         grid=(groups, GROUP // STEP),
         in_specs=[
             pl.BlockSpec(memory_space=pltpu.SMEM),
-            pl.BlockSpec((STEP, COLS, rows), lambda g, t: (2 * (g + base) + t, 0, 0)),
-            pl.BlockSpec((STEP, lats, rows), lambda g, t: (2 * (g + base) + t, 0, 0)),
+            pl.BlockSpec((STEP, COLS, rows), lambda g, t: (GROUP // STEP * (g + base) + t, 0, 0)),
+            pl.BlockSpec((STEP, lats, rows), lambda g, t: (GROUP // STEP * (g + base) + t, 0, 0)),
         ],
         out_specs=pl.BlockSpec((waves, 1, height, WIDE), lambda g, t: (0, g, 0, 0)),
         scratch_shapes=[pltpu.VMEM((2, lats, 128), F32)],
@@ -160,9 +161,9 @@
             pl.BlockSpec(memory_space=pltpu.SMEM),
             pl.BlockSpec((WIDE, WIDE), lambda g, t: (0, 0)),
             pl.BlockSpec((waves, 1, height, WIDE), lambda g, t: (0, g, 0, 0)),
-            pl.BlockSpec((STEP, lats, rows), lambda g, t: (2 * (g + base) + t, 0, 0)),
+            pl.BlockSpec((STEP, lats, rows), lambda g, t: (GROUP // STEP * (g + base) + t, 0, 0)),
         ],
-        out_specs=pl.BlockSpec((STEP * COLS, rows), lambda g, t: (2 * g + t, 0)),
+        out_specs=pl.BlockSpec((STEP * COLS, rows), lambda g, t: (GROUP // STEP * g + t, 0)),
         scratch_shapes=[pltpu.VMEM((2, lats, 128), F32), pltpu.VMEM((WIDE, lats), BF16)],
         compiler_params=pltpu.CompilerParams(vmem_limit_bytes=VMEM_LIMIT),
         cost_estimate=pl.CostEstimate(
@@ -175,27 +176,32 @@
 
 
 def table_kernel(cos_ref, sin_ref, step_ref, out_ref):
+    batch = 4 * GROUP
+
     def rotate(c, s, step_c, step_s):
         return c * step_c - s * step_s, s * step_c + c * step_s
 
     def body(i, carry):
-        rows = pl.ds(pl.multiple_of(i * GROUP, GROUP), GROUP)
-        to = pl.ds(pl.multiple_of(i * 2 * GROUP, 2 * GROUP), 2 * GROUP)
+        rows = pl.ds(pl.multiple_of(i * batch, batch), batch)
         steps = step_ref[rows, :]
-        steps = [jnp.broadcast_to(steps[:, n : n + 1], (GROUP, 128)) for n in range(4)]
+        steps = [jnp.broadcast_to(steps[:, n : n + 1], (batch, 128)) for n in range(4)]
         first = cos_ref[rows, :], sin_ref[rows, :]
         for j in range(FINE):
             c, s = first
             for chunk in range(HALF // CHUNK):
                 at = chunk * CHUNK + j * 128
-                out_ref[to, at : at + 128] = jnp.concatenate([c, -s], axis=0).astype(BF16)
+                parts = []
+                for g in range(batch // GROUP):
+                    parts += [c[GROUP * g : GROUP * g + GROUP], -s[GROUP * g : GROUP * g + GROUP]]
+                to = pl.ds(pl.multiple_of(i * 2 * batch, 2 * batch), 2 * batch)
+                out_ref[to, at : at + 128] = jnp.concatenate(parts, axis=0).astype(BF16)
                 if chunk < HALF // CHUNK - 1:
                     c, s = rotate(c, s, *steps[2:])
             if j < FINE - 1:
                 first = rotate(*first, *steps[:2])
         return carry
 
-    lax.fori_loop(0, cos_ref.shape[0] // GROUP, body, 0)
+    lax.fori_loop(0, cos_ref.shape[0] // batch, body, 0)
 
 
 def angle_tables(slot_pair):
@@ -255,7 +261,7 @@
     recv_refs, arrival_ref, coef_refs = refs[:parts], refs[parts], refs[parts + 1 : 2 * parts + 1]
     (
         table_ref, depart_ref, pick_ref, left_ref, plus_ref, minus_ref, grid_ref, near_ref,
-        stage_ref, code_ref, moved_ref, pair_ref, sums_ref, sems,
+        stage_ref, code_ref, tap_ref, shift_ref, moved_ref, pair_ref, sums_ref, sems,
     ) = refs[2 * parts + 1 :]
     per_part = TILES // parts
     copies = [
@@ -369,31 +375,55 @@
         for j in range(FINE):
             code_ref[j] = code[:, 128 * j : 128 * j + 128]
 
+        def weigh(j, carry):
+            for k in range(RUN):
+                codes = [
+                    code_ref[j, pl.ds(h * RUN * SUB + k, SUB, stride=RUN), :] for h in range(2)
+                ]
+                codes = jnp.concatenate(codes, axis=0)
+                pick = (codes >> 4).astype(F32).astype(BF16)
+                one, zero = jnp.ones((16, 128), BF16), jnp.zeros((16, 128), BF16)
+                picked = [jnp.where(pick == jnp.asarray(t, BF16), one, zero) for t in range(NSTEN)]
+                found = jnp.dot(
+                    taps_ref[...], jnp.concatenate(picked, axis=0), preferred_element_type=F32
+                )
+                tap_ref[j, k] = found.astype(BF16)
+                shift_ref[j, k, 0] = ((codes >> 2) & 3).astype(F32).astype(BF16)
+                shift_ref[j, k, 1] = (codes & 3).astype(F32).astype(BF16)
+            return carry
+
+        lax.fori_loop(0, FINE, weigh, 0)
+
+        def choose(hits, values):
+            if len(values) == 4:
+                result, rest = values[3][1], values[:3]
+            else:
+                result, rest = jnp.zeros((16, 128), BF16), values
+            for d, value in rest:
+                result = jnp.where(hits[d], value, result)
+            return result
+
         def points(j, carry):
             at_lanes = pl.ds(pl.multiple_of(chunk * CHUNK + j * 128, 128), 128)
             for k in range(RUN):
-                index, column = [], []
-                for h in range(2):
-                    code = code_ref[j, pl.ds(h * RUN * SUB + k, SUB, stride=RUN), :]
-                    index.append(code >> 2)
-                    column.append(code & 3)
-                column = jnp.concatenate(column, axis=0).astype(F32).astype(BF16)
-                hits = [column == jnp.asarray(d, BF16) for d in range(4)]
+                row_step, column_step = shift_ref[j, k, 0], shift_ref[j, k, 1]
+                row_hits = [row_step == jnp.asarray(d, BF16) for d in range(4)]
+                hits = [column_step == jnp.asarray(d, BF16) for d in range(4)]
                 totals = [jnp.zeros((16, 128), F32) for _ in range(FIELDS)]
                 for r in range(7):
                     weights = []
                     for b in range(4):
-                        entry = taps_ref[r * 4 + b]
-                        found = [jnp.take_along_axis(entry, index[h], axis=1) for h in range(2)]
-                        weights.append(jnp.concatenate(found, axis=0).astype(BF16))
+                        values = []
+                        for d in range(4):
+                            a = r - d
+                            if 0 <= a < 4:
+                                at = (4 * a + b) * 16
+                                values.append((d, tap_ref[j, k, at : at + 16, :]))
+                        weights.append(choose(row_hits, values))
                     factors = []
-                    for c in range(-RIM, RIM + 1):
-                        factor = jnp.zeros((16, 128), BF16)
-                        for d in range(4):
-                            b = c - (d - 2) + 1
-                            if 0 <= b < 4:
-                                factor = jnp.where(hits[d], weights[b], factor)
-                        factors.append(factor)
+                    for c in range(7):
+                        values = [(d, weights[c - d]) for d in range(4) if 0 <= c - d < 4]
+                        factors.append(choose(hits, values))
                     for f in range(FIELDS):
                         row = f * REACH + k + r
                         part = None
@@ -497,6 +527,8 @@
             pltpu.VMEM((FIELDS * REACH, 16, CHUNK + 2 * RIM * 128), BF16),
             pltpu.VMEM((FINE, FIELDS * 2, lats, 128), F32),
             pltpu.VMEM((FINE, 2 * lats, 128), jnp.int32),
+            pltpu.VMEM((FINE, RUN, WIDE, 128), BF16),
+            pltpu.VMEM((FINE, RUN, 2, 16, 128), BF16),
             pltpu.VMEM((own, NLON), BF16),
             pltpu.VMEM((2, own, HALF), BF16),
             pltpu.VMEM((2, TILES, own, 128), F32),
@@ -513,16 +545,9 @@
 
 
 def tap_tables(stencil_weight):
-    choose = np.zeros((16, 7, 4, 4), np.float32)
-    for r in range(7):
-        for d in range(4):
-            a = (r - 3) - (d - 2) + 1
-            if 0 <= a < 4:
-                for b in range(4):
-                    choose[4 * a + b, r, b, d] = 1.0
-    table = jnp.einsum("tw,wnd->ntd", stencil_weight, choose.reshape(16, 28, 4), precision="highest")
-    table = jnp.pad(table.reshape(28, 4 * NSTEN), ((0, 0), (0, 128 - 4 * NSTEN)))
-    return jnp.broadcast_to(table[:, None, :], (28, 8, 128))
+    same = jnp.eye(16, dtype=F32)
+    table = stencil_weight.T[:, None, :, None] * same[None, :, None, :]
+    return table.reshape(16 * 16, NSTEN * 16).astype(BF16)
 
 
 def exchange(array, axis, distance):

time: 290 us -> 312 us (1.076)
  Pallas kernels: 159 us -> 175 us
  waiting for transfers between devices: 35.4 us -> 38.7 us
    pallas_call x1, Pallas kernels: 68.2 us -> 101 us  [transport(): pl.pallas_call(functools.partial(middle_kernel, sub, parts), out_shape=(j...]
    pallas_call x1, Pallas kernels: 18.4 us -> 11.4 us  [angle_tables(): pl.pallas_call(table_kernel, out_shape=jax.ShapeDtypeStruct((2 * count, H...]
    pallas_call x2, Pallas kernels: 34.4 us -> 29.4 us  [legendre_backward(): pl.pallas_call(functools.partial(backward_kernel, height, base), out_shap...]
    pallas_call x2, Pallas kernels: 38.1 us -> 33.4 us  [legendre_forward(): pl.pallas_call(functools.partial(forward_kernel, height, base), out_shape...]
  transfers between devices with their start and end apart: 14 -> 14, of which waited for: 6 -> 7; matrix products, arithmetic and copies ran while one was open for 7% -> 7% of each run, Pallas kernels for 25% -> 19%
where the time goes in v6:
time: 312 us; the launch traced here: 310 us
  Pallas kernels  175 us (56%)
  waiting for transfers between devices  38.7 us (12%)
  blocking collectives  33.9 us (11%)
  starting transfers between devices  28 us (9%)
  local copies, waits for them, and re-layouts  21.1 us (7%)
  other arithmetic  12.2 us (4%)
    pallas_call x1, Pallas kernels, transport(): pl.pallas_call(functools.partial(middle_kernel, sub, parts), out_shape=(j...  101 us
    all_to_all x1, blocking collectives, per_device(): lax.all_to_all(leaving, 'wave', split_axis=0, concat_axis=0, tiled=True)  33.9 us
    pallas_call x2, Pallas kernels, legendre_forward(): pl.pallas_call(functools.partial(forward_kernel, height, base), out_shape...  33.4 us
    pallas_call x2, Pallas kernels, legendre_backward(): pl.pallas_call(functools.partial(backward_kernel, height, base), out_shap...  29.4 us
    all_to_all x2, waiting for transfers between devices, per_device(): lax.all_to_all(sent, 'wave', split_axis=0, concat_axis=0, tiled=True)  25.4 us
    ppermute x9, starting transfers between devices, exchange(): lax.ppermute(array, axis, [(i, i ^ distance) for i in range(devices)])  12.6 us
    pallas_call x1, Pallas kernels, angle_tables(): pl.pallas_call(table_kernel, out_shape=jax.ShapeDtypeStruct((2 * count, H...  11.4 us
    ppermute x9, waiting for transfers between devices, exchange(): lax.ppermute(array, axis, [(i, i ^ distance) for i in range(devices)])  11.1 us
  transfers between devices with their start and end apart: 14, of which 7 were waited for; matrix products, arithmetic and copies ran while one was open for 7% of the time, Pallas kernels for 19%

profile of v6, /device:TPU:0, one launch (start us, length us, event | category | flops | bytes accessed | tf_op | source)
XLA Modules:
  0.0 310.1 jit_solution(9924215807173857992)
XLA Ops:
  0.6 3.0 collective-permute-start.1
  3.7 1.5 collective-permute-start
  5.2 0.8 reshape.156
  6.2 1.3 dynamic_slice.49.pair_ref
  7.5 0.8 dynamic_slice.48
  8.4 0.8 copy.35
  10.2 1.7 convert_element_type.62.taps_ref
  11.8 4.2 %sine_multiply_fusion = (f32[1280,128]{1,0:T(8,128)}, f32[1280,128]{1,0:T(8,128)}) fusion(s32[128]{0:T(128)S(1)} %iota_multiply_fusion, s32[1280]{0:T(1024)S(1)} %pad_add_fusion, f32[1280]{0:T(1024)S(1)} %compare_select_fusion), kind=kLoop, calls=%fused_computation.14 | loop fusion | flops 1802240 | bytes 1321472 | tf_op jit(solution)/shard_map/mul | solution.py:220
  16.0 3.8 %sine_select_fusion.step_ref = f32[1280,4]{1,0:T(8,128)} fusion(s32[1280]{0:T(1024)S(1)} %pad_add_fusion, s32[4]{0:T(128)S(1)} %copy-done.4, pred[4]{0:T(512)(128)(4,1)S(1)} %fusion.29), kind=kLoop, calls=%fused_computation.10 | loop fusion | flops 51200 | bytes 25620 | tf_op jit(solution)/shard_map/jit(_where)/select_n | solution.py:222
  19.7 11.4 %angle_tables.1 = bf16[2560,2560]{1,0:T(8,128)(2,1)} custom-call(f32[1280,128]{1,0:T(8,128)} %get-tuple-element.57.cos_ref, f32[1280,128]{1,0:T(8,128)} %get-tuple-element.56.sin_ref, f32[1280,4]{1,0:T(8,128)} %sine_select_fusion.step_ref), custom_call_target="tpu_custom_call" | custom-call | flops 19660800 | bytes 13107200 | tf_op jit(solution)/shard_map/angle_tables/pallas_call | solution.py:224
  31.1 0.7 add_convert_fusion.edge_ref
  32.5 2.5 concatenate.25.spec_ref
  35.0 0.6 broadcast_in_dim.53.scale_ref
  35.6 0.8 broadcast_in_dim.56.weight_ref
  36.4 16.7 %legendre_forward.3 = bf16[8,5,40,256]{3,2,1,0:T(8,128)(2,1)} custom-call(s32[80]{0:T(128)} %dynamic_slice.49.pair_ref, bf16[80,8,1408]{2,1,0:T(8,128)(2,1)} %concatenate.25.spec_ref, bf16[80,320,1408]{2,1,0:T(8,128)(2,1)} %leg_ref.7), custom_call_target="tpu_custom_call" | custom-call | flops 1153433600 | bytes 36044800 | tf_op jit(solution)/shard_map/legendre_forward/pallas_call | solution.py:100
  53.1 5.3 %all-to-all-start = ((bf16[8,5,40,256]{3,2,1,0:T(8,128)(2,1)}), bf16[8,5,40,256]{3,2,1,0:T(8,128)(2,1)S(1)}, u32[]{:S(2)}, u32[]{:S(2)}) async-start(bf16[8,5,40,256]{3,2,1,0:T(8,128)(2,1)} %legendre_forward.3), calls=%async_computation | async-start | bytes 1638400 | tf_op jit(solution)/shard_map/all_to_all | solution.py:622
  58.4 16.7 %legendre_forward.2 = bf16[8,5,40,256]{3,2,1,0:T(8,128)(2,1)} custom-call(s32[80]{0:T(128)} %dynamic_slice.49.pair_ref, bf16[80,8,1408]{2,1,0:T(8,128)(2,1)} %concatenate.25.spec_ref, bf16[80,320,1408]{2,1,0:T(8,128)(2,1)} %leg_ref.7), custom_call_target="tpu_custom_call" | custom-call | flops 1153433600 | bytes 36044800 | tf_op jit(solution)/shard_map/legendre_forward/pallas_call | solution.py:100
  75.1 5.0 %all-to-all-done = bf16[8,5,40,256]{3,2,1,0:T(8,128)(2,1)S(1)} async-done(((bf16[8,5,40,256]{3,2,1,0:T(8,128)(2,1)}), bf16[8,5,40,256]{3,2,1,0:T(8,128)(2,1)S(1)}, u32[]{:S(2)}, u32[]{:S(2)}) %all-to-all-start) | async-done | bytes 819232 | tf_op jit(solution)/shard_map/all_to_all | solution.py:622
  80.1 3.5 %all-to-all-start.1 = ((bf16[8,5,40,256]{3,2,1,0:T(8,128)(2,1)}), bf16[8,5,40,256]{3,2,1,0:T(8,128)(2,1)S(1)}, u32[]{:S(2)}, u32[]{:S(2)}) async-start(bf16[8,5,40,256]{3,2,1,0:T(8,128)(2,1)} %legendre_forward.2), calls=%async_computation.1 | async-start | bytes 1638400 | tf_op jit(solution)/shard_map/all_to_all | solution.py:622
  83.6 1.2 slice.75
  84.8 20.4 %all-to-all-done.1 = bf16[8,5,40,256]{3,2,1,0:T(8,128)(2,1)S(1)} async-done(((bf16[8,5,40,256]{3,2,1,0:T(8,128)(2,1)}), bf16[8,5,40,256]{3,2,1,0:T(8,128)(2,1)S(1)}, u32[]{:S(2)}, u32[]{:S(2)}) %all-to-all-start.1) | async-done | bytes 819232 | tf_op jit(solution)/shard_map/all_to_all | solution.py:622
  105.2 1.1 slice.76
  106.5 1.6 collective-permute-start.3
  108.0 0.5 slice.72
  108.6 0.5 slice.73
  109.2 1.5 collective-permute-start.4
  110.7 0.5 broadcast_select_fusion.3
  111.2 1.3 collective-permute-done.4
  113.1 3.1 stack.75
  116.1 101.0 %transport.1 = (bf16[4,2,40,5120]{3,2,1,0:T(8,128)(2,1)}, bf16[1600,256]{1,0:T(8,128)(2,1)}, bf16[1600,256]{1,0:T(8,128)(2,1)}) custom-call(s32[2]{0:T(128)} %add_convert_fusion.edge_ref, bf16[640,256]{1,0:T(8,128)(2,1)} %bitcast.90, bf16[256,256]{1,0:T(8,128)(2,1)} %constant.120.clone.perm_ref, bf16[2,512,512]{2,1,0:T(8,128)(2,1)} %constant.123.clone.order_ref, ...), custom_call_target="tpu_custom_call" | custom-call | flops 10066329600 | bytes 19660800 | tf_op jit(solution)/shard_map/transport/pallas_call | solution.py:511
  217.2 33.9 %all_to_all.20.coef_ref = bf16[8,5,40,256]{3,2,1,0:T(8,128)(2,1)} all-to-all(bf16[8,5,40,256]{3,2,1,0:T(8,128)(2,1)} %bitcast.82), channel_id=1, replica_groups=mesh['band'=4,'wave'=8] {'wave'}, dimensions={0} | all-to-all | bytes 1638400 | tf_op jit(solution)/shard_map/all_to_all | solution.py:665
  251.1 3.5 %all-to-all-start.3 = ((bf16[8,5,40,256]{3,2,1,0:T(8,128)(2,1)}), bf16[8,5,40,256]{3,2,1,0:T(8,128)(2,1)S(1)}, u32[]{:S(2)}, u32[]{:S(2)}) async-start(bf16[8,5,40,256]{3,2,1,0:T(8,128)(2,1)} %bitcast.81), calls=%async_computation.3 | async-start | bytes 1638400 | tf_op jit(solution)/shard_map/all_to_all | solution.py:665
  254.7 14.7 %legendre_backward.2 = bf16[320,1408]{1,0:T(8,128)(2,1)} custom-call(s32[80]{0:T(128)} %dynamic_slice.49.pair_ref, bf16[256,256]{1,0:T(8,128)(2,1)} %constant.120.clone.perm_ref, bf16[8,5,40,256]{3,2,1,0:T(8,128)(2,1)} %all_to_all.20.coef_ref, bf16[80,320,1408]{2,1,0:T(8,128)(2,1)} %leg_ref.7), custom_call_target="tpu_custom_call" | custom-call | flops 1153433600 | bytes 36044800 | tf_op jit(solution)/shard_map/legendre_backward/pallas_call | solution.py:156
  269.4 1.7 slice_bitcast_fusion.7
  271.4 2.5 collective-permute-start.5
  273.9 0.6 collective-permute-start.7
  274.4 1.0 collective-permute-start.6
  275.4 0.9 all-to-all-done.3.coef_ref
  276.3 0.9 copy-done
  277.2 14.7 %legendre_backward.3 = bf16[320,1408]{1,0:T(8,128)(2,1)} custom-call(s32[80]{0:T(128)} %dynamic_slice.49.pair_ref, bf16[256,256]{1,0:T(8,128)(2,1)} %constant.120.clone.perm_ref, bf16[8,5,40,256]{3,2,1,0:T(8,128)(2,1)} %copy-done, bf16[80,320,1408]{2,1,0:T(8,128)(2,1)} %leg_ref.7), custom_call_target="tpu_custom_call" | custom-call | flops 1153433600 | bytes 36044800 | tf_op jit(solution)/shard_map/legendre_backward/pallas_call | solution.py:156
  291.9 1.7 slice_bitcast_fusion.3
  293.9 2.5 collective-permute-start.8
  296.3 0.6 collective-permute-start.10
  296.9 1.0 collective-permute-start.9
  298.0 5.1 %collective-permute-done.8 = bf16[40,8,352]{2,1,0:T(8,128)(2,1)S(1)} collective-permute-done((bf16[40,8,352]{2,1,0:T(8,128)(2,1)S(1)}, bf16[40,8,352]{2,1,0:T(8,128)(2,1)S(1)}, u32[]{:S(2)}, u32[]{:S(2)}) %collective-permute-start.8) | collective-permute-done | bytes 225312 | tf_op jit(solution)/shard_map/ppermute | solution.py:555
  303.1 4.6 %collective-permute-done.10 = bf16[40,8,352]{2,1,0:T(8,128)(2,1)S(1)} collective-permute-done((bf16[40,8,352]{2,1,0:T(8,128)(2,1)S(1)}, bf16[40,8,352]{2,1,0:T(8,128)(2,1)S(1)}, u32[]{:S(2)}, u32[]{:S(2)}) %collective-permute-start.10) | collective-permute-done | bytes 225312 | tf_op jit(solution)/shard_map/ppermute | solution.py:555
  307.7 1.4 collective-permute-done.9
  309.2 0.9 pad_maximum_fusion.3
  (50 shorter events, 3.7 us)
Async XLA Ops:
  0.6 31.2 %collective-permute-start.1 = (bf16[80,8,352]{2,1,0:T(8,128)(2,1)}, bf16[80,8,352]{2,1,0:T(8,128)(2,1)S(1)}, u32[]{:S(2)}, u32[]{:S(2)}) collective-permute-start(bf16[80,8,352]{2,1,0:T(8,128)(2,1)} %bitcast.83), channel_id=1, source_target_pairs={{0,16},{8,24},{16,0},{24,8},{1,17},{9,25},{17,1},{25,9},{2,18},{10... | collective-permute-start | bytes 1351688 | tf_op jit(solution)/shard_map/ppermute | solution.py:555
  3.7 28.1 %collective-permute-start = (bf16[80,8,352]{2,1,0:T(8,128)(2,1)}, bf16[80,8,352]{2,1,0:T(8,128)(2,1)S(1)}, u32[]{:S(2)}, u32[]{:S(2)}) collective-permute-start(bf16[80,8,352]{2,1,0:T(8,128)(2,1)} %bitcast.84), channel_id=1, source_target_pairs={{0,8},{8,0},{16,24},{24,16},{1,9},{9,1},{17,25},{25,17},{2,10},{10... | collective-permute-start | bytes 1351688 | tf_op jit(solution)/shard_map/ppermute | solution.py:555
  5.2 26.7 %collective-permute-start.2 = (bf16[80,8,352]{2,1,0:T(8,128)(2,1)}, bf16[80,8,352]{2,1,0:T(8,128)(2,1)S(1)}, u32[]{:S(2)}, u32[]{:S(2)}) collective-permute-start(bf16[80,8,352]{2,1,0:T(8,128)(2,1)} %bitcast.85), channel_id=1, source_target_pairs={{0,24},{8,16},{16,8},{24,0},{1,25},{9,17},{17,9},{25,1},{2,26},{10... | collective-permute-start | bytes 1351688 | tf_op jit(solution)/shard_map/ppermute | solution.py:555
  9.6 6.4 %copy-start.4 = (s32[4]{0:T(128)S(1)}, s32[4]{0:T(128)}, u32[]{:S(2)}) copy-start(s32[4]{0:T(128)} %constant.122.clone) | copy-start | bytes 52
  19.7 12.1 %copy-start.3 = (bf16[80,352,8]{1,2,0:T(8,128)(2,1)S(1)}, bf16[80,352,8]{1,2,0:T(8,128)(2,1)}, u32[]{:S(2)}) copy-start(bf16[80,352,8]{1,2,0:T(8,128)(2,1)} %param.11) | copy-start | bytes 1351684
  53.1 27.0 %all-to-all-start = ((bf16[8,5,40,256]{3,2,1,0:T(8,128)(2,1)}), bf16[8,5,40,256]{3,2,1,0:T(8,128)(2,1)S(1)}, u32[]{:S(2)}, u32[]{:S(2)}) async-start(bf16[8,5,40,256]{3,2,1,0:T(8,128)(2,1)} %legendre_forward.3), calls=%async_computation | async-start | bytes 1638400 | tf_op jit(solution)/shard_map/all_to_all | solution.py:622
  80.1 32.9 %copy-start.1 = (bf16[8,5,40,256]{3,2,1,0:T(8,128)(2,1)}, bf16[8,5,40,256]{3,2,1,0:T(8,128)(2,1)S(1)}, u32[]{:S(2)}) copy-start(bf16[8,5,40,256]{3,2,1,0:T(8,128)(2,1)S(1)} %all-to-all-done) | copy-start | bytes 2457604
  80.1 25.2 %all-to-all-start.1 = ((bf16[8,5,40,256]{3,2,1,0:T(8,128)(2,1)}), bf16[8,5,40,256]{3,2,1,0:T(8,128)(2,1)S(1)}, u32[]{:S(2)}, u32[]{:S(2)}) async-start(bf16[8,5,40,256]{3,2,1,0:T(8,128)(2,1)} %legendre_forward.2), calls=%async_computation.1 | async-start | bytes 1638400 | tf_op jit(solution)/shard_map/all_to_all | solution.py:622
  105.2 10.9 %copy-start.2 = (bf16[8,5,40,256]{3,2,1,0:T(8,128)(2,1)}, bf16[8,5,40,256]{3,2,1,0:T(8,128)(2,1)S(1)}, u32[]{:S(2)}) copy-start(bf16[8,5,40,256]{3,2,1,0:T(8,128)(2,1)S(1)} %all-to-all-done.1) | copy-start | bytes 2457604
  106.5 4.2 %collective-permute-start.3 = (bf16[80,3,256]{2,1,0:T(4,128)(2,1)S(1)}, bf16[80,3,256]{2,1,0:T(4,128)(2,1)S(1)}, u32[]{:S(2)}, u32[]{:S(2)}) collective-permute-start(bf16[80,3,256]{2,1,0:T(4,128)(2,1)S(1)} %pad_maximum_fusion.5), channel_id=1, source_target_pairs={{0,1},{1,2},{2,3},{3,4},{4,5},{5,6},{6,7},{7,8},{8,9},{9,10},{10,1... | collective-permute-start | bytes 368648 | tf_op jit(solution)/shard_map/ppermute | solution.py:629
  109.2 3.3 %collective-permute-start.4 = (bf16[80,3,256]{2,1,0:T(4,128)(2,1)S(1)}, bf16[80,3,256]{2,1,0:T(4,128)(2,1)S(1)}, u32[]{:S(2)}, u32[]{:S(2)}) collective-permute-start(bf16[80,3,256]{2,1,0:T(4,128)(2,1)S(1)} %pad_maximum_fusion.4), channel_id=1, source_target_pairs={{1,0},{2,1},{3,2},{4,3},{5,4},{6,5},{7,6},{8,7},{9,8},{10,9},{11,1... | collective-permute-start | bytes 368648 | tf_op jit(solution)/shard_map/ppermute | solution.py:630
  251.1 25.2 %all-to-all-start.3 = ((bf16[8,5,40,256]{3,2,1,0:T(8,128)(2,1)}), bf16[8,5,40,256]{3,2,1,0:T(8,128)(2,1)S(1)}, u32[]{:S(2)}, u32[]{:S(2)}) async-start(bf16[8,5,40,256]{3,2,1,0:T(8,128)(2,1)} %bitcast.81), calls=%async_computation.3 | async-start | bytes 1638400 | tf_op jit(solution)/shard_map/all_to_all | solution.py:665
  271.4 25.5 %collective-permute-start.5 = (bf16[40,8,352]{2,1,0:T(8,128)(2,1)S(1)}, bf16[40,8,352]{2,1,0:T(8,128)(2,1)S(1)}, u32[]{:S(2)}, u32[]{:S(2)}) collective-permute-start(bf16[40,8,352]{2,1,0:T(8,128)(2,1)S(1)} %get-tuple-element.34), channel_id=1, source_target_pairs={{0,8},{8,0},{16,24},{24,16},{1,9},{9,1},{17,25},{25,17},{2,10},{10... | collective-permute-start | bytes 675848 | tf_op jit(solution)/shard_map/ppermute | solution.py:555
  273.9 24.0 %collective-permute-start.7 = (bf16[40,8,352]{2,1,0:T(8,128)(2,1)S(1)}, bf16[40,8,352]{2,1,0:T(8,128)(2,1)S(1)}, u32[]{:S(2)}, u32[]{:S(2)}) collective-permute-start(bf16[40,8,352]{2,1,0:T(8,128)(2,1)S(1)} %get-tuple-element.35), channel_id=1, source_target_pairs={{0,24},{8,16},{16,8},{24,0},{1,25},{9,17},{17,9},{25,1},{2,26},{10... | collective-permute-start | bytes 675848 | tf_op jit(solution)/shard_map/ppermute | solution.py:555
  274.4 23.5 %collective-permute-start.6 = (bf16[40,8,352]{2,1,0:T(8,128)(2,1)S(1)}, bf16[40,8,352]{2,1,0:T(8,128)(2,1)S(1)}, u32[]{:S(2)}, u32[]{:S(2)}) collective-permute-start(bf16[40,8,352]{2,1,0:T(8,128)(2,1)S(1)} %get-tuple-element.36), channel_id=1, source_target_pairs={{0,16},{8,24},{16,0},{24,8},{1,17},{9,25},{17,1},{25,9},{2,18},{10... | collective-permute-start | bytes 675848 | tf_op jit(solution)/shard_map/ppermute | solution.py:555
  276.3 0.9 copy-start
  293.9 9.3 %collective-permute-start.8 = (bf16[40,8,352]{2,1,0:T(8,128)(2,1)S(1)}, bf16[40,8,352]{2,1,0:T(8,128)(2,1)S(1)}, u32[]{:S(2)}, u32[]{:S(2)}) collective-permute-start(bf16[40,8,352]{2,1,0:T(8,128)(2,1)S(1)} %get-tuple-element.37), channel_id=1, source_target_pairs={{0,8},{8,0},{16,24},{24,16},{1,9},{9,1},{17,25},{25,17},{2,10},{10... | collective-permute-start | bytes 675848 | tf_op jit(solution)/shard_map/ppermute | solution.py:555
  296.3 11.4 %collective-permute-start.10 = (bf16[40,8,352]{2,1,0:T(8,128)(2,1)S(1)}, bf16[40,8,352]{2,1,0:T(8,128)(2,1)S(1)}, u32[]{:S(2)}, u32[]{:S(2)}) collective-permute-start(bf16[40,8,352]{2,1,0:T(8,128)(2,1)S(1)} %get-tuple-element.38), channel_id=1, source_target_pairs={{0,24},{8,16},{16,8},{24,0},{1,25},{9,17},{17,9},{25,1},{2,26},{10... | collective-permute-start | bytes 675848 | tf_op jit(solution)/shard_map/ppermute | solution.py:555
  296.9 12.2 %collective-permute-start.9 = (bf16[40,8,352]{2,1,0:T(8,128)(2,1)S(1)}, bf16[40,8,352]{2,1,0:T(8,128)(2,1)S(1)}, u32[]{:S(2)}, u32[]{:S(2)}) collective-permute-start(bf16[40,8,352]{2,1,0:T(8,128)(2,1)S(1)} %get-tuple-element.39), channel_id=1, source_target_pairs={{0,16},{8,24},{16,0},{24,8},{1,17},{9,25},{17,1},{25,9},{2,18},{10... | collective-permute-start | bytes 675848 | tf_op jit(solution)/shard_map/ppermute | solution.py:555

commit v7 on v5

--- a/solution.py
+++ b/solution.py
@@ -319,7 +319,7 @@
             for f in range(FIELDS):
                 for k in range(RUN):
                     at = (f * RUN + k) * 16
-                    grid_ref[f * REACH + RIM + k, :, to] = ref[at : at + 16, :]
+                    grid_ref[f * REACH + RIM + k, :, to] = ref[at : at + 16, :].astype(BF16)
                 for k in range(RIM):
                     before, after = [], []
                     for h in range(2):
@@ -333,8 +333,10 @@
                         after.append(
                             jnp.where(place == sub - 1, ref[end + k : end + k + 1, :], rolled)
                         )
-                    grid_ref[f * REACH + k, :, to] = jnp.concatenate(before, 0)
-                    grid_ref[f * REACH + RIM + RUN + k, :, to] = jnp.concatenate(after, 0)
+                    grid_ref[f * REACH + k, :, to] = jnp.concatenate(before, 0).astype(BF16)
+                    grid_ref[f * REACH + RIM + RUN + k, :, to] = jnp.concatenate(after, 0).astype(
+                        BF16
+                    )
         return carry
 
     lax.fori_loop(0, HALF // 256, to_grid, 0)
@@ -351,16 +353,19 @@
             for j in range(FINE):
                 here = grid_ref[row, :, pl.ds(pl.multiple_of(chunk * CHUNK + j * 128, 128), 128)]
                 near_ref[row, :, (RIM + j) * 128 : (RIM + j + 1) * 128] = here
+                here = here.astype(F32)
                 if j >= FINE - RIM:
                     at = pl.ds(pl.multiple_of(previous * CHUNK + j * 128, 128), 128)
-                    mixed = pltpu.roll(jnp.where(lane == 127, grid_ref[row, :, at], here), 1, 1)
-                    to = (j - (FINE - RIM)) * 128
-                    near_ref[row, :, to : to + 128] = mixed
+                    there = grid_ref[row, :, at].astype(F32)
+                    mixed = pltpu.roll(jnp.where(lane == 127, there, here), 1, 1)
+                    slot = j - (FINE - RIM)
+                    near_ref[row, :, slot * 128 : slot * 128 + 128] = mixed.astype(BF16)
                 if j < RIM:
                     at = pl.ds(pl.multiple_of(following * CHUNK + j * 128, 128), 128)
-                    mixed = pltpu.roll(jnp.where(lane == 0, grid_ref[row, :, at], here), 127, 1)
-                    to = (RIM + FINE + j) * 128
-                    near_ref[row, :, to : to + 128] = mixed
+                    there = grid_ref[row, :, at].astype(F32)
+                    mixed = pltpu.roll(jnp.where(lane == 0, there, here), 127, 1)
+                    slot = RIM + FINE + j
+                    near_ref[row, :, slot * 128 : slot * 128 + 128] = mixed.astype(BF16)
             return carry
 
         lax.fori_loop(0, FIELDS * REACH, neighbours, 0, unroll=4)
@@ -379,8 +384,9 @@
                         code_ref[j, pl.ds(h * RUN * SUB + k, SUB, stride=RUN), :] for h in range(2)
                     ]
                     index[k] = [code >> 2 for code in codes]
-                    column = jnp.concatenate(codes, axis=0) & 3
-                    hits[k] = [column == d for d in range(4)]
+                    column = jnp.concatenate([code & 3 for code in codes], axis=0)
+                    column = column.astype(F32).astype(BF16)
+                    hits[k] = [column == jnp.asarray(d, BF16) for d in range(4)]
                 totals = {}
                 for row in range(ks[0], ks[-1] + 7):
                     factors = {}
@@ -392,22 +398,28 @@
                         for b in range(4):
                             entry = taps_ref[r * 4 + b]
                             found = [jnp.take_along_axis(entry, index[k][h], axis=1) for h in range(2)]
-                            weights.append(jnp.concatenate(found, axis=0))
+                            weights.append(jnp.concatenate(found, axis=0).astype(BF16))
                         factors[k] = []
-                        for c in range(-RIM, RIM + 1):
-                            factor = jnp.zeros((16, 128), F32)
-                            for d in range(4):
-                                b = c - (d - 2) + 1
-                                if 0 <= b < 4:
-                                    factor = jnp.where(hits[k][d], weights[b], factor)
+                        for c in range(7):
+                            values = [(d, weights[c - d]) for d in range(4) if 0 <= c - d < 4]
+                            if len(values) == 4:
+                                factor, values = values[3][1], values[:3]
+                            else:
+                                factor = jnp.zeros((16, 128), BF16)
+                            for d, value in values:
+                                factor = jnp.where(hits[k][d], value, factor)
                             factors[k].append(factor)
                     for f in range(FIELDS):
+                        part = {}
                         for c in range(7):
                             lanes_c = pl.ds(pl.multiple_of((j + c) * 128, 128), 128)
                             near = near_ref[f * REACH + row, :, lanes_c]
                             for k in factors:
                                 term = factors[k][c] * near
-                                totals[f, k] = totals[f, k] + term if (f, k) in totals else term
+                                part[k] = part[k] + term if k in part else term
+                        for k in part:
+                            wide = part[k].astype(F32)
+                            totals[f, k] = totals[f, k] + wide if (f, k) in totals else wide
                 for f in range(FIELDS):
                     for k in ks:
                         at = (f * RUN + k) * 16
@@ -501,8 +513,8 @@
             pltpu.VMEM((2, left, slots2), BF16),
             pltpu.VMEM((left, 256), F32),
             pltpu.VMEM((left, 256), F32),
-            pltpu.VMEM((FIELDS * REACH, 16, NLON), F32),
-            pltpu.VMEM((FIELDS * REACH, 16, CHUNK + 2 * RIM * 128), F32),
+            pltpu.VMEM((FIELDS * REACH, 16, NLON), BF16),
+            pltpu.VMEM((FIELDS * REACH, 16, CHUNK + 2 * RIM * 128), BF16),
             pltpu.VMEM((FINE, FIELDS * 2, lats, 128), F32),
             pltpu.VMEM((FINE, 2 * lats, 128), jnp.int32),
             pltpu.VMEM((own, NLON), BF16),

time: 294 us -> 278 us (0.946)
  Pallas kernels: 158 us -> 143 us
    pallas_call x1, Pallas kernels: 84.2 us -> 68.6 us  [transport(): pl.pallas_call(functools.partial(middle_kernel, sub, parts), out_shape=(j...]
  transfers between devices with their start and end apart: 14 -> 14, of which waited for: 7 -> 7; matrix products, arithmetic and copies ran while one was open for 7% -> 7% of each run, Pallas kernels for 20% -> 21%
where the time goes in v7:
time: 278 us; the launch traced here: 277 us
  Pallas kernels  143 us (51%)
  waiting for transfers between devices  38.7 us (14%)
  blocking collectives  33.9 us (12%)
  starting transfers between devices  28 us (10%)
  local copies, waits for them, and re-layouts  19.5 us (7%)
  other arithmetic  12 us (4%)
    pallas_call x1, Pallas kernels, transport(): pl.pallas_call(functools.partial(middle_kernel, sub, parts), out_shape=(j...  68.6 us
    all_to_all x1, blocking collectives, per_device(): lax.all_to_all(leaving, 'wave', split_axis=0, concat_axis=0, tiled=True)  33.9 us
    pallas_call x2, Pallas kernels, legendre_forward(): pl.pallas_call(functools.partial(forward_kernel, height, base), out_shape...  33.4 us
    pallas_call x2, Pallas kernels, legendre_backward(): pl.pallas_call(functools.partial(backward_kernel, height, base), out_shap...  29.4 us
    all_to_all x2, waiting for transfers between devices, per_device(): lax.all_to_all(sent, 'wave', split_axis=0, concat_axis=0, tiled=True)  25.4 us
    ppermute x9, starting transfers between devices, exchange(): lax.ppermute(array, axis, [(i, i ^ distance) for i in range(devices)])  12.6 us
    pallas_call x1, Pallas kernels, angle_tables(): pl.pallas_call(table_kernel, out_shape=jax.ShapeDtypeStruct((2 * count, H...  11.4 us
    ppermute x9, waiting for transfers between devices, exchange(): lax.ppermute(array, axis, [(i, i ^ distance) for i in range(devices)])  11.1 us
  transfers between devices with their start and end apart: 14, of which 7 were waited for; matrix products, arithmetic and copies ran while one was open for 7% of the time, Pallas kernels for 21%

profile of v7, /device:TPU:0, one launch (start us, length us, event | category | flops | bytes accessed | tf_op | source)
XLA Modules:
  0.0 276.8 jit_solution(6987683422213588920)
XLA Ops:
  0.7 3.0 %collective-permute-start.1 = (bf16[80,8,352]{2,1,0:T(8,128)(2,1)}, bf16[80,8,352]{2,1,0:T(8,128)(2,1)S(1)}, u32[]{:S(2)}, u32[]{:S(2)}) collective-permute-start(bf16[80,8,352]{2,1,0:T(8,128)(2,1)} %bitcast.87), channel_id=1, source_target_pairs={{0,16},{8,24},{16,0},{24,8},{1,17},{9,25},{17,1},{25,9},{2,18},{10... | collective-permute-start | bytes 1351688 | tf_op jit(solution)/shard_map/ppermute | solution.py:550
  3.7 1.5 collective-permute-start
  5.2 0.8 reshape.146
  6.2 1.3 dynamic_slice.49.pair_ref
  7.5 0.8 dynamic_slice.48
  8.5 0.9 convolution_bitcast_fusion
  10.2 4.2 %sine_multiply_fusion = (f32[1280,128]{1,0:T(8,128)}, f32[1280,128]{1,0:T(8,128)}) fusion(s32[128]{0:T(128)S(1)} %iota_multiply_fusion, s32[1280]{0:T(1024)S(1)} %pad_add_fusion, f32[1280]{0:T(1024)S(1)} %compare_select_fusion), kind=kLoop, calls=%fused_computation.14 | loop fusion | flops 1802240 | bytes 1321472 | tf_op jit(solution)/shard_map/mul | solution.py:220
  14.4 3.8 %sine_select_fusion.step_ref = f32[1280,4]{1,0:T(8,128)} fusion(s32[1280]{0:T(1024)S(1)} %pad_add_fusion, s32[4]{0:T(128)S(1)} %copy-done.5, pred[4]{0:T(512)(128)(4,1)S(1)} %fusion.29), kind=kLoop, calls=%fused_computation.10 | loop fusion | flops 51200 | bytes 25620 | tf_op jit(solution)/shard_map/jit(_where)/select_n | solution.py:222
  18.2 11.4 %angle_tables.1 = bf16[2560,2560]{1,0:T(8,128)(2,1)} custom-call(f32[1280,128]{1,0:T(8,128)} %get-tuple-element.57.cos_ref, f32[1280,128]{1,0:T(8,128)} %get-tuple-element.56.sin_ref, f32[1280,4]{1,0:T(8,128)} %sine_select_fusion.step_ref), custom_call_target="tpu_custom_call" | custom-call | flops 19660800 | bytes 13107200 | tf_op jit(solution)/shard_map/angle_tables/pallas_call | solution.py:224
  29.6 0.7 add_convert_fusion.edge_ref
  30.9 2.5 concatenate.25.spec_ref
  33.4 0.6 broadcast_in_dim.57.scale_ref
  34.1 0.7 broadcast_in_dim.58.taps_ref
  34.7 0.8 broadcast_in_dim.61.weight_ref
  35.5 16.7 %legendre_forward.3 = bf16[8,5,40,256]{3,2,1,0:T(8,128)(2,1)} custom-call(s32[80]{0:T(128)} %dynamic_slice.49.pair_ref, bf16[80,8,1408]{2,1,0:T(8,128)(2,1)} %concatenate.25.spec_ref, bf16[80,320,1408]{2,1,0:T(8,128)(2,1)} %leg_ref.7), custom_call_target="tpu_custom_call" | custom-call | flops 1153433600 | bytes 36044800 | tf_op jit(solution)/shard_map/legendre_forward/pallas_call | solution.py:100
  52.2 5.3 %all-to-all-start = ((bf16[8,5,40,256]{3,2,1,0:T(8,128)(2,1)}), bf16[8,5,40,256]{3,2,1,0:T(8,128)(2,1)S(1)}, u32[]{:S(2)}, u32[]{:S(2)}) async-start(bf16[8,5,40,256]{3,2,1,0:T(8,128)(2,1)} %legendre_forward.3), calls=%async_computation | async-start | bytes 1638400 | tf_op jit(solution)/shard_map/all_to_all | solution.py:617
  57.5 16.7 %legendre_forward.2 = bf16[8,5,40,256]{3,2,1,0:T(8,128)(2,1)} custom-call(s32[80]{0:T(128)} %dynamic_slice.49.pair_ref, bf16[80,8,1408]{2,1,0:T(8,128)(2,1)} %concatenate.25.spec_ref, bf16[80,320,1408]{2,1,0:T(8,128)(2,1)} %leg_ref.7), custom_call_target="tpu_custom_call" | custom-call | flops 1153433600 | bytes 36044800 | tf_op jit(solution)/shard_map/legendre_forward/pallas_call | solution.py:100
  74.2 5.0 %all-to-all-done = bf16[8,5,40,256]{3,2,1,0:T(8,128)(2,1)S(1)} async-done(((bf16[8,5,40,256]{3,2,1,0:T(8,128)(2,1)}), bf16[8,5,40,256]{3,2,1,0:T(8,128)(2,1)S(1)}, u32[]{:S(2)}, u32[]{:S(2)}) %all-to-all-start) | async-done | bytes 819232 | tf_op jit(solution)/shard_map/all_to_all | solution.py:617
  79.2 3.5 %all-to-all-start.1 = ((bf16[8,5,40,256]{3,2,1,0:T(8,128)(2,1)}), bf16[8,5,40,256]{3,2,1,0:T(8,128)(2,1)S(1)}, u32[]{:S(2)}, u32[]{:S(2)}) async-start(bf16[8,5,40,256]{3,2,1,0:T(8,128)(2,1)} %legendre_forward.2), calls=%async_computation.1 | async-start | bytes 1638400 | tf_op jit(solution)/shard_map/all_to_all | solution.py:617
  82.7 1.2 slice.75
  83.9 20.4 %all-to-all-done.1 = bf16[8,5,40,256]{3,2,1,0:T(8,128)(2,1)S(1)} async-done(((bf16[8,5,40,256]{3,2,1,0:T(8,128)(2,1)}), bf16[8,5,40,256]{3,2,1,0:T(8,128)(2,1)S(1)}, u32[]{:S(2)}, u32[]{:S(2)}) %all-to-all-start.1) | async-done | bytes 819232 | tf_op jit(solution)/shard_map/all_to_all | solution.py:617
  104.3 1.1 slice.76
  105.6 1.6 collective-permute-start.3
  107.1 0.5 slice.72
  107.7 0.5 slice.73
  108.3 1.5 collective-permute-start.4
  109.8 0.5 broadcast_select_fusion.3
  110.3 1.3 collective-permute-done.4
  112.2 3.1 %stack.75 = bf16[80,8,256]{2,1,0:T(8,128)(2,1)} concatenate(bf16[80,1,256]{2,1,0:T(2,128)(2,1)S(1)} %get-tuple-element.53, bf16[80,1,256]{2,1,0:T(2,128)(2,1)S(1)} %get-tuple-element.52, bf16[80,1,256]{2,1,0:T(2,128)(2,1)S(1)} %get-tuple-element.51, bf16[80,1,256]{2,1,0:T(2,128)(2,1)S(1)} %get-tuple-element.50, bf16[80,1,256]{2,1,0:T(2,128)(2,1)S(1)} %get-tuple-element.49, ...), dimensions={1} | concatenate | bytes 655360 | tf_op jit(solution)/shard_map/stack | solution.py:629
  115.2 68.6 %transport.1 = (bf16[4,2,40,5120]{3,2,1,0:T(8,128)(2,1)}, bf16[1600,256]{1,0:T(8,128)(2,1)}, bf16[1600,256]{1,0:T(8,128)(2,1)}) custom-call(s32[2]{0:T(128)} %add_convert_fusion.edge_ref, bf16[640,256]{1,0:T(8,128)(2,1)} %bitcast.94, bf16[256,256]{1,0:T(8,128)(2,1)} %constant.124.clone.perm_ref, bf16[2,512,512]{2,1,0:T(8,128)(2,1)} %constant.128.clone.order_ref, ...), custom_call_target="tpu_custom_call" | custom-call | flops 10066329600 | bytes 19660800 | tf_op jit(solution)/shard_map/transport/pallas_call | solution.py:501
  183.8 33.9 %all_to_all.20.coef_ref = bf16[8,5,40,256]{3,2,1,0:T(8,128)(2,1)} all-to-all(bf16[8,5,40,256]{3,2,1,0:T(8,128)(2,1)} %bitcast.86), channel_id=1, replica_groups=mesh['band'=4,'wave'=8] {'wave'}, dimensions={0} | all-to-all | bytes 1638400 | tf_op jit(solution)/shard_map/all_to_all | solution.py:660
  217.8 3.5 %all-to-all-start.3 = ((bf16[8,5,40,256]{3,2,1,0:T(8,128)(2,1)}), bf16[8,5,40,256]{3,2,1,0:T(8,128)(2,1)S(1)}, u32[]{:S(2)}, u32[]{:S(2)}) async-start(bf16[8,5,40,256]{3,2,1,0:T(8,128)(2,1)} %bitcast.85), calls=%async_computation.3 | async-start | bytes 1638400 | tf_op jit(solution)/shard_map/all_to_all | solution.py:660
  221.3 14.7 %legendre_backward.2 = bf16[320,1408]{1,0:T(8,128)(2,1)} custom-call(s32[80]{0:T(128)} %dynamic_slice.49.pair_ref, bf16[256,256]{1,0:T(8,128)(2,1)} %constant.124.clone.perm_ref, bf16[8,5,40,256]{3,2,1,0:T(8,128)(2,1)} %all_to_all.20.coef_ref, bf16[80,320,1408]{2,1,0:T(8,128)(2,1)} %leg_ref.7), custom_call_target="tpu_custom_call" | custom-call | flops 1153433600 | bytes 36044800 | tf_op jit(solution)/shard_map/legendre_backward/pallas_call | solution.py:156
  236.0 1.7 slice_bitcast_fusion.7
  238.0 2.5 collective-permute-start.5
  240.5 0.6 collective-permute-start.7
  241.1 0.9 collective-permute-start.6
  242.0 0.9 all-to-all-done.3.coef_ref
  242.9 0.9 copy-done.1
  243.8 14.7 %legendre_backward.3 = bf16[320,1408]{1,0:T(8,128)(2,1)} custom-call(s32[80]{0:T(128)} %dynamic_slice.49.pair_ref, bf16[256,256]{1,0:T(8,128)(2,1)} %constant.124.clone.perm_ref, bf16[8,5,40,256]{3,2,1,0:T(8,128)(2,1)} %copy-done.1, bf16[80,320,1408]{2,1,0:T(8,128)(2,1)} %leg_ref.7), custom_call_target="tpu_custom_call" | custom-call | flops 1153433600 | bytes 36044800 | tf_op jit(solution)/shard_map/legendre_backward/pallas_call | solution.py:156
  258.5 1.7 slice_bitcast_fusion.3
  260.5 2.5 collective-permute-start.8
  262.9 0.6 collective-permute-start.10
  263.5 1.0 collective-permute-start.9
  264.6 5.1 %collective-permute-done.8 = bf16[40,8,352]{2,1,0:T(8,128)(2,1)S(1)} collective-permute-done((bf16[40,8,352]{2,1,0:T(8,128)(2,1)S(1)}, bf16[40,8,352]{2,1,0:T(8,128)(2,1)S(1)}, u32[]{:S(2)}, u32[]{:S(2)}) %collective-permute-start.8) | collective-permute-done | bytes 225312 | tf_op jit(solution)/shard_map/ppermute | solution.py:550
  269.8 4.6 %collective-permute-done.10 = bf16[40,8,352]{2,1,0:T(8,128)(2,1)S(1)} collective-permute-done((bf16[40,8,352]{2,1,0:T(8,128)(2,1)S(1)}, bf16[40,8,352]{2,1,0:T(8,128)(2,1)S(1)}, u32[]{:S(2)}, u32[]{:S(2)}) %collective-permute-start.10) | collective-permute-done | bytes 225312 | tf_op jit(solution)/shard_map/ppermute | solution.py:550
  274.4 1.4 collective-permute-done.9
  275.9 0.9 pad_maximum_fusion.3
  (53 shorter events, 3.6 us)
Async XLA Ops:
  0.6 7.9 %copy-start = (f32[16,16]{1,0:T(8,128)S(1)}, f32[16,16]{1,0:T(8,128)}, u32[]{:S(2)}) copy-start(f32[16,16]{1,0:T(8,128)} %param.18) | copy-start | bytes 3076
  0.6 13.8 %copy-start.5 = (s32[4]{0:T(128)S(1)}, s32[4]{0:T(128)}, u32[]{:S(2)}) copy-start(s32[4]{0:T(128)} %constant.126.clone) | copy-start | bytes 52
  0.7 29.6 %collective-permute-start.1 = (bf16[80,8,352]{2,1,0:T(8,128)(2,1)}, bf16[80,8,352]{2,1,0:T(8,128)(2,1)S(1)}, u32[]{:S(2)}, u32[]{:S(2)}) collective-permute-start(bf16[80,8,352]{2,1,0:T(8,128)(2,1)} %bitcast.87), channel_id=1, source_target_pairs={{0,16},{8,24},{16,0},{24,8},{1,17},{9,25},{17,1},{25,9},{2,18},{10... | collective-permute-start | bytes 1351688 | tf_op jit(solution)/shard_map/ppermute | solution.py:550
  3.7 26.5 %collective-permute-start = (bf16[80,8,352]{2,1,0:T(8,128)(2,1)}, bf16[80,8,352]{2,1,0:T(8,128)(2,1)S(1)}, u32[]{:S(2)}, u32[]{:S(2)}) collective-permute-start(bf16[80,8,352]{2,1,0:T(8,128)(2,1)} %bitcast.88), channel_id=1, source_target_pairs={{0,8},{8,0},{16,24},{24,16},{1,9},{9,1},{17,25},{25,17},{2,10},{10... | collective-permute-start | bytes 1351688 | tf_op jit(solution)/shard_map/ppermute | solution.py:550
  5.2 25.1 %collective-permute-start.2 = (bf16[80,8,352]{2,1,0:T(8,128)(2,1)}, bf16[80,8,352]{2,1,0:T(8,128)(2,1)S(1)}, u32[]{:S(2)}, u32[]{:S(2)}) collective-permute-start(bf16[80,8,352]{2,1,0:T(8,128)(2,1)} %bitcast.89), channel_id=1, source_target_pairs={{0,24},{8,16},{16,8},{24,0},{1,25},{9,17},{17,9},{25,1},{2,26},{10... | collective-permute-start | bytes 1351688 | tf_op jit(solution)/shard_map/ppermute | solution.py:550
  18.2 12.1 %copy-start.4 = (bf16[80,352,8]{1,2,0:T(8,128)(2,1)S(1)}, bf16[80,352,8]{1,2,0:T(8,128)(2,1)}, u32[]{:S(2)}) copy-start(bf16[80,352,8]{1,2,0:T(8,128)(2,1)} %param.12) | copy-start | bytes 1351684
  52.2 27.0 %all-to-all-start = ((bf16[8,5,40,256]{3,2,1,0:T(8,128)(2,1)}), bf16[8,5,40,256]{3,2,1,0:T(8,128)(2,1)S(1)}, u32[]{:S(2)}, u32[]{:S(2)}) async-start(bf16[8,5,40,256]{3,2,1,0:T(8,128)(2,1)} %legendre_forward.3), calls=%async_computation | async-start | bytes 1638400 | tf_op jit(solution)/shard_map/all_to_all | solution.py:617
  79.2 32.9 %copy-start.2 = (bf16[8,5,40,256]{3,2,1,0:T(8,128)(2,1)}, bf16[8,5,40,256]{3,2,1,0:T(8,128)(2,1)S(1)}, u32[]{:S(2)}) copy-start(bf16[8,5,40,256]{3,2,1,0:T(8,128)(2,1)S(1)} %all-to-all-done) | copy-start | bytes 2457604
  79.2 25.2 %all-to-all-start.1 = ((bf16[8,5,40,256]{3,2,1,0:T(8,128)(2,1)}), bf16[8,5,40,256]{3,2,1,0:T(8,128)(2,1)S(1)}, u32[]{:S(2)}, u32[]{:S(2)}) async-start(bf16[8,5,40,256]{3,2,1,0:T(8,128)(2,1)} %legendre_forward.2), calls=%async_computation.1 | async-start | bytes 1638400 | tf_op jit(solution)/shard_map/all_to_all | solution.py:617
  104.3 10.9 %copy-start.3 = (bf16[8,5,40,256]{3,2,1,0:T(8,128)(2,1)}, bf16[8,5,40,256]{3,2,1,0:T(8,128)(2,1)S(1)}, u32[]{:S(2)}) copy-start(bf16[8,5,40,256]{3,2,1,0:T(8,128)(2,1)S(1)} %all-to-all-done.1) | copy-start | bytes 2457604
  105.6 4.2 %collective-permute-start.3 = (bf16[80,3,256]{2,1,0:T(4,128)(2,1)S(1)}, bf16[80,3,256]{2,1,0:T(4,128)(2,1)S(1)}, u32[]{:S(2)}, u32[]{:S(2)}) collective-permute-start(bf16[80,3,256]{2,1,0:T(4,128)(2,1)S(1)} %pad_maximum_fusion.5), channel_id=1, source_target_pairs={{0,1},{1,2},{2,3},{3,4},{4,5},{5,6},{6,7},{7,8},{8,9},{9,10},{10,1... | collective-permute-start | bytes 368648 | tf_op jit(solution)/shard_map/ppermute | solution.py:624
  108.3 3.3 %collective-permute-start.4 = (bf16[80,3,256]{2,1,0:T(4,128)(2,1)S(1)}, bf16[80,3,256]{2,1,0:T(4,128)(2,1)S(1)}, u32[]{:S(2)}, u32[]{:S(2)}) collective-permute-start(bf16[80,3,256]{2,1,0:T(4,128)(2,1)S(1)} %pad_maximum_fusion.4), channel_id=1, source_target_pairs={{1,0},{2,1},{3,2},{4,3},{5,4},{6,5},{7,6},{8,7},{9,8},{10,9},{11,1... | collective-permute-start | bytes 368648 | tf_op jit(solution)/shard_map/ppermute | solution.py:625
  217.8 25.2 %all-to-all-start.3 = ((bf16[8,5,40,256]{3,2,1,0:T(8,128)(2,1)}), bf16[8,5,40,256]{3,2,1,0:T(8,128)(2,1)S(1)}, u32[]{:S(2)}, u32[]{:S(2)}) async-start(bf16[8,5,40,256]{3,2,1,0:T(8,128)(2,1)} %bitcast.85), calls=%async_computation.3 | async-start | bytes 1638400 | tf_op jit(solution)/shard_map/all_to_all | solution.py:660
  238.0 25.5 %collective-permute-start.5 = (bf16[40,8,352]{2,1,0:T(8,128)(2,1)S(1)}, bf16[40,8,352]{2,1,0:T(8,128)(2,1)S(1)}, u32[]{:S(2)}, u32[]{:S(2)}) collective-permute-start(bf16[40,8,352]{2,1,0:T(8,128)(2,1)S(1)} %get-tuple-element.34), channel_id=1, source_target_pairs={{0,8},{8,0},{16,24},{24,16},{1,9},{9,1},{17,25},{25,17},{2,10},{10... | collective-permute-start | bytes 675848 | tf_op jit(solution)/shard_map/ppermute | solution.py:550
  240.5 24.0 %collective-permute-start.7 = (bf16[40,8,352]{2,1,0:T(8,128)(2,1)S(1)}, bf16[40,8,352]{2,1,0:T(8,128)(2,1)S(1)}, u32[]{:S(2)}, u32[]{:S(2)}) collective-permute-start(bf16[40,8,352]{2,1,0:T(8,128)(2,1)S(1)} %get-tuple-element.35), channel_id=1, source_target_pairs={{0,24},{8,16},{16,8},{24,0},{1,25},{9,17},{17,9},{25,1},{2,26},{10... | collective-permute-start | bytes 675848 | tf_op jit(solution)/shard_map/ppermute | solution.py:550
  241.1 23.4 %collective-permute-start.6 = (bf16[40,8,352]{2,1,0:T(8,128)(2,1)S(1)}, bf16[40,8,352]{2,1,0:T(8,128)(2,1)S(1)}, u32[]{:S(2)}, u32[]{:S(2)}) collective-permute-start(bf16[40,8,352]{2,1,0:T(8,128)(2,1)S(1)} %get-tuple-element.36), channel_id=1, source_target_pairs={{0,16},{8,24},{16,0},{24,8},{1,17},{9,25},{17,1},{25,9},{2,18},{10... | collective-permute-start | bytes 675848 | tf_op jit(solution)/shard_map/ppermute | solution.py:550
  242.9 0.9 copy-start.1
  260.5 9.3 %collective-permute-start.8 = (bf16[40,8,352]{2,1,0:T(8,128)(2,1)S(1)}, bf16[40,8,352]{2,1,0:T(8,128)(2,1)S(1)}, u32[]{:S(2)}, u32[]{:S(2)}) collective-permute-start(bf16[40,8,352]{2,1,0:T(8,128)(2,1)S(1)} %get-tuple-element.37), channel_id=1, source_target_pairs={{0,8},{8,0},{16,24},{24,16},{1,9},{9,1},{17,25},{25,17},{2,10},{10... | collective-permute-start | bytes 675848 | tf_op jit(solution)/shard_map/ppermute | solution.py:550
  262.9 11.4 %collective-permute-start.10 = (bf16[40,8,352]{2,1,0:T(8,128)(2,1)S(1)}, bf16[40,8,352]{2,1,0:T(8,128)(2,1)S(1)}, u32[]{:S(2)}, u32[]{:S(2)}) collective-permute-start(bf16[40,8,352]{2,1,0:T(8,128)(2,1)S(1)} %get-tuple-element.38), channel_id=1, source_target_pairs={{0,24},{8,16},{16,8},{24,0},{1,25},{9,17},{17,9},{25,1},{2,26},{10... | collective-permute-start | bytes 675848 | tf_op jit(solution)/shard_map/ppermute | solution.py:550
  263.5 12.2 %collective-permute-start.9 = (bf16[40,8,352]{2,1,0:T(8,128)(2,1)S(1)}, bf16[40,8,352]{2,1,0:T(8,128)(2,1)S(1)}, u32[]{:S(2)}, u32[]{:S(2)}) collective-permute-start(bf16[40,8,352]{2,1,0:T(8,128)(2,1)S(1)} %get-tuple-element.39), channel_id=1, source_target_pairs={{0,16},{8,24},{16,0},{24,8},{1,17},{9,25},{17,1},{25,9},{2,18},{10... | collective-permute-start | bytes 675848 | tf_op jit(solution)/shard_map/ppermute | solution.py:550

commit v8 on v7

--- a/solution.py
+++ b/solution.py
@@ -352,20 +352,20 @@
         def neighbours(row, carry):
             for j in range(FINE):
                 here = grid_ref[row, :, pl.ds(pl.multiple_of(chunk * CHUNK + j * 128, 128), 128)]
+                here = here.astype(F32)
                 near_ref[row, :, (RIM + j) * 128 : (RIM + j + 1) * 128] = here
-                here = here.astype(F32)
                 if j >= FINE - RIM:
                     at = pl.ds(pl.multiple_of(previous * CHUNK + j * 128, 128), 128)
                     there = grid_ref[row, :, at].astype(F32)
                     mixed = pltpu.roll(jnp.where(lane == 127, there, here), 1, 1)
                     slot = j - (FINE - RIM)
-                    near_ref[row, :, slot * 128 : slot * 128 + 128] = mixed.astype(BF16)
+                    near_ref[row, :, slot * 128 : slot * 128 + 128] = mixed
                 if j < RIM:
                     at = pl.ds(pl.multiple_of(following * CHUNK + j * 128, 128), 128)
                     there = grid_ref[row, :, at].astype(F32)
                     mixed = pltpu.roll(jnp.where(lane == 0, there, here), 127, 1)
                     slot = RIM + FINE + j
-                    near_ref[row, :, slot * 128 : slot * 128 + 128] = mixed.astype(BF16)
+                    near_ref[row, :, slot * 128 : slot * 128 + 128] = mixed
             return carry
 
         lax.fori_loop(0, FIELDS * REACH, neighbours, 0, unroll=4)
@@ -413,7 +413,7 @@
                         part = {}
                         for c in range(7):
                             lanes_c = pl.ds(pl.multiple_of((j + c) * 128, 128), 128)
-                            near = near_ref[f * REACH + row, :, lanes_c]
+                            near = near_ref[f * REACH + row, :, lanes_c].astype(BF16)
                             for k in factors:
                                 term = factors[k][c] * near
                                 part[k] = part[k] + term if k in part else term
@@ -514,7 +514,7 @@
             pltpu.VMEM((left, 256), F32),
             pltpu.VMEM((left, 256), F32),
             pltpu.VMEM((FIELDS * REACH, 16, NLON), BF16),
-            pltpu.VMEM((FIELDS * REACH, 16, CHUNK + 2 * RIM * 128), BF16),
+            pltpu.VMEM((FIELDS * REACH, 16, CHUNK + 2 * RIM * 128), F32),
             pltpu.VMEM((FINE, FIELDS * 2, lats, 128), F32),
             pltpu.VMEM((FINE, 2 * lats, 128), jnp.int32),
             pltpu.VMEM((own, NLON), BF16),

time: 278 us -> 281 us (1.011)
  Pallas kernels: 143 us -> 146 us
    pallas_call x1, Pallas kernels: 68.6 us -> 71.5 us  [transport(): pl.pallas_call(functools.partial(middle_kernel, sub, parts), out_shape=(j...]
where the time goes in v8:
time: 281 us; the launch traced here: 280 us
  Pallas kernels  146 us (52%)
  waiting for transfers between devices  38.7 us (14%)
  blocking collectives  34 us (12%)
  starting transfers between devices  28 us (10%)
  local copies, waits for them, and re-layouts  19.5 us (7%)
  other arithmetic  12 us (4%)
    pallas_call x1, Pallas kernels, transport(): pl.pallas_call(functools.partial(middle_kernel, sub, parts), out_shape=(j...  71.5 us
    all_to_all x1, blocking collectives, per_device(): lax.all_to_all(leaving, 'wave', split_axis=0, concat_axis=0, tiled=True)  34 us
    pallas_call x2, Pallas kernels, legendre_forward(): pl.pallas_call(functools.partial(forward_kernel, height, base), out_shape...  33.4 us
    pallas_call x2, Pallas kernels, legendre_backward(): pl.pallas_call(functools.partial(backward_kernel, height, base), out_shap...  29.4 us
    all_to_all x2, waiting for transfers between devices, per_device(): lax.all_to_all(sent, 'wave', split_axis=0, concat_axis=0, tiled=True)  25.4 us
    ppermute x9, starting transfers between devices, exchange(): lax.ppermute(array, axis, [(i, i ^ distance) for i in range(devices)])  12.6 us
    pallas_call x1, Pallas kernels, angle_tables(): pl.pallas_call(table_kernel, out_shape=jax.ShapeDtypeStruct((2 * count, H...  11.4 us
    ppermute x9, waiting for transfers between devices, exchange(): lax.ppermute(array, axis, [(i, i ^ distance) for i in range(devices)])  11.1 us
  transfers between devices with their start and end apart: 14, of which 7 were waited for; matrix products, arithmetic and copies ran while one was open for 7% of the time, Pallas kernels for 21%

profile of v8, /device:TPU:0, one launch (start us, length us, event | category | flops | bytes accessed | tf_op | source)
XLA Modules:
  0.0 279.8 jit_solution(1416476090379489532)
XLA Ops:
  0.7 3.0 %collective-permute-start.1 = (bf16[80,8,352]{2,1,0:T(8,128)(2,1)}, bf16[80,8,352]{2,1,0:T(8,128)(2,1)S(1)}, u32[]{:S(2)}, u32[]{:S(2)}) collective-permute-start(bf16[80,8,352]{2,1,0:T(8,128)(2,1)} %bitcast.87), channel_id=1, source_target_pairs={{0,16},{8,24},{16,0},{24,8},{1,17},{9,25},{17,1},{25,9},{2,18},{10... | collective-permute-start | bytes 1351688 | tf_op jit(solution)/shard_map/ppermute | solution.py:550
  3.7 1.5 collective-permute-start
  5.2 0.8 reshape.146
  6.2 1.3 dynamic_slice.49.pair_ref
  7.5 0.8 dynamic_slice.48
  8.5 0.9 convolution_bitcast_fusion
  10.2 4.2 %sine_multiply_fusion = (f32[1280,128]{1,0:T(8,128)}, f32[1280,128]{1,0:T(8,128)}) fusion(s32[128]{0:T(128)S(1)} %iota_multiply_fusion, s32[1280]{0:T(1024)S(1)} %pad_add_fusion, f32[1280]{0:T(1024)S(1)} %compare_select_fusion), kind=kLoop, calls=%fused_computation.14 | loop fusion | flops 1802240 | bytes 1321472 | tf_op jit(solution)/shard_map/mul | solution.py:220
  14.4 3.8 %sine_select_fusion.step_ref = f32[1280,4]{1,0:T(8,128)} fusion(s32[1280]{0:T(1024)S(1)} %pad_add_fusion, s32[4]{0:T(128)S(1)} %copy-done.5, pred[4]{0:T(512)(128)(4,1)S(1)} %fusion.29), kind=kLoop, calls=%fused_computation.10 | loop fusion | flops 51200 | bytes 25620 | tf_op jit(solution)/shard_map/jit(_where)/select_n | solution.py:222
  18.2 11.4 %angle_tables.1 = bf16[2560,2560]{1,0:T(8,128)(2,1)} custom-call(f32[1280,128]{1,0:T(8,128)} %get-tuple-element.57.cos_ref, f32[1280,128]{1,0:T(8,128)} %get-tuple-element.56.sin_ref, f32[1280,4]{1,0:T(8,128)} %sine_select_fusion.step_ref), custom_call_target="tpu_custom_call" | custom-call | flops 19660800 | bytes 13107200 | tf_op jit(solution)/shard_map/angle_tables/pallas_call | solution.py:224
  29.6 0.7 add_convert_fusion.edge_ref
  30.9 2.5 concatenate.25.spec_ref
  33.4 0.6 broadcast_in_dim.57.scale_ref
  34.1 0.7 broadcast_in_dim.58.taps_ref
  34.7 0.8 broadcast_in_dim.61.weight_ref
  35.5 16.7 %legendre_forward.3 = bf16[8,5,40,256]{3,2,1,0:T(8,128)(2,1)} custom-call(s32[80]{0:T(128)} %dynamic_slice.49.pair_ref, bf16[80,8,1408]{2,1,0:T(8,128)(2,1)} %concatenate.25.spec_ref, bf16[80,320,1408]{2,1,0:T(8,128)(2,1)} %leg_ref.7), custom_call_target="tpu_custom_call" | custom-call | flops 1153433600 | bytes 36044800 | tf_op jit(solution)/shard_map/legendre_forward/pallas_call | solution.py:100
  52.2 5.3 %all-to-all-start = ((bf16[8,5,40,256]{3,2,1,0:T(8,128)(2,1)}), bf16[8,5,40,256]{3,2,1,0:T(8,128)(2,1)S(1)}, u32[]{:S(2)}, u32[]{:S(2)}) async-start(bf16[8,5,40,256]{3,2,1,0:T(8,128)(2,1)} %legendre_forward.3), calls=%async_computation | async-start | bytes 1638400 | tf_op jit(solution)/shard_map/all_to_all | solution.py:617
  57.5 16.7 %legendre_forward.2 = bf16[8,5,40,256]{3,2,1,0:T(8,128)(2,1)} custom-call(s32[80]{0:T(128)} %dynamic_slice.49.pair_ref, bf16[80,8,1408]{2,1,0:T(8,128)(2,1)} %concatenate.25.spec_ref, bf16[80,320,1408]{2,1,0:T(8,128)(2,1)} %leg_ref.7), custom_call_target="tpu_custom_call" | custom-call | flops 1153433600 | bytes 36044800 | tf_op jit(solution)/shard_map/legendre_forward/pallas_call | solution.py:100
  74.2 5.0 %all-to-all-done = bf16[8,5,40,256]{3,2,1,0:T(8,128)(2,1)S(1)} async-done(((bf16[8,5,40,256]{3,2,1,0:T(8,128)(2,1)}), bf16[8,5,40,256]{3,2,1,0:T(8,128)(2,1)S(1)}, u32[]{:S(2)}, u32[]{:S(2)}) %all-to-all-start) | async-done | bytes 819232 | tf_op jit(solution)/shard_map/all_to_all | solution.py:617
  79.2 3.5 %all-to-all-start.1 = ((bf16[8,5,40,256]{3,2,1,0:T(8,128)(2,1)}), bf16[8,5,40,256]{3,2,1,0:T(8,128)(2,1)S(1)}, u32[]{:S(2)}, u32[]{:S(2)}) async-start(bf16[8,5,40,256]{3,2,1,0:T(8,128)(2,1)} %legendre_forward.2), calls=%async_computation.1 | async-start | bytes 1638400 | tf_op jit(solution)/shard_map/all_to_all | solution.py:617
  82.7 1.2 slice.75
  83.9 20.4 %all-to-all-done.1 = bf16[8,5,40,256]{3,2,1,0:T(8,128)(2,1)S(1)} async-done(((bf16[8,5,40,256]{3,2,1,0:T(8,128)(2,1)}), bf16[8,5,40,256]{3,2,1,0:T(8,128)(2,1)S(1)}, u32[]{:S(2)}, u32[]{:S(2)}) %all-to-all-start.1) | async-done | bytes 819232 | tf_op jit(solution)/shard_map/all_to_all | solution.py:617
  104.3 1.1 slice.76
  105.6 1.6 collective-permute-start.3
  107.1 0.5 slice.72
  107.7 0.5 slice.73
  108.3 1.5 collective-permute-start.4
  109.8 0.5 broadcast_select_fusion.3
  110.3 1.3 collective-permute-done.4
  112.2 3.1 %stack.75 = bf16[80,8,256]{2,1,0:T(8,128)(2,1)} concatenate(bf16[80,1,256]{2,1,0:T(2,128)(2,1)S(1)} %get-tuple-element.53, bf16[80,1,256]{2,1,0:T(2,128)(2,1)S(1)} %get-tuple-element.52, bf16[80,1,256]{2,1,0:T(2,128)(2,1)S(1)} %get-tuple-element.51, bf16[80,1,256]{2,1,0:T(2,128)(2,1)S(1)} %get-tuple-element.50, bf16[80,1,256]{2,1,0:T(2,128)(2,1)S(1)} %get-tuple-element.49, ...), dimensions={1} | concatenate | bytes 655360 | tf_op jit(solution)/shard_map/stack | solution.py:629
  115.2 71.5 %transport.1 = (bf16[4,2,40,5120]{3,2,1,0:T(8,128)(2,1)}, bf16[1600,256]{1,0:T(8,128)(2,1)}, bf16[1600,256]{1,0:T(8,128)(2,1)}) custom-call(s32[2]{0:T(128)} %add_convert_fusion.edge_ref, bf16[640,256]{1,0:T(8,128)(2,1)} %bitcast.94, bf16[256,256]{1,0:T(8,128)(2,1)} %constant.124.clone.perm_ref, bf16[2,512,512]{2,1,0:T(8,128)(2,1)} %constant.128.clone.order_ref, ...), custom_call_target="tpu_custom_call" | custom-call | flops 10066329600 | bytes 19660800 | tf_op jit(solution)/shard_map/transport/pallas_call | solution.py:501
  186.8 34.0 %all_to_all.20.coef_ref = bf16[8,5,40,256]{3,2,1,0:T(8,128)(2,1)} all-to-all(bf16[8,5,40,256]{3,2,1,0:T(8,128)(2,1)} %bitcast.86), channel_id=1, replica_groups=mesh['band'=4,'wave'=8] {'wave'}, dimensions={0} | all-to-all | bytes 1638400 | tf_op jit(solution)/shard_map/all_to_all | solution.py:660
  220.8 3.5 %all-to-all-start.3 = ((bf16[8,5,40,256]{3,2,1,0:T(8,128)(2,1)}), bf16[8,5,40,256]{3,2,1,0:T(8,128)(2,1)S(1)}, u32[]{:S(2)}, u32[]{:S(2)}) async-start(bf16[8,5,40,256]{3,2,1,0:T(8,128)(2,1)} %bitcast.85), calls=%async_computation.3 | async-start | bytes 1638400 | tf_op jit(solution)/shard_map/all_to_all | solution.py:660
  224.3 14.7 %legendre_backward.2 = bf16[320,1408]{1,0:T(8,128)(2,1)} custom-call(s32[80]{0:T(128)} %dynamic_slice.49.pair_ref, bf16[256,256]{1,0:T(8,128)(2,1)} %constant.124.clone.perm_ref, bf16[8,5,40,256]{3,2,1,0:T(8,128)(2,1)} %all_to_all.20.coef_ref, bf16[80,320,1408]{2,1,0:T(8,128)(2,1)} %leg_ref.7), custom_call_target="tpu_custom_call" | custom-call | flops 1153433600 | bytes 36044800 | tf_op jit(solution)/shard_map/legendre_backward/pallas_call | solution.py:156
  239.0 1.7 slice_bitcast_fusion.7
  241.0 2.5 collective-permute-start.5
  243.5 0.6 collective-permute-start.7
  244.1 0.9 collective-permute-start.6
  245.0 0.9 all-to-all-done.3.coef_ref
  245.9 0.9 copy-done.1
  246.8 14.7 %legendre_backward.3 = bf16[320,1408]{1,0:T(8,128)(2,1)} custom-call(s32[80]{0:T(128)} %dynamic_slice.49.pair_ref, bf16[256,256]{1,0:T(8,128)(2,1)} %constant.124.clone.perm_ref, bf16[8,5,40,256]{3,2,1,0:T(8,128)(2,1)} %copy-done.1, bf16[80,320,1408]{2,1,0:T(8,128)(2,1)} %leg_ref.7), custom_call_target="tpu_custom_call" | custom-call | flops 1153433600 | bytes 36044800 | tf_op jit(solution)/shard_map/legendre_backward/pallas_call | solution.py:156
  261.5 1.7 slice_bitcast_fusion.3
  263.5 2.5 collective-permute-start.8
  266.0 0.6 collective-permute-start.10
  266.5 1.0 collective-permute-start.9
  267.6 5.1 %collective-permute-done.8 = bf16[40,8,352]{2,1,0:T(8,128)(2,1)S(1)} collective-permute-done((bf16[40,8,352]{2,1,0:T(8,128)(2,1)S(1)}, bf16[40,8,352]{2,1,0:T(8,128)(2,1)S(1)}, u32[]{:S(2)}, u32[]{:S(2)}) %collective-permute-start.8) | collective-permute-done | bytes 225312 | tf_op jit(solution)/shard_map/ppermute | solution.py:550
  272.8 4.6 %collective-permute-done.10 = bf16[40,8,352]{2,1,0:T(8,128)(2,1)S(1)} collective-permute-done((bf16[40,8,352]{2,1,0:T(8,128)(2,1)S(1)}, bf16[40,8,352]{2,1,0:T(8,128)(2,1)S(1)}, u32[]{:S(2)}, u32[]{:S(2)}) %collective-permute-start.10) | collective-permute-done | bytes 225312 | tf_op jit(solution)/shard_map/ppermute | solution.py:550
  277.4 1.4 collective-permute-done.9
  278.9 0.9 pad_maximum_fusion.3
  (53 shorter events, 3.6 us)
Async XLA Ops:
  0.6 7.9 %copy-start = (f32[16,16]{1,0:T(8,128)S(1)}, f32[16,16]{1,0:T(8,128)}, u32[]{:S(2)}) copy-start(f32[16,16]{1,0:T(8,128)} %param.18) | copy-start | bytes 3076
  0.6 13.8 %copy-start.5 = (s32[4]{0:T(128)S(1)}, s32[4]{0:T(128)}, u32[]{:S(2)}) copy-start(s32[4]{0:T(128)} %constant.126.clone) | copy-start | bytes 52
  0.7 29.6 %collective-permute-start.1 = (bf16[80,8,352]{2,1,0:T(8,128)(2,1)}, bf16[80,8,352]{2,1,0:T(8,128)(2,1)S(1)}, u32[]{:S(2)}, u32[]{:S(2)}) collective-permute-start(bf16[80,8,352]{2,1,0:T(8,128)(2,1)} %bitcast.87), channel_id=1, source_target_pairs={{0,16},{8,24},{16,0},{24,8},{1,17},{9,25},{17,1},{25,9},{2,18},{10... | collective-permute-start | bytes 1351688 | tf_op jit(solution)/shard_map/ppermute | solution.py:550
  3.7 26.5 %collective-permute-start = (bf16[80,8,352]{2,1,0:T(8,128)(2,1)}, bf16[80,8,352]{2,1,0:T(8,128)(2,1)S(1)}, u32[]{:S(2)}, u32[]{:S(2)}) collective-permute-start(bf16[80,8,352]{2,1,0:T(8,128)(2,1)} %bitcast.88), channel_id=1, source_target_pairs={{0,8},{8,0},{16,24},{24,16},{1,9},{9,1},{17,25},{25,17},{2,10},{10... | collective-permute-start | bytes 1351688 | tf_op jit(solution)/shard_map/ppermute | solution.py:550
  5.2 25.1 %collective-permute-start.2 = (bf16[80,8,352]{2,1,0:T(8,128)(2,1)}, bf16[80,8,352]{2,1,0:T(8,128)(2,1)S(1)}, u32[]{:S(2)}, u32[]{:S(2)}) collective-permute-start(bf16[80,8,352]{2,1,0:T(8,128)(2,1)} %bitcast.89), channel_id=1, source_target_pairs={{0,24},{8,16},{16,8},{24,0},{1,25},{9,17},{17,9},{25,1},{2,26},{10... | collective-permute-start | bytes 1351688 | tf_op jit(solution)/shard_map/ppermute | solution.py:550
  18.2 12.1 %copy-start.4 = (bf16[80,352,8]{1,2,0:T(8,128)(2,1)S(1)}, bf16[80,352,8]{1,2,0:T(8,128)(2,1)}, u32[]{:S(2)}) copy-start(bf16[80,352,8]{1,2,0:T(8,128)(2,1)} %param.12) | copy-start | bytes 1351684
  52.2 27.0 %all-to-all-start = ((bf16[8,5,40,256]{3,2,1,0:T(8,128)(2,1)}), bf16[8,5,40,256]{3,2,1,0:T(8,128)(2,1)S(1)}, u32[]{:S(2)}, u32[]{:S(2)}) async-start(bf16[8,5,40,256]{3,2,1,0:T(8,128)(2,1)} %legendre_forward.3), calls=%async_computation | async-start | bytes 1638400 | tf_op jit(solution)/shard_map/all_to_all | solution.py:617
  79.2 32.9 %copy-start.2 = (bf16[8,5,40,256]{3,2,1,0:T(8,128)(2,1)}, bf16[8,5,40,256]{3,2,1,0:T(8,128)(2,1)S(1)}, u32[]{:S(2)}) copy-start(bf16[8,5,40,256]{3,2,1,0:T(8,128)(2,1)S(1)} %all-to-all-done) | copy-start | bytes 2457604
  79.2 25.2 %all-to-all-start.1 = ((bf16[8,5,40,256]{3,2,1,0:T(8,128)(2,1)}), bf16[8,5,40,256]{3,2,1,0:T(8,128)(2,1)S(1)}, u32[]{:S(2)}, u32[]{:S(2)}) async-start(bf16[8,5,40,256]{3,2,1,0:T(8,128)(2,1)} %legendre_forward.2), calls=%async_computation.1 | async-start | bytes 1638400 | tf_op jit(solution)/shard_map/all_to_all | solution.py:617
  104.3 10.9 %copy-start.3 = (bf16[8,5,40,256]{3,2,1,0:T(8,128)(2,1)}, bf16[8,5,40,256]{3,2,1,0:T(8,128)(2,1)S(1)}, u32[]{:S(2)}) copy-start(bf16[8,5,40,256]{3,2,1,0:T(8,128)(2,1)S(1)} %all-to-all-done.1) | copy-start | bytes 2457604
  105.6 4.2 %collective-permute-start.3 = (bf16[80,3,256]{2,1,0:T(4,128)(2,1)S(1)}, bf16[80,3,256]{2,1,0:T(4,128)(2,1)S(1)}, u32[]{:S(2)}, u32[]{:S(2)}) collective-permute-start(bf16[80,3,256]{2,1,0:T(4,128)(2,1)S(1)} %pad_maximum_fusion.5), channel_id=1, source_target_pairs={{0,1},{1,2},{2,3},{3,4},{4,5},{5,6},{6,7},{7,8},{8,9},{9,10},{10,1... | collective-permute-start | bytes 368648 | tf_op jit(solution)/shard_map/ppermute | solution.py:624
  108.3 3.3 %collective-permute-start.4 = (bf16[80,3,256]{2,1,0:T(4,128)(2,1)S(1)}, bf16[80,3,256]{2,1,0:T(4,128)(2,1)S(1)}, u32[]{:S(2)}, u32[]{:S(2)}) collective-permute-start(bf16[80,3,256]{2,1,0:T(4,128)(2,1)S(1)} %pad_maximum_fusion.4), channel_id=1, source_target_pairs={{1,0},{2,1},{3,2},{4,3},{5,4},{6,5},{7,6},{8,7},{9,8},{10,9},{11,1... | collective-permute-start | bytes 368648 | tf_op jit(solution)/shard_map/ppermute | solution.py:625
  220.8 25.2 %all-to-all-start.3 = ((bf16[8,5,40,256]{3,2,1,0:T(8,128)(2,1)}), bf16[8,5,40,256]{3,2,1,0:T(8,128)(2,1)S(1)}, u32[]{:S(2)}, u32[]{:S(2)}) async-start(bf16[8,5,40,256]{3,2,1,0:T(8,128)(2,1)} %bitcast.85), calls=%async_computation.3 | async-start | bytes 1638400 | tf_op jit(solution)/shard_map/all_to_all | solution.py:660
  241.0 25.5 %collective-permute-start.5 = (bf16[40,8,352]{2,1,0:T(8,128)(2,1)S(1)}, bf16[40,8,352]{2,1,0:T(8,128)(2,1)S(1)}, u32[]{:S(2)}, u32[]{:S(2)}) collective-permute-start(bf16[40,8,352]{2,1,0:T(8,128)(2,1)S(1)} %get-tuple-element.34), channel_id=1, source_target_pairs={{0,8},{8,0},{16,24},{24,16},{1,9},{9,1},{17,25},{25,17},{2,10},{10... | collective-permute-start | bytes 675848 | tf_op jit(solution)/shard_map/ppermute | solution.py:550
  243.5 24.0 %collective-permute-start.7 = (bf16[40,8,352]{2,1,0:T(8,128)(2,1)S(1)}, bf16[40,8,352]{2,1,0:T(8,128)(2,1)S(1)}, u32[]{:S(2)}, u32[]{:S(2)}) collective-permute-start(bf16[40,8,352]{2,1,0:T(8,128)(2,1)S(1)} %get-tuple-element.35), channel_id=1, source_target_pairs={{0,24},{8,16},{16,8},{24,0},{1,25},{9,17},{17,9},{25,1},{2,26},{10... | collective-permute-start | bytes 675848 | tf_op jit(solution)/shard_map/ppermute | solution.py:550
  244.1 23.4 %collective-permute-start.6 = (bf16[40,8,352]{2,1,0:T(8,128)(2,1)S(1)}, bf16[40,8,352]{2,1,0:T(8,128)(2,1)S(1)}, u32[]{:S(2)}, u32[]{:S(2)}) collective-permute-start(bf16[40,8,352]{2,1,0:T(8,128)(2,1)S(1)} %get-tuple-element.36), channel_id=1, source_target_pairs={{0,16},{8,24},{16,0},{24,8},{1,17},{9,25},{17,1},{25,9},{2,18},{10... | collective-permute-start | bytes 675848 | tf_op jit(solution)/shard_map/ppermute | solution.py:550
  245.9 0.9 copy-start.1
  263.5 9.3 %collective-permute-start.8 = (bf16[40,8,352]{2,1,0:T(8,128)(2,1)S(1)}, bf16[40,8,352]{2,1,0:T(8,128)(2,1)S(1)}, u32[]{:S(2)}, u32[]{:S(2)}) collective-permute-start(bf16[40,8,352]{2,1,0:T(8,128)(2,1)S(1)} %get-tuple-element.37), channel_id=1, source_target_pairs={{0,8},{8,0},{16,24},{24,16},{1,9},{9,1},{17,25},{25,17},{2,10},{10... | collective-permute-start | bytes 675848 | tf_op jit(solution)/shard_map/ppermute | solution.py:550
  266.0 11.4 %collective-permute-start.10 = (bf16[40,8,352]{2,1,0:T(8,128)(2,1)S(1)}, bf16[40,8,352]{2,1,0:T(8,128)(2,1)S(1)}, u32[]{:S(2)}, u32[]{:S(2)}) collective-permute-start(bf16[40,8,352]{2,1,0:T(8,128)(2,1)S(1)} %get-tuple-element.38), channel_id=1, source_target_pairs={{0,24},{8,16},{16,8},{24,0},{1,25},{9,17},{17,9},{25,1},{2,26},{10... | collective-permute-start | bytes 675848 | tf_op jit(solution)/shard_map/ppermute | solution.py:550
  266.5 12.2 %collective-permute-start.9 = (bf16[40,8,352]{2,1,0:T(8,128)(2,1)S(1)}, bf16[40,8,352]{2,1,0:T(8,128)(2,1)S(1)}, u32[]{:S(2)}, u32[]{:S(2)}) collective-permute-start(bf16[40,8,352]{2,1,0:T(8,128)(2,1)S(1)} %get-tuple-element.39), channel_id=1, source_target_pairs={{0,16},{8,24},{16,0},{24,8},{1,17},{9,25},{17,1},{25,9},{2,18},{10... | collective-permute-start | bytes 675848 | tf_op jit(solution)/shard_map/ppermute | solution.py:550
